TPU v7x, 768 devices: a whole 4x8x12 slice. The times are simulated.
768 devices in a mesh: user: 64 (over x, y, core), item: 12 (over z).
Axes of the slice: x: 4, y: 8, z: 12, core: 2. Of those that a mesh axis runs over, the one named last changes fastest.
Arguments:
- ratings: bfloat16 [24576, 3072], P('user', 'item'), may hold values from -64 to 64
- counts: int32 [384], P('user'), may hold values from 0 to 64, as said below
Outputs:
- similarity: bfloat16 [3072, 3072], P('user', 'item')
Inputs may be any that keep to these rules, and one draw needn't show every extreme that they name: `counts`: live rows of each aligned block of 64 user rows; rows at or past the count are padding; each index of user holds a block with 64 live rows.
All inputs are finite; a program needn't handle non-finite values.
Results may differ from a plain program's by a relative error of at most 0.0034.
Values may be sent and summed in bfloat16 or wider, within the bound.
No kernel may reach another device: no remote copies, remote signals or barrier semaphores. Data moves between devices by JAX's collectives and lax.ppermute only.
A program may use at most 32 MiB of HBM per device.

v0:
```python
import jax
import jax.numpy as jnp
from jax import lax
from jax.sharding import PartitionSpec as P


def per_device(ratings, counts):
    row_count, panel_width = ratings.shape
    block_rows = row_count // counts.shape[0]
    live_rows = (
        (counts[:, None] > jnp.arange(block_rows)[None, :]).reshape(row_count).astype(jnp.float32)
    )
    values = ratings.astype(jnp.float32)
    total_items = panel_width * lax.axis_size("item")
    share_rows = total_items // lax.axis_size("user")
    gathered = lax.all_gather(ratings, "item", axis=1, tiled=True)
    square_part = jnp.sum(values * values, axis=1)
    square_sum = lax.psum(square_part, "item")
    user_scale = live_rows / jnp.sqrt(square_sum / total_items + 1e-05)
    weighted = (user_scale[:, None] * values).astype(jnp.bfloat16)
    own_degree = jnp.sum(values * weighted.astype(jnp.float32), axis=0)
    panel_sum = lax.psum(own_degree, "user")
    full_degree = lax.all_gather(panel_sum, "item", axis=0, tiled=True)
    inverse_root = 1.0 / jnp.sqrt(full_degree)
    column_inverse = lax.dynamic_slice_in_dim(
        inverse_root, lax.axis_index("item") * panel_width, panel_width
    )
    product = lax.dot_general(
        gathered, weighted, (((0,), (0,)), ((), ())), preferred_element_type=jnp.float32
    )
    gram_block = lax.psum_scatter(product, "user", scatter_dimension=0, tiled=True)
    row_inverse = lax.dynamic_slice_in_dim(
        inverse_root, lax.axis_index("user") * share_rows, share_rows
    )
    scaled = gram_block * row_inverse[:, None] * column_inverse[None, :]
    return scaled.astype(jnp.bfloat16)


def solution(mesh):
    in_specs = (P("user", "item"), P("user"))
    out_specs = P("user", "item")
    return jax.shard_map(
        per_device, mesh=mesh, in_specs=in_specs, out_specs=out_specs, check_vma=False
    )
```

profile of v0, /device:TPU:16, one launch (start us, length us, event | category | flops | bytes accessed | tf_op | source)
XLA Modules:
  0.0 255.3 jit_solution(5604534101060439710)
XLA Ops:
  6.5 0.0 all-gather.3.cloned.1.call-start
  6.5 0.7 all-gather.3.cloned.1.call-update
  7.3 0.0 reduce-scatter.4.cloned.1.call-start
  7.3 0.7 iota_compare_fusion
  8.0 0.1 gt.20
  8.1 1.1 fusion
  9.2 33.3 %psum.14 = f32[384]{0:T(512)S(1)} all-reduce(f32[384]{0:T(512)S(1)} %fusion), channel_id=1, replica_groups=mesh['user'=64,'item'=12] {'item'}, use_global_device_ids=true, to_apply=%region_1.0 | all-reduce | flops 384 | bytes 3072 | tf_op jit(solution)/shard_map/psum | solution.py:18
  42.5 42.6 %all-gather.3.cloned.1.call-done = bf16[384,3072]{1,0:T(8,128)(2,1)} async-done(((bf16[384,256]{1,0:T(8,128)(2,1)}), bf16[384,3072]{1,0:T(8,128)(2,1)}) %all-gather.3.cloned.1.call-update) | async-done | bytes 2359312 | tf_op jit(solution)/shard_map/all_gather | solution.py:16
  85.1 2.9 %convolution_bitcast_fusion = f32[3072,256]{0,1:T(8,128)S(1)} fusion(bf16[384,3072]{1,0:T(8,128)(2,1)} %all-gather.3.cloned.1.call-done, bf16[384,256]{1,0:T(8,128)(2,1)} %param.2, f32[384]{0:T(512)S(1)} %rsqrt_select_fusion), kind=kOutput, calls=%fused_computation | convolution fusion | flops 604274688 | bytes 5703168 | tf_op jit(solution)/shard_map/dot_general | solution.py:28
  88.0 2.4 copy.6
  90.3 0.0 copy-start
  90.3 0.0 reduce-scatter.4.cloned.1.call-update
  90.4 0.9 copy-done
  91.3 0.1 fusion.2
  91.4 114.1 %psum.15 = f32[256]{0:T(256)S(1)} all-reduce(f32[256]{0:T(256)S(1)} %fusion.2), channel_id=1, replica_groups=mesh['user'=64,'item'=12] {'user'}, use_global_device_ids=true, to_apply=%region_4.0 | all-reduce | flops 256 | bytes 2048 | tf_op jit(solution)/shard_map/psum | solution.py:22
  205.5 21.5 %all-gather = f32[12,1,256]{2,1,0:T(1,128)S(1)} all-gather(f32[1,1,256]{2,1,0:T(1,128)S(1)} %bitcast.8), channel_id=1, replica_groups=mesh['user'=64,'item'=12] {'item'}, dimensions={0}, use_global_device_ids=true | all-gather | bytes 13312 | tf_op jit(solution)/shard_map/all_gather | solution.py:23
  227.1 0.1 dynamic_slice.6
  227.2 0.1 dynamic_slice.7
  227.3 19.7 %reduce-scatter.4.cloned.1.call-done = f32[48,256]{1,0:T(8,128)} async-done(((f32[3072,256]{1,0:T(8,128)}), f32[48,256]{1,0:T(8,128)}) %reduce-scatter.4.cloned.1.call-update) | async-done | bytes 49168 | tf_op jit(solution)/shard_map/reduce_scatter | solution.py:31
  247.0 1.5 multiply_convert_fusion
  (2 shorter events, 0.0 us)
Async XLA Ops:
  6.5 78.6 %all-gather.3.cloned.1.call-start = ((), (), s32[]{:S(2)}) async-start(), calls=%async_computation.1 | async-start | bytes 2555904 | tf_op jit(solution)/shard_map/all_gather | solution.py:16
  7.3 239.7 %reduce-scatter.4.cloned.1.call-start = ((), (), s32[]{:S(2)}) async-start(), calls=%async_computation.2 | async-start | bytes 3194880 | tf_op jit(solution)/shard_map/reduce_scatter | solution.py:31
  90.3 0.9 copy-start
Sparse Core Ops, SparseCore 0:
  9.7 75.3 all-gather.2
  90.5 156.4 reduce-scatter.3
where the time goes:
time: 256 us; the launch traced here: 255 us
  blocking collectives  169 us (66%)
  waiting for transfers between devices  63 us (25%)
  between operations  13.4 us (5%)
  local copies, waits for them, and re-layouts  3.52 us (1%)
  other arithmetic  3.42 us (1%)
  matrix products  2.87 us (1%)
    psum x1, blocking collectives, per_device(): panel_sum = lax.psum(own_degree, 'user')  114 us
    all_gather x1, waiting for transfers between devices, per_device(): gathered = lax.all_gather(ratings, 'item', axis=1, tiled=True)  42.6 us
    psum x1, blocking collectives, per_device(): square_sum = lax.psum(square_part, 'item')  33.3 us
    all_gather x1, blocking collectives, per_device(): full_degree = lax.all_gather(panel_sum, 'item', axis=0, tiled=True)  21.5 us
    reduce_scatter x1, waiting for transfers between devices, per_device(): lax.psum_scatter(product, 'user', scatter_dimension=0, tiled=True)  19.7 us
  transfers between devices with their start and end apart: 2, of which 2 were waited for; matrix products, arithmetic and copies ran while one was open for 1% of the time, Pallas kernels for 0%

commit v1 on v0

v1 whole, which is shorter than its diff:
```python
import functools

import jax
import jax.numpy as jnp
from jax import lax
from jax.experimental import pallas as pl
from jax.experimental.pallas import tpu as pltpu
from jax.sharding import Mesh, PartitionSpec as P

X, Y, CORES, PANELS = 4, 8, 2, 12
SLOTS = X * Y
BLOCK = 64
ITEMS = 3072
SHARE = 48
SLOT_ROWS = SHARE + 8


def split_rows(total):
    high = total.astype(jnp.bfloat16).astype(jnp.float32)
    first = lax.broadcasted_iota(jnp.int32, total.shape, 0) < 4
    return jnp.where(first, high, total - high)


def partial_kernel(place_ref, counts_ref, *refs):
    panels, (keep_ref, send_ref, gram_ref, degree_ref) = refs[:PANELS], refs[PANELS:]
    me, core = place_ref[0], place_ref[1]
    rows, width = panels[0].shape
    squares = jnp.zeros((rows, width), jnp.float32)
    for panel in panels:
        values = panel[...].astype(jnp.float32)
        squares = squares + values * values
    square_sum = jnp.sum(squares, axis=1, keepdims=True)
    position = lax.broadcasted_iota(jnp.int32, (BLOCK, 1), 0)
    live = jnp.concatenate(
        [(position < counts_ref[i]).astype(jnp.float32) for i in range(rows // BLOCK)], axis=0
    )
    scale = live / jnp.sqrt(square_sum / ITEMS + 1e-05)
    weighted = (scale * panels[0][...].astype(jnp.float32)).astype(jnp.bfloat16)
    for k, panel in enumerate(panels):
        owner = lax.rem(me + k, PANELS)
        product = lax.dot_general(
            panel[...], weighted, (((0,), (0,)), ((), ())), preferred_element_type=jnp.float32
        )
        gram_ref[pl.ds(pl.multiple_of(owner * width, width), width), :] = product
        values = panel[...].astype(jnp.float32)
        own_weighted = (scale * values).astype(jnp.bfloat16).astype(jnp.float32)
        degree_ref[pl.ds(owner, 1), :] = jnp.sum(values * own_weighted, axis=0, keepdims=True)
    column_degree = degree_ref[pl.ds(me, 1), :]
    blank = jnp.zeros((1, width), jnp.float32)
    for slot in range(SLOTS):
        for mine in (True, False):
            start = (2 * slot + (core if mine else 1 - core)) * SHARE
            low = degree_ref[pl.ds(lax.shift_right_logical(start, 8), 1), :]
            high = degree_ref[pl.ds(lax.shift_right_logical(start + SHARE - 1, 8), 1), :]
            block = gram_ref[pl.ds(pl.multiple_of(start, 16), SHARE), :]
            four = [column_degree, low, high, blank]
            if mine:
                extra = jnp.concatenate(four + [blank] * 4, axis=0)
                keep_ref[slot] = jnp.concatenate([block, extra], axis=0)
            else:
                extra = split_rows(jnp.concatenate(four + four, axis=0))
                send_ref[slot] = jnp.concatenate([block, extra], axis=0).astype(jnp.bfloat16)


def add_kernel(keep_ref, got_ref, out_ref):
    for slot in range(SLOTS):
        total = keep_ref[slot] + got_ref[slot].astype(jnp.float32)
        extra = total[SHARE:]
        extra = split_rows(extra + pltpu.roll(extra, 4, 0))
        out_ref[slot] = jnp.concatenate([total[:SHARE], extra], axis=0).astype(jnp.bfloat16)


def finish_kernel(place_ref, got_ref, out_ref):
    start = place_ref[2] * SHARE
    offset = start - lax.shift_left(lax.shift_right_logical(start, 8), 8)
    total = got_ref[0].astype(jnp.float32)
    for slot in range(1, SLOTS):
        total = total + got_ref[slot].astype(jnp.float32)
    extra = total[SHARE:]
    extra = extra + pltpu.roll(extra, 4, 0)
    width = total.shape[1]
    lane = lax.broadcasted_iota(jnp.int32, (SHARE, width), 1)
    row = lax.broadcasted_iota(jnp.int32, (SHARE, width), 0) + offset
    row_degree = jnp.sum(
        jnp.where(lane == row, extra[1:2], 0.0) + jnp.where(lane + width == row, extra[2:3], 0.0),
        axis=1,
        keepdims=True,
    )
    row_inverse = 1.0 / jnp.sqrt(row_degree)
    column_inverse = 1.0 / jnp.sqrt(extra[0:1])
    out_ref[...] = (total[:SHARE] * row_inverse * column_inverse).astype(jnp.bfloat16)


VMEM = pl.BlockSpec(memory_space=pltpu.VMEM)
SMEM = pl.BlockSpec(memory_space=pltpu.SMEM)
PARAMS = pltpu.CompilerParams(vmem_limit_bytes=48 * 1024 * 1024)


def per_device(ratings, counts):
    width = ratings.shape[1]
    x, y, core, me = (lax.axis_index(name) for name in ("x", "y", "core", "z"))
    place = jnp.stack([me, core, (x * Y + y) * CORES + core]).astype(jnp.int32)

    def step(array, by):
        return lax.ppermute(array, "z", [(i, (i + by) % PANELS) for i in range(PANELS)])

    panels = [ratings] + [None] * (PANELS - 1)
    up = down = ratings
    for hop in range(1, 7):
        up = step(up, 1)
        panels[PANELS - hop] = up
        if hop < 6:
            down = step(down, -1)
            panels[hop] = down
    slots = (SLOTS, SLOT_ROWS, width)
    keep, send = pl.pallas_call(
        partial_kernel,
        out_shape=(
            jax.ShapeDtypeStruct(slots, jnp.float32),
            jax.ShapeDtypeStruct(slots, jnp.bfloat16),
        ),
        in_specs=[SMEM, SMEM] + [VMEM] * PANELS,
        out_specs=(VMEM, VMEM),
        scratch_shapes=[
            pltpu.VMEM((ITEMS, width), jnp.float32),
            pltpu.VMEM((16, width), jnp.float32),
        ],
        compiler_params=PARAMS,
        name="partial",
    )(place, counts, *panels)
    got = lax.ppermute(send, "core", [(0, 1), (1, 0)])
    total = pl.pallas_call(
        add_kernel,
        out_shape=jax.ShapeDtypeStruct(slots, jnp.bfloat16),
        in_specs=[VMEM, VMEM],
        out_specs=VMEM,
        compiler_params=PARAMS,
        name="add",
    )(keep, got)
    parts = lax.all_to_all(total, ("x", "y"), 0, 0, tiled=True)
    return pl.pallas_call(
        finish_kernel,
        out_shape=jax.ShapeDtypeStruct((SHARE, width), jnp.bfloat16),
        in_specs=[SMEM, VMEM],
        out_specs=VMEM,
        compiler_params=PARAMS,
        name="finish",
    )(place, parts)


def solution(mesh):
    fine = Mesh(mesh.devices.reshape(X, Y, CORES, PANELS), ("x", "y", "core", "z"))
    users = ("x", "y", "core")
    return jax.shard_map(
        per_device,
        mesh=fine,
        in_specs=(P(users, "z"), P(users)),
        out_specs=P(users, "z"),
        check_vma=False,
    )
```

time: 256 us -> 112 us (0.44)
  the two profiles are of different devices: /device:TPU:16 before, /device:TPU:8 now
where the time goes in v1:
time: 112 us; the launch traced here: 111 us
  starting transfers between devices  48.5 us (43%)
  blocking collectives  36.1 us (32%)
  waiting for transfers between devices  19.6 us (18%)
  Pallas kernels  5.05 us (5%)
  local copies, waits for them, and re-layouts  1.58 us (1%)
    ppermute x11, starting transfers between devices, step(): lax.ppermute(array, 'z', [(i, (i + by) % PANELS) for i in range(PANELS)])  46.6 us
    all_to_all x1, blocking collectives, per_device(): parts = lax.all_to_all(total, ('x', 'y'), 0, 0, tiled=True)  36.1 us
    ppermute x11, waiting for transfers between devices, step(): lax.ppermute(array, 'z', [(i, (i + by) % PANELS) for i in range(PANELS)])  17.1 us
    pallas_call x1, Pallas kernels, per_device(): pl.pallas_call(partial_kernel, out_shape=(jax.ShapeDtypeStruct(slots, jnp...  3.5 us
    ppermute x1, waiting for transfers between devices, per_device(): got = lax.ppermute(send, 'core', [(0, 1), (1, 0)])  2.44 us
  transfers between devices with their start and end apart: 12, of which 7 were waited for; matrix products, arithmetic and copies ran while one was open for 0% of the time, Pallas kernels for 0%

profile of v1, /device:TPU:8, one launch (start us, length us, event | category | flops | bytes accessed | tf_op | source)
XLA Modules:
  0.0 111.0 jit_solution(9528365384409553029)
XLA Ops:
  0.0 4.3 %collective-permute-start.5 = (bf16[384,256]{1,0:T(8,128)(2,1)}, bf16[384,256]{1,0:T(8,128)(2,1)S(1)}, u32[]{:S(2)}, u32[]{:S(2)}) collective-permute-start(bf16[384,256]{1,0:T(8,128)(2,1)} %refs_0_.1), channel_id=1, source_target_pairs={{0,1},{1,2},{2,3},{3,4},{4,5},{5,6},{6,7},{7,8},{8,9},{9,10},{10,1... | collective-permute-start | bytes 589832 | tf_op jit(solution)/shard_map/ppermute | solution.py:105
  4.3 12.2 %collective-permute-start = (bf16[384,256]{1,0:T(8,128)(2,1)}, bf16[384,256]{1,0:T(8,128)(2,1)S(1)}, u32[]{:S(2)}, u32[]{:S(2)}) collective-permute-start(bf16[384,256]{1,0:T(8,128)(2,1)} %refs_0_.1), channel_id=1, source_target_pairs={{0,11},{1,0},{2,1},{3,2},{4,3},{5,4},{6,5},{7,6},{8,7},{9,8},{10,9... | collective-permute-start | bytes 589832 | tf_op jit(solution)/shard_map/ppermute | solution.py:105
  16.5 3.2 %collective-permute-done.5.refs_11_ = bf16[384,256]{1,0:T(8,128)(2,1)S(1)} collective-permute-done((bf16[384,256]{1,0:T(8,128)(2,1)}, bf16[384,256]{1,0:T(8,128)(2,1)S(1)}, u32[]{:S(2)}, u32[]{:S(2)}) %collective-permute-start.5) | collective-permute-done | bytes 196640 | tf_op jit(solution)/shard_map/ppermute | solution.py:105
  19.7 1.9 %collective-permute-start.6 = (bf16[384,256]{1,0:T(8,128)(2,1)S(1)}, bf16[384,256]{1,0:T(8,128)(2,1)S(1)}, u32[]{:S(2)}, u32[]{:S(2)}) collective-permute-start(bf16[384,256]{1,0:T(8,128)(2,1)S(1)} %collective-permute-done.5.refs_11_), channel_id=1, source_target_pairs={{0,1},{1,2},{2,3},{3,4},{4,5},{5,6},{6,7},{7,8},{8,9},{9,10},{10,1... | collective-permute-start | bytes 589832 | tf_op jit(solution)/shard_map/ppermute | solution.py:105
  21.6 0.0 collective-permute-done.refs_1_
  21.6 5.1 %collective-permute-start.1 = (bf16[384,256]{1,0:T(8,128)(2,1)S(1)}, bf16[384,256]{1,0:T(8,128)(2,1)S(1)}, u32[]{:S(2)}, u32[]{:S(2)}) collective-permute-start(bf16[384,256]{1,0:T(8,128)(2,1)S(1)} %collective-permute-done.refs_1_), channel_id=1, source_target_pairs={{0,11},{1,0},{2,1},{3,2},{4,3},{5,4},{6,5},{7,6},{8,7},{9,8},{10,9... | collective-permute-start | bytes 589832 | tf_op jit(solution)/shard_map/ppermute | solution.py:105
  26.7 2.1 %collective-permute-done.6.refs_10_ = bf16[384,256]{1,0:T(8,128)(2,1)S(1)} collective-permute-done((bf16[384,256]{1,0:T(8,128)(2,1)S(1)}, bf16[384,256]{1,0:T(8,128)(2,1)S(1)}, u32[]{:S(2)}, u32[]{:S(2)}) %collective-permute-start.6) | collective-permute-done | bytes 196640 | tf_op jit(solution)/shard_map/ppermute | solution.py:105
  28.9 1.9 %collective-permute-start.7 = (bf16[384,256]{1,0:T(8,128)(2,1)S(1)}, bf16[384,256]{1,0:T(8,128)(2,1)S(1)}, u32[]{:S(2)}, u32[]{:S(2)}) collective-permute-start(bf16[384,256]{1,0:T(8,128)(2,1)S(1)} %collective-permute-done.6.refs_10_), channel_id=1, source_target_pairs={{0,1},{1,2},{2,3},{3,4},{4,5},{5,6},{6,7},{7,8},{8,9},{9,10},{10,1... | collective-permute-start | bytes 589832 | tf_op jit(solution)/shard_map/ppermute | solution.py:105
  30.8 0.0 collective-permute-done.1.refs_2_
  30.8 5.1 %collective-permute-start.2 = (bf16[384,256]{1,0:T(8,128)(2,1)S(1)}, bf16[384,256]{1,0:T(8,128)(2,1)S(1)}, u32[]{:S(2)}, u32[]{:S(2)}) collective-permute-start(bf16[384,256]{1,0:T(8,128)(2,1)S(1)} %collective-permute-done.1.refs_2_), channel_id=1, source_target_pairs={{0,11},{1,0},{2,1},{3,2},{4,3},{5,4},{6,5},{7,6},{8,7},{9,8},{10,9... | collective-permute-start | bytes 589832 | tf_op jit(solution)/shard_map/ppermute | solution.py:105
  35.9 1.7 %collective-permute-done.7.refs_9_ = bf16[384,256]{1,0:T(8,128)(2,1)S(1)} collective-permute-done((bf16[384,256]{1,0:T(8,128)(2,1)S(1)}, bf16[384,256]{1,0:T(8,128)(2,1)S(1)}, u32[]{:S(2)}, u32[]{:S(2)}) %collective-permute-start.7) | collective-permute-done | bytes 196640 | tf_op jit(solution)/shard_map/ppermute | solution.py:105
  37.6 1.9 %collective-permute-start.8 = (bf16[384,256]{1,0:T(8,128)(2,1)S(1)}, bf16[384,256]{1,0:T(8,128)(2,1)S(1)}, u32[]{:S(2)}, u32[]{:S(2)}) collective-permute-start(bf16[384,256]{1,0:T(8,128)(2,1)S(1)} %collective-permute-done.7.refs_9_), channel_id=1, source_target_pairs={{0,1},{1,2},{2,3},{3,4},{4,5},{5,6},{6,7},{7,8},{8,9},{9,10},{10,1... | collective-permute-start | bytes 589832 | tf_op jit(solution)/shard_map/ppermute | solution.py:105
  39.5 0.0 collective-permute-done.2.refs_3_
  39.6 5.1 %collective-permute-start.3 = (bf16[384,256]{1,0:T(8,128)(2,1)S(1)}, bf16[384,256]{1,0:T(8,128)(2,1)S(1)}, u32[]{:S(2)}, u32[]{:S(2)}) collective-permute-start(bf16[384,256]{1,0:T(8,128)(2,1)S(1)} %collective-permute-done.2.refs_3_), channel_id=1, source_target_pairs={{0,11},{1,0},{2,1},{3,2},{4,3},{5,4},{6,5},{7,6},{8,7},{9,8},{10,9... | collective-permute-start | bytes 589832 | tf_op jit(solution)/shard_map/ppermute | solution.py:105
  44.7 1.7 %collective-permute-done.8.refs_8_ = bf16[384,256]{1,0:T(8,128)(2,1)S(1)} collective-permute-done((bf16[384,256]{1,0:T(8,128)(2,1)S(1)}, bf16[384,256]{1,0:T(8,128)(2,1)S(1)}, u32[]{:S(2)}, u32[]{:S(2)}) %collective-permute-start.8) | collective-permute-done | bytes 196640 | tf_op jit(solution)/shard_map/ppermute | solution.py:105
  46.4 1.9 %collective-permute-start.9 = (bf16[384,256]{1,0:T(8,128)(2,1)S(1)}, bf16[384,256]{1,0:T(8,128)(2,1)S(1)}, u32[]{:S(2)}, u32[]{:S(2)}) collective-permute-start(bf16[384,256]{1,0:T(8,128)(2,1)S(1)} %collective-permute-done.8.refs_8_), channel_id=1, source_target_pairs={{0,1},{1,2},{2,3},{3,4},{4,5},{5,6},{6,7},{7,8},{8,9},{9,10},{10,1... | collective-permute-start | bytes 589832 | tf_op jit(solution)/shard_map/ppermute | solution.py:105
  48.3 0.0 collective-permute-done.3.refs_4_
  48.3 5.1 %collective-permute-start.4 = (bf16[384,256]{1,0:T(8,128)(2,1)S(1)}, bf16[384,256]{1,0:T(8,128)(2,1)S(1)}, u32[]{:S(2)}, u32[]{:S(2)}) collective-permute-start(bf16[384,256]{1,0:T(8,128)(2,1)S(1)} %collective-permute-done.3.refs_4_), channel_id=1, source_target_pairs={{0,11},{1,0},{2,1},{3,2},{4,3},{5,4},{6,5},{7,6},{8,7},{9,8},{10,9... | collective-permute-start | bytes 589832 | tf_op jit(solution)/shard_map/ppermute | solution.py:105
  53.5 1.7 %collective-permute-done.9.refs_7_ = bf16[384,256]{1,0:T(8,128)(2,1)S(1)} collective-permute-done((bf16[384,256]{1,0:T(8,128)(2,1)S(1)}, bf16[384,256]{1,0:T(8,128)(2,1)S(1)}, u32[]{:S(2)}, u32[]{:S(2)}) %collective-permute-start.9) | collective-permute-done | bytes 196640 | tf_op jit(solution)/shard_map/ppermute | solution.py:105
  55.2 1.9 %collective-permute-start.10 = (bf16[384,256]{1,0:T(8,128)(2,1)S(1)}, bf16[384,256]{1,0:T(8,128)(2,1)S(1)}, u32[]{:S(2)}, u32[]{:S(2)}) collective-permute-start(bf16[384,256]{1,0:T(8,128)(2,1)S(1)} %collective-permute-done.9.refs_7_), channel_id=1, source_target_pairs={{0,1},{1,2},{2,3},{3,4},{4,5},{5,6},{6,7},{7,8},{8,9},{9,10},{10,1... | collective-permute-start | bytes 589832 | tf_op jit(solution)/shard_map/ppermute | solution.py:105
  57.1 0.1 pad_add_fusion.place_ref
  57.2 0.0 collective-permute-done.4.refs_5_
  57.2 6.7 %collective-permute-done.10.refs_6_ = bf16[384,256]{1,0:T(8,128)(2,1)S(1)} collective-permute-done((bf16[384,256]{1,0:T(8,128)(2,1)S(1)}, bf16[384,256]{1,0:T(8,128)(2,1)S(1)}, u32[]{:S(2)}, u32[]{:S(2)}) %collective-permute-start.10) | collective-permute-done | bytes 196640 | tf_op jit(solution)/shard_map/ppermute | solution.py:105
  63.9 0.0 copy-start
  63.9 0.9 copy-done
  64.8 0.0 copy-start.1
  64.8 0.7 copy-done.1
  65.5 3.5 %partial.1 = (f32[32,56,256]{2,1,0:T(8,128)S(1)}, bf16[32,56,256]{2,1,0:T(8,128)(2,1)S(1)}) custom-call(s32[3]{0:T(128)S(1)} %pad_add_fusion.place_ref, s32[6]{0:T(128)S(1)} %copy-done.1, bf16[384,256]{1,0:T(8,128)(2,1)S(1)} %copy-done, bf16[384,256]{1,0:T(8,128)(2,1)S(1)} %collective-permute-done.refs_1_, ...), custom_call_target="tpu_custom_call" | custom-call | tf_op jit(solution)/shard_map/partial/pallas_call | solution.py:116
  69.0 1.9 %collective-permute-start.11 = (bf16[32,56,256]{2,1,0:T(8,128)(2,1)S(1)}, bf16[32,56,256]{2,1,0:T(8,128)(2,1)S(1)}, u32[]{:S(2)}, u32[]{:S(2)}) collective-permute-start(bf16[32,56,256]{2,1,0:T(8,128)(2,1)S(1)} %get-tuple-element.8), channel_id=1, source_target_pairs={{0,12},{12,0},{1,13},{13,1},{2,14},{14,2},{3,15},{15,3},{4,16},{16... | collective-permute-start | bytes 2752520 | tf_op jit(solution)/shard_map/ppermute | solution.py:131
  70.9 2.4 %collective-permute-done.11.got_ref = bf16[32,56,256]{2,1,0:T(8,128)(2,1)S(1)} collective-permute-done((bf16[32,56,256]{2,1,0:T(8,128)(2,1)S(1)}, bf16[32,56,256]{2,1,0:T(8,128)(2,1)S(1)}, u32[]{:S(2)}, u32[]{:S(2)}) %collective-permute-start.11) | collective-permute-done | bytes 917536 | tf_op jit(solution)/shard_map/ppermute | solution.py:131
  73.4 0.3 add.13
  73.6 36.1 %all_to_all.5.got_ref = bf16[32,56,256]{2,1,0:T(8,128)(2,1)S(1)} all-to-all(bf16[32,56,256]{2,1,0:T(8,128)(2,1)S(1)} %add.13), channel_id=1, replica_groups=mesh['x'=4,'y'=8,'core'=2,'z'=12] {'x','y'}, dimensions={0} | all-to-all | bytes 1835008 | tf_op jit(solution)/shard_map/all_to_all | solution.py:140
  109.7 1.3 %finish.1 = bf16[48,256]{1,0:T(8,128)(2,1)} custom-call(s32[3]{0:T(128)S(1)} %pad_add_fusion.place_ref, bf16[32,56,256]{2,1,0:T(8,128)(2,1)S(1)} %all_to_all.5.got_ref), custom_call_target="tpu_custom_call" | custom-call | tf_op jit(solution)/shard_map/finish/pallas_call | solution.py:141
Async XLA Ops:
  0.0 19.7 %collective-permute-start.5 = (bf16[384,256]{1,0:T(8,128)(2,1)}, bf16[384,256]{1,0:T(8,128)(2,1)S(1)}, u32[]{:S(2)}, u32[]{:S(2)}) collective-permute-start(bf16[384,256]{1,0:T(8,128)(2,1)} %refs_0_.1), channel_id=1, source_target_pairs={{0,1},{1,2},{2,3},{3,4},{4,5},{5,6},{6,7},{7,8},{8,9},{9,10},{10,1... | collective-permute-start | bytes 589832 | tf_op jit(solution)/shard_map/ppermute | solution.py:105
  4.3 17.3 %collective-permute-start = (bf16[384,256]{1,0:T(8,128)(2,1)}, bf16[384,256]{1,0:T(8,128)(2,1)S(1)}, u32[]{:S(2)}, u32[]{:S(2)}) collective-permute-start(bf16[384,256]{1,0:T(8,128)(2,1)} %refs_0_.1), channel_id=1, source_target_pairs={{0,11},{1,0},{2,1},{3,2},{4,3},{5,4},{6,5},{7,6},{8,7},{9,8},{10,9... | collective-permute-start | bytes 589832 | tf_op jit(solution)/shard_map/ppermute | solution.py:105
  19.7 9.2 %collective-permute-start.6 = (bf16[384,256]{1,0:T(8,128)(2,1)S(1)}, bf16[384,256]{1,0:T(8,128)(2,1)S(1)}, u32[]{:S(2)}, u32[]{:S(2)}) collective-permute-start(bf16[384,256]{1,0:T(8,128)(2,1)S(1)} %collective-permute-done.5.refs_11_), channel_id=1, source_target_pairs={{0,1},{1,2},{2,3},{3,4},{4,5},{5,6},{6,7},{7,8},{8,9},{9,10},{10,1... | collective-permute-start | bytes 589832 | tf_op jit(solution)/shard_map/ppermute | solution.py:105
  21.6 9.2 %collective-permute-start.1 = (bf16[384,256]{1,0:T(8,128)(2,1)S(1)}, bf16[384,256]{1,0:T(8,128)(2,1)S(1)}, u32[]{:S(2)}, u32[]{:S(2)}) collective-permute-start(bf16[384,256]{1,0:T(8,128)(2,1)S(1)} %collective-permute-done.refs_1_), channel_id=1, source_target_pairs={{0,11},{1,0},{2,1},{3,2},{4,3},{5,4},{6,5},{7,6},{8,7},{9,8},{10,9... | collective-permute-start | bytes 589832 | tf_op jit(solution)/shard_map/ppermute | solution.py:105
  28.9 8.8 %collective-permute-start.7 = (bf16[384,256]{1,0:T(8,128)(2,1)S(1)}, bf16[384,256]{1,0:T(8,128)(2,1)S(1)}, u32[]{:S(2)}, u32[]{:S(2)}) collective-permute-start(bf16[384,256]{1,0:T(8,128)(2,1)S(1)} %collective-permute-done.6.refs_10_), channel_id=1, source_target_pairs={{0,1},{1,2},{2,3},{3,4},{4,5},{5,6},{6,7},{7,8},{8,9},{9,10},{10,1... | collective-permute-start | bytes 589832 | tf_op jit(solution)/shard_map/ppermute | solution.py:105
  30.8 8.8 %collective-permute-start.2 = (bf16[384,256]{1,0:T(8,128)(2,1)S(1)}, bf16[384,256]{1,0:T(8,128)(2,1)S(1)}, u32[]{:S(2)}, u32[]{:S(2)}) collective-permute-start(bf16[384,256]{1,0:T(8,128)(2,1)S(1)} %collective-permute-done.1.refs_2_), channel_id=1, source_target_pairs={{0,11},{1,0},{2,1},{3,2},{4,3},{5,4},{6,5},{7,6},{8,7},{9,8},{10,9... | collective-permute-start | bytes 589832 | tf_op jit(solution)/shard_map/ppermute | solution.py:105
  37.6 8.8 %collective-permute-start.8 = (bf16[384,256]{1,0:T(8,128)(2,1)S(1)}, bf16[384,256]{1,0:T(8,128)(2,1)S(1)}, u32[]{:S(2)}, u32[]{:S(2)}) collective-permute-start(bf16[384,256]{1,0:T(8,128)(2,1)S(1)} %collective-permute-done.7.refs_9_), channel_id=1, source_target_pairs={{0,1},{1,2},{2,3},{3,4},{4,5},{5,6},{6,7},{7,8},{8,9},{9,10},{10,1... | collective-permute-start | bytes 589832 | tf_op jit(solution)/shard_map/ppermute | solution.py:105
  39.6 8.8 %collective-permute-start.3 = (bf16[384,256]{1,0:T(8,128)(2,1)S(1)}, bf16[384,256]{1,0:T(8,128)(2,1)S(1)}, u32[]{:S(2)}, u32[]{:S(2)}) collective-permute-start(bf16[384,256]{1,0:T(8,128)(2,1)S(1)} %collective-permute-done.2.refs_3_), channel_id=1, source_target_pairs={{0,11},{1,0},{2,1},{3,2},{4,3},{5,4},{6,5},{7,6},{8,7},{9,8},{10,9... | collective-permute-start | bytes 589832 | tf_op jit(solution)/shard_map/ppermute | solution.py:105
  46.4 8.8 %collective-permute-start.9 = (bf16[384,256]{1,0:T(8,128)(2,1)S(1)}, bf16[384,256]{1,0:T(8,128)(2,1)S(1)}, u32[]{:S(2)}, u32[]{:S(2)}) collective-permute-start(bf16[384,256]{1,0:T(8,128)(2,1)S(1)} %collective-permute-done.8.refs_8_), channel_id=1, source_target_pairs={{0,1},{1,2},{2,3},{3,4},{4,5},{5,6},{6,7},{7,8},{8,9},{9,10},{10,1... | collective-permute-start | bytes 589832 | tf_op jit(solution)/shard_map/ppermute | solution.py:105
  48.3 8.8 %collective-permute-start.4 = (bf16[384,256]{1,0:T(8,128)(2,1)S(1)}, bf16[384,256]{1,0:T(8,128)(2,1)S(1)}, u32[]{:S(2)}, u32[]{:S(2)}) collective-permute-start(bf16[384,256]{1,0:T(8,128)(2,1)S(1)} %collective-permute-done.3.refs_4_), channel_id=1, source_target_pairs={{0,11},{1,0},{2,1},{3,2},{4,3},{5,4},{6,5},{7,6},{8,7},{9,8},{10,9... | collective-permute-start | bytes 589832 | tf_op jit(solution)/shard_map/ppermute | solution.py:105
  55.2 8.8 %collective-permute-start.10 = (bf16[384,256]{1,0:T(8,128)(2,1)S(1)}, bf16[384,256]{1,0:T(8,128)(2,1)S(1)}, u32[]{:S(2)}, u32[]{:S(2)}) collective-permute-start(bf16[384,256]{1,0:T(8,128)(2,1)S(1)} %collective-permute-done.9.refs_7_), channel_id=1, source_target_pairs={{0,1},{1,2},{2,3},{3,4},{4,5},{5,6},{6,7},{7,8},{8,9},{9,10},{10,1... | collective-permute-start | bytes 589832 | tf_op jit(solution)/shard_map/ppermute | solution.py:105
  63.9 0.9 copy-start
  64.8 0.7 copy-start.1
  69.0 4.4 %collective-permute-start.11 = (bf16[32,56,256]{2,1,0:T(8,128)(2,1)S(1)}, bf16[32,56,256]{2,1,0:T(8,128)(2,1)S(1)}, u32[]{:S(2)}, u32[]{:S(2)}) collective-permute-start(bf16[32,56,256]{2,1,0:T(8,128)(2,1)S(1)} %get-tuple-element.8), channel_id=1, source_target_pairs={{0,12},{12,0},{1,13},{13,1},{2,14},{14,2},{3,15},{15,3},{4,16},{16... | collective-permute-start | bytes 2752520 | tf_op jit(solution)/shard_map/ppermute | solution.py:131

commit v2 on v1

--- a/solution.py
+++ b/solution.py
@@ -13,6 +13,7 @@
 ITEMS = 3072
 SHARE = 48
 SLOT_ROWS = SHARE + 8
+COUNTS = 4
 
 
 def split_rows(total):
@@ -21,18 +22,24 @@
     return jnp.where(first, high, total - high)
 
 
-def partial_kernel(place_ref, counts_ref, *refs):
-    panels, (keep_ref, send_ref, gram_ref, degree_ref) = refs[:PANELS], refs[PANELS:]
+def partial_kernel(place_ref, ratings_ref, *refs):
+    others, scratch = refs[: PANELS - 1], refs[PANELS - 1 :]
+    keep_ref, send_ref, gram_ref, degree_ref, own_ref, fetched = scratch
+    fetch = pltpu.make_async_copy(ratings_ref, own_ref, fetched)
+    fetch.start()
+    panels = (own_ref,) + others
     me, core = place_ref[0], place_ref[1]
-    rows, width = panels[0].shape
+    rows, width = own_ref.shape
     squares = jnp.zeros((rows, width), jnp.float32)
-    for panel in panels:
+    for panel in others + (own_ref,):
+        if panel is own_ref:
+            fetch.wait()
         values = panel[...].astype(jnp.float32)
         squares = squares + values * values
     square_sum = jnp.sum(squares, axis=1, keepdims=True)
     position = lax.broadcasted_iota(jnp.int32, (BLOCK, 1), 0)
     live = jnp.concatenate(
-        [(position < counts_ref[i]).astype(jnp.float32) for i in range(rows // BLOCK)], axis=0
+        [(position < place_ref[COUNTS + i]).astype(jnp.float32) for i in range(rows // BLOCK)], axis=0
     )
     scale = live / jnp.sqrt(square_sum / ITEMS + 1e-05)
     weighted = (scale * panels[0][...].astype(jnp.float32)).astype(jnp.bfloat16)
@@ -62,19 +69,37 @@
                 send_ref[slot] = jnp.concatenate([block, extra], axis=0).astype(jnp.bfloat16)
 
 
-def add_kernel(keep_ref, got_ref, out_ref):
-    for slot in range(SLOTS):
-        total = keep_ref[slot] + got_ref[slot].astype(jnp.float32)
+def add_kernel(place_ref, keep_ref, got_ref, own_ref, *send_refs):
+    x = place_ref[3]
+    for by, ref in enumerate((own_ref,) + send_refs):
+        first = lax.rem(x + by, X) * Y
+        for j in range(Y):
+            total = keep_ref[first + j] + got_ref[first + j].astype(jnp.float32)
+            extra = total[SHARE:]
+            extra = extra + pltpu.roll(extra, 4, 0)
+            if by:
+                extra = split_rows(extra)
+            else:
+                extra = 0.5 * extra
+            ref[j] = jnp.concatenate([total[:SHARE], extra], axis=0).astype(ref.dtype)
+
+
+def fold_kernel(own_ref, *refs):
+    out_ref = refs[-1]
+    for j in range(Y):
+        total = own_ref[j]
+        for ref in refs[:-1]:
+            total = total + ref[j].astype(jnp.float32)
         extra = total[SHARE:]
         extra = split_rows(extra + pltpu.roll(extra, 4, 0))
-        out_ref[slot] = jnp.concatenate([total[:SHARE], extra], axis=0).astype(jnp.bfloat16)
+        out_ref[j] = jnp.concatenate([total[:SHARE], extra], axis=0).astype(jnp.bfloat16)
 
 
 def finish_kernel(place_ref, got_ref, out_ref):
     start = place_ref[2] * SHARE
     offset = start - lax.shift_left(lax.shift_right_logical(start, 8), 8)
     total = got_ref[0].astype(jnp.float32)
-    for slot in range(1, SLOTS):
+    for slot in range(1, Y):
         total = total + got_ref[slot].astype(jnp.float32)
     extra = total[SHARE:]
     extra = extra + pltpu.roll(extra, 4, 0)
@@ -99,10 +124,11 @@
 def per_device(ratings, counts):
     width = ratings.shape[1]
     x, y, core, me = (lax.axis_index(name) for name in ("x", "y", "core", "z"))
-    place = jnp.stack([me, core, (x * Y + y) * CORES + core]).astype(jnp.int32)
+    place = jnp.stack([me, core, (x * Y + y) * CORES + core, x]).astype(jnp.int32)
+    place = jnp.concatenate([place, counts])
 
-    def step(array, by):
-        return lax.ppermute(array, "z", [(i, (i + by) % PANELS) for i in range(PANELS)])
+    def step(array, by, axis="z", size=PANELS):
+        return lax.ppermute(array, axis, [(i, (i + by) % size) for i in range(size)])
 
     panels = [ratings] + [None] * (PANELS - 1)
     up = down = ratings
@@ -119,25 +145,38 @@
             jax.ShapeDtypeStruct(slots, jnp.float32),
             jax.ShapeDtypeStruct(slots, jnp.bfloat16),
         ),
-        in_specs=[SMEM, SMEM] + [VMEM] * PANELS,
+        in_specs=[SMEM, pl.BlockSpec(memory_space=pltpu.HBM)] + [VMEM] * (PANELS - 1),
         out_specs=(VMEM, VMEM),
         scratch_shapes=[
             pltpu.VMEM((ITEMS, width), jnp.float32),
             pltpu.VMEM((16, width), jnp.float32),
+            pltpu.VMEM(ratings.shape, ratings.dtype),
+            pltpu.SemaphoreType.DMA,
         ],
         compiler_params=PARAMS,
         name="partial",
-    )(place, counts, *panels)
+    )(place, *panels)
     got = lax.ppermute(send, "core", [(0, 1), (1, 0)])
+    quarter = (Y, SLOT_ROWS, width)
+    own, *parts = pl.pallas_call(
+        add_kernel,
+        out_shape=(jax.ShapeDtypeStruct(quarter, jnp.float32),)
+        + (jax.ShapeDtypeStruct(quarter, jnp.bfloat16),) * (X - 1),
+        in_specs=[SMEM, VMEM, VMEM],
+        out_specs=(VMEM,) * X,
+        compiler_params=PARAMS,
+        name="add",
+    )(place, keep, got)
+    parts = [step(part, by, "x", X) for by, part in enumerate(parts, 1)]
     total = pl.pallas_call(
-        add_kernel,
-        out_shape=jax.ShapeDtypeStruct(slots, jnp.bfloat16),
-        in_specs=[VMEM, VMEM],
+        fold_kernel,
+        out_shape=jax.ShapeDtypeStruct(quarter, jnp.bfloat16),
+        in_specs=[VMEM] * X,
         out_specs=VMEM,
         compiler_params=PARAMS,
-        name="add",
-    )(keep, got)
-    parts = lax.all_to_all(total, ("x", "y"), 0, 0, tiled=True)
+        name="fold",
+    )(own, *parts)
+    parts = lax.all_to_all(total, "y", 0, 0, tiled=True)
     return pl.pallas_call(
         finish_kernel,
         out_shape=jax.ShapeDtypeStruct((SHARE, width), jnp.bfloat16),

time: 112 us -> 113 us (level)
  the two profiles are of different devices: /device:TPU:8 before, /device:TPU:2 now
where the time goes in v2:
time: 113 us
  starting transfers between devices  59 us (52%)
  waiting for transfers between devices  27.5 us (24%)
  blocking collectives  18.3 us (16%)
  Pallas kernels  6.1 us (5%)
  local copies, waits for them, and re-layouts  1.66 us (1%)
    ppermute x14, starting transfers between devices, step(): lax.ppermute(array, axis, [(i, (i + by) % size) for i in range(size)])  57.1 us
    ppermute x14, waiting for transfers between devices, step(): lax.ppermute(array, axis, [(i, (i + by) % size) for i in range(size)])  25 us
    all_to_all x1, blocking collectives, per_device(): parts = lax.all_to_all(total, 'y', 0, 0, tiled=True)  18.3 us
    pallas_call x1, Pallas kernels, per_device(): pl.pallas_call(partial_kernel, out_shape=(jax.ShapeDtypeStruct(slots, jnp...  3.98 us
    ppermute x1, waiting for transfers between devices, per_device(): got = lax.ppermute(send, 'core', [(0, 1), (1, 0)])  2.44 us
  transfers between devices with their start and end apart: 15, of which 9 were waited for; matrix products, arithmetic and copies ran while one was open for 1% of the time, Pallas kernels for 0%

profile of v2, /device:TPU:2, one launch (start us, length us, event | category | flops | bytes accessed | tf_op | source)
XLA Modules:
  0.0 112.7 jit_solution(4487445364467295309)
XLA Ops:
  0.0 4.3 %collective-permute-start.5 = (bf16[384,256]{1,0:T(8,128)(2,1)}, bf16[384,256]{1,0:T(8,128)(2,1)S(1)}, u32[]{:S(2)}, u32[]{:S(2)}) collective-permute-start(bf16[384,256]{1,0:T(8,128)(2,1)} %ratings_ref.1), channel_id=1, source_target_pairs={{0,1},{1,2},{2,3},{3,4},{4,5},{5,6},{6,7},{7,8},{8,9},{9,10},{10,1... | collective-permute-start | bytes 589832 | tf_op jit(solution)/shard_map/ppermute | solution.py:131
  4.3 12.2 %collective-permute-start = (bf16[384,256]{1,0:T(8,128)(2,1)}, bf16[384,256]{1,0:T(8,128)(2,1)S(1)}, u32[]{:S(2)}, u32[]{:S(2)}) collective-permute-start(bf16[384,256]{1,0:T(8,128)(2,1)} %ratings_ref.1), channel_id=1, source_target_pairs={{0,11},{1,0},{2,1},{3,2},{4,3},{5,4},{6,5},{7,6},{8,7},{9,8},{10,9... | collective-permute-start | bytes 589832 | tf_op jit(solution)/shard_map/ppermute | solution.py:131
  16.5 3.2 %collective-permute-done.5.refs_10_ = bf16[384,256]{1,0:T(8,128)(2,1)S(1)} collective-permute-done((bf16[384,256]{1,0:T(8,128)(2,1)}, bf16[384,256]{1,0:T(8,128)(2,1)S(1)}, u32[]{:S(2)}, u32[]{:S(2)}) %collective-permute-start.5) | collective-permute-done | bytes 196640 | tf_op jit(solution)/shard_map/ppermute | solution.py:131
  19.7 1.9 %collective-permute-start.6 = (bf16[384,256]{1,0:T(8,128)(2,1)S(1)}, bf16[384,256]{1,0:T(8,128)(2,1)S(1)}, u32[]{:S(2)}, u32[]{:S(2)}) collective-permute-start(bf16[384,256]{1,0:T(8,128)(2,1)S(1)} %collective-permute-done.5.refs_10_), channel_id=1, source_target_pairs={{0,1},{1,2},{2,3},{3,4},{4,5},{5,6},{6,7},{7,8},{8,9},{9,10},{10,1... | collective-permute-start | bytes 589832 | tf_op jit(solution)/shard_map/ppermute | solution.py:131
  21.6 0.0 collective-permute-done.refs_0_
  21.6 5.1 %collective-permute-start.1 = (bf16[384,256]{1,0:T(8,128)(2,1)S(1)}, bf16[384,256]{1,0:T(8,128)(2,1)S(1)}, u32[]{:S(2)}, u32[]{:S(2)}) collective-permute-start(bf16[384,256]{1,0:T(8,128)(2,1)S(1)} %collective-permute-done.refs_0_), channel_id=1, source_target_pairs={{0,11},{1,0},{2,1},{3,2},{4,3},{5,4},{6,5},{7,6},{8,7},{9,8},{10,9... | collective-permute-start | bytes 589832 | tf_op jit(solution)/shard_map/ppermute | solution.py:131
  26.7 2.1 %collective-permute-done.6.refs_9_ = bf16[384,256]{1,0:T(8,128)(2,1)S(1)} collective-permute-done((bf16[384,256]{1,0:T(8,128)(2,1)S(1)}, bf16[384,256]{1,0:T(8,128)(2,1)S(1)}, u32[]{:S(2)}, u32[]{:S(2)}) %collective-permute-start.6) | collective-permute-done | bytes 196640 | tf_op jit(solution)/shard_map/ppermute | solution.py:131
  28.9 1.9 %collective-permute-start.7 = (bf16[384,256]{1,0:T(8,128)(2,1)S(1)}, bf16[384,256]{1,0:T(8,128)(2,1)S(1)}, u32[]{:S(2)}, u32[]{:S(2)}) collective-permute-start(bf16[384,256]{1,0:T(8,128)(2,1)S(1)} %collective-permute-done.6.refs_9_), channel_id=1, source_target_pairs={{0,1},{1,2},{2,3},{3,4},{4,5},{5,6},{6,7},{7,8},{8,9},{9,10},{10,1... | collective-permute-start | bytes 589832 | tf_op jit(solution)/shard_map/ppermute | solution.py:131
  30.8 0.0 collective-permute-done.1.refs_1_
  30.8 5.1 %collective-permute-start.2 = (bf16[384,256]{1,0:T(8,128)(2,1)S(1)}, bf16[384,256]{1,0:T(8,128)(2,1)S(1)}, u32[]{:S(2)}, u32[]{:S(2)}) collective-permute-start(bf16[384,256]{1,0:T(8,128)(2,1)S(1)} %collective-permute-done.1.refs_1_), channel_id=1, source_target_pairs={{0,11},{1,0},{2,1},{3,2},{4,3},{5,4},{6,5},{7,6},{8,7},{9,8},{10,9... | collective-permute-start | bytes 589832 | tf_op jit(solution)/shard_map/ppermute | solution.py:131
  35.9 1.7 %collective-permute-done.7.refs_8_ = bf16[384,256]{1,0:T(8,128)(2,1)S(1)} collective-permute-done((bf16[384,256]{1,0:T(8,128)(2,1)S(1)}, bf16[384,256]{1,0:T(8,128)(2,1)S(1)}, u32[]{:S(2)}, u32[]{:S(2)}) %collective-permute-start.7) | collective-permute-done | bytes 196640 | tf_op jit(solution)/shard_map/ppermute | solution.py:131
  37.6 1.9 %collective-permute-start.8 = (bf16[384,256]{1,0:T(8,128)(2,1)S(1)}, bf16[384,256]{1,0:T(8,128)(2,1)S(1)}, u32[]{:S(2)}, u32[]{:S(2)}) collective-permute-start(bf16[384,256]{1,0:T(8,128)(2,1)S(1)} %collective-permute-done.7.refs_8_), channel_id=1, source_target_pairs={{0,1},{1,2},{2,3},{3,4},{4,5},{5,6},{6,7},{7,8},{8,9},{9,10},{10,1... | collective-permute-start | bytes 589832 | tf_op jit(solution)/shard_map/ppermute | solution.py:131
  39.5 0.0 collective-permute-done.2.refs_2_
  39.6 5.1 %collective-permute-start.3 = (bf16[384,256]{1,0:T(8,128)(2,1)S(1)}, bf16[384,256]{1,0:T(8,128)(2,1)S(1)}, u32[]{:S(2)}, u32[]{:S(2)}) collective-permute-start(bf16[384,256]{1,0:T(8,128)(2,1)S(1)} %collective-permute-done.2.refs_2_), channel_id=1, source_target_pairs={{0,11},{1,0},{2,1},{3,2},{4,3},{5,4},{6,5},{7,6},{8,7},{9,8},{10,9... | collective-permute-start | bytes 589832 | tf_op jit(solution)/shard_map/ppermute | solution.py:131
  44.7 1.7 %collective-permute-done.8.refs_7_ = bf16[384,256]{1,0:T(8,128)(2,1)S(1)} collective-permute-done((bf16[384,256]{1,0:T(8,128)(2,1)S(1)}, bf16[384,256]{1,0:T(8,128)(2,1)S(1)}, u32[]{:S(2)}, u32[]{:S(2)}) %collective-permute-start.8) | collective-permute-done | bytes 196640 | tf_op jit(solution)/shard_map/ppermute | solution.py:131
  46.4 1.9 %collective-permute-start.9 = (bf16[384,256]{1,0:T(8,128)(2,1)S(1)}, bf16[384,256]{1,0:T(8,128)(2,1)S(1)}, u32[]{:S(2)}, u32[]{:S(2)}) collective-permute-start(bf16[384,256]{1,0:T(8,128)(2,1)S(1)} %collective-permute-done.8.refs_7_), channel_id=1, source_target_pairs={{0,1},{1,2},{2,3},{3,4},{4,5},{5,6},{6,7},{7,8},{8,9},{9,10},{10,1... | collective-permute-start | bytes 589832 | tf_op jit(solution)/shard_map/ppermute | solution.py:131
  48.3 0.0 collective-permute-done.3.refs_3_
  48.3 5.1 %collective-permute-start.4 = (bf16[384,256]{1,0:T(8,128)(2,1)S(1)}, bf16[384,256]{1,0:T(8,128)(2,1)S(1)}, u32[]{:S(2)}, u32[]{:S(2)}) collective-permute-start(bf16[384,256]{1,0:T(8,128)(2,1)S(1)} %collective-permute-done.3.refs_3_), channel_id=1, source_target_pairs={{0,11},{1,0},{2,1},{3,2},{4,3},{5,4},{6,5},{7,6},{8,7},{9,8},{10,9... | collective-permute-start | bytes 589832 | tf_op jit(solution)/shard_map/ppermute | solution.py:131
  53.5 1.7 %collective-permute-done.9.refs_6_ = bf16[384,256]{1,0:T(8,128)(2,1)S(1)} collective-permute-done((bf16[384,256]{1,0:T(8,128)(2,1)S(1)}, bf16[384,256]{1,0:T(8,128)(2,1)S(1)}, u32[]{:S(2)}, u32[]{:S(2)}) %collective-permute-start.9) | collective-permute-done | bytes 196640 | tf_op jit(solution)/shard_map/ppermute | solution.py:131
  55.2 1.9 %collective-permute-start.10 = (bf16[384,256]{1,0:T(8,128)(2,1)S(1)}, bf16[384,256]{1,0:T(8,128)(2,1)S(1)}, u32[]{:S(2)}, u32[]{:S(2)}) collective-permute-start(bf16[384,256]{1,0:T(8,128)(2,1)S(1)} %collective-permute-done.9.refs_6_), channel_id=1, source_target_pairs={{0,1},{1,2},{2,3},{3,4},{4,5},{5,6},{6,7},{7,8},{8,9},{9,10},{10,1... | collective-permute-start | bytes 589832 | tf_op jit(solution)/shard_map/ppermute | solution.py:131
  57.1 0.7 concatenate.3.place_ref
  57.8 0.0 collective-permute-done.4.refs_4_
  57.8 6.1 %collective-permute-done.10.refs_5_ = bf16[384,256]{1,0:T(8,128)(2,1)S(1)} collective-permute-done((bf16[384,256]{1,0:T(8,128)(2,1)S(1)}, bf16[384,256]{1,0:T(8,128)(2,1)S(1)}, u32[]{:S(2)}, u32[]{:S(2)}) %collective-permute-start.10) | collective-permute-done | bytes 196640 | tf_op jit(solution)/shard_map/ppermute | solution.py:131
  63.9 0.0 copy-start
  63.9 0.9 copy-done
  64.8 4.0 %partial.1 = (f32[32,56,256]{2,1,0:T(8,128)S(1)}, bf16[32,56,256]{2,1,0:T(8,128)(2,1)S(1)}) custom-call(s32[10]{0:T(128)S(1)} %concatenate.3.place_ref, bf16[384,256]{1,0:T(8,128)(2,1)S(1)} %copy-done, bf16[384,256]{1,0:T(8,128)(2,1)S(1)} %collective-permute-done.refs_0_, bf16[384,256]{1,0:T(8,128)(2,1)S(1)} %collective-permute-done.1.refs_1_, ...), custom_call_target="tpu_custom_call" | custom-call | tf_op jit(solution)/shard_map/partial/pallas_call | solution.py:142
  68.8 1.9 %collective-permute-start.11 = (bf16[32,56,256]{2,1,0:T(8,128)(2,1)S(1)}, bf16[32,56,256]{2,1,0:T(8,128)(2,1)S(1)}, u32[]{:S(2)}, u32[]{:S(2)}) collective-permute-start(bf16[32,56,256]{2,1,0:T(8,128)(2,1)S(1)} %get-tuple-element.12), channel_id=1, source_target_pairs={{0,12},{12,0},{1,13},{13,1},{2,14},{14,2},{3,15},{15,3},{4,16},{16... | collective-permute-start | bytes 2752520 | tf_op jit(solution)/shard_map/ppermute | solution.py:159
  70.8 2.4 %collective-permute-done.11.got_ref = bf16[32,56,256]{2,1,0:T(8,128)(2,1)S(1)} collective-permute-done((bf16[32,56,256]{2,1,0:T(8,128)(2,1)S(1)}, bf16[32,56,256]{2,1,0:T(8,128)(2,1)S(1)}, u32[]{:S(2)}, u32[]{:S(2)}) %collective-permute-start.11) | collective-permute-done | bytes 917536 | tf_op jit(solution)/shard_map/ppermute | solution.py:159
  73.2 0.7 add.9
  73.9 3.4 %collective-permute-start.12 = (bf16[8,56,256]{2,1,0:T(8,128)(2,1)S(1)}, bf16[8,56,256]{2,1,0:T(8,128)(2,1)S(1)}, u32[]{:S(2)}, u32[]{:S(2)}) collective-permute-start(bf16[8,56,256]{2,1,0:T(8,128)(2,1)S(1)} %get-tuple-element.14), channel_id=1, source_target_pairs={{0,192},{192,384},{384,576},{576,0},{1,193},{193,385},{385,577},{5... | collective-permute-start | bytes 688136 | tf_op jit(solution)/shard_map/ppermute | solution.py:131
  77.3 3.0 %collective-permute-start.13 = (bf16[8,56,256]{2,1,0:T(8,128)(2,1)S(1)}, bf16[8,56,256]{2,1,0:T(8,128)(2,1)S(1)}, u32[]{:S(2)}, u32[]{:S(2)}) collective-permute-start(bf16[8,56,256]{2,1,0:T(8,128)(2,1)S(1)} %get-tuple-element.15), channel_id=1, source_target_pairs={{0,384},{192,576},{384,0},{576,192},{1,385},{193,577},{385,1},{577... | collective-permute-start | bytes 688136 | tf_op jit(solution)/shard_map/ppermute | solution.py:131
  80.4 4.1 %collective-permute-start.14 = (bf16[8,56,256]{2,1,0:T(8,128)(2,1)S(1)}, bf16[8,56,256]{2,1,0:T(8,128)(2,1)S(1)}, u32[]{:S(2)}, u32[]{:S(2)}) collective-permute-start(bf16[8,56,256]{2,1,0:T(8,128)(2,1)S(1)} %get-tuple-element.16), channel_id=1, source_target_pairs={{0,576},{192,0},{384,192},{576,384},{1,577},{193,1},{385,193},{577... | collective-permute-start | bytes 688136 | tf_op jit(solution)/shard_map/ppermute | solution.py:131
  84.5 0.0 collective-permute-done.12.refs_0_
  84.5 4.8 %collective-permute-done.13.refs_1_ = bf16[8,56,256]{2,1,0:T(8,128)(2,1)S(1)} collective-permute-done((bf16[8,56,256]{2,1,0:T(8,128)(2,1)S(1)}, bf16[8,56,256]{2,1,0:T(8,128)(2,1)S(1)}, u32[]{:S(2)}, u32[]{:S(2)}) %collective-permute-start.13) | collective-permute-done | bytes 229408 | tf_op jit(solution)/shard_map/ppermute | solution.py:131
  89.3 3.7 %collective-permute-done.14.refs_2_ = bf16[8,56,256]{2,1,0:T(8,128)(2,1)S(1)} collective-permute-done((bf16[8,56,256]{2,1,0:T(8,128)(2,1)S(1)}, bf16[8,56,256]{2,1,0:T(8,128)(2,1)S(1)}, u32[]{:S(2)}, u32[]{:S(2)}) %collective-permute-start.14) | collective-permute-done | bytes 229408 | tf_op jit(solution)/shard_map/ppermute | solution.py:131
  93.0 0.1 fold.1
  93.1 18.3 %all_to_all.5.got_ref = bf16[8,56,256]{2,1,0:T(8,128)(2,1)S(1)} all-to-all(bf16[8,56,256]{2,1,0:T(8,128)(2,1)S(1)} %fold.1), channel_id=1, replica_groups=mesh['x'=4,'y'=8,'core'=2,'z'=12] {'y'}, dimensions={0} | all-to-all | bytes 458752 | tf_op jit(solution)/shard_map/all_to_all | solution.py:179
  111.4 1.3 %finish.1 = bf16[48,256]{1,0:T(8,128)(2,1)} custom-call(s32[10]{0:T(128)S(1)} %concatenate.3.place_ref, bf16[8,56,256]{2,1,0:T(8,128)(2,1)S(1)} %all_to_all.5.got_ref), custom_call_target="tpu_custom_call" | custom-call | tf_op jit(solution)/shard_map/finish/pallas_call | solution.py:180
Async XLA Ops:
  0.0 19.7 %collective-permute-start.5 = (bf16[384,256]{1,0:T(8,128)(2,1)}, bf16[384,256]{1,0:T(8,128)(2,1)S(1)}, u32[]{:S(2)}, u32[]{:S(2)}) collective-permute-start(bf16[384,256]{1,0:T(8,128)(2,1)} %ratings_ref.1), channel_id=1, source_target_pairs={{0,1},{1,2},{2,3},{3,4},{4,5},{5,6},{6,7},{7,8},{8,9},{9,10},{10,1... | collective-permute-start | bytes 589832 | tf_op jit(solution)/shard_map/ppermute | solution.py:131
  4.3 17.3 %collective-permute-start = (bf16[384,256]{1,0:T(8,128)(2,1)}, bf16[384,256]{1,0:T(8,128)(2,1)S(1)}, u32[]{:S(2)}, u32[]{:S(2)}) collective-permute-start(bf16[384,256]{1,0:T(8,128)(2,1)} %ratings_ref.1), channel_id=1, source_target_pairs={{0,11},{1,0},{2,1},{3,2},{4,3},{5,4},{6,5},{7,6},{8,7},{9,8},{10,9... | collective-permute-start | bytes 589832 | tf_op jit(solution)/shard_map/ppermute | solution.py:131
  19.7 9.2 %collective-permute-start.6 = (bf16[384,256]{1,0:T(8,128)(2,1)S(1)}, bf16[384,256]{1,0:T(8,128)(2,1)S(1)}, u32[]{:S(2)}, u32[]{:S(2)}) collective-permute-start(bf16[384,256]{1,0:T(8,128)(2,1)S(1)} %collective-permute-done.5.refs_10_), channel_id=1, source_target_pairs={{0,1},{1,2},{2,3},{3,4},{4,5},{5,6},{6,7},{7,8},{8,9},{9,10},{10,1... | collective-permute-start | bytes 589832 | tf_op jit(solution)/shard_map/ppermute | solution.py:131
  21.6 9.2 %collective-permute-start.1 = (bf16[384,256]{1,0:T(8,128)(2,1)S(1)}, bf16[384,256]{1,0:T(8,128)(2,1)S(1)}, u32[]{:S(2)}, u32[]{:S(2)}) collective-permute-start(bf16[384,256]{1,0:T(8,128)(2,1)S(1)} %collective-permute-done.refs_0_), channel_id=1, source_target_pairs={{0,11},{1,0},{2,1},{3,2},{4,3},{5,4},{6,5},{7,6},{8,7},{9,8},{10,9... | collective-permute-start | bytes 589832 | tf_op jit(solution)/shard_map/ppermute | solution.py:131
  28.9 8.8 %collective-permute-start.7 = (bf16[384,256]{1,0:T(8,128)(2,1)S(1)}, bf16[384,256]{1,0:T(8,128)(2,1)S(1)}, u32[]{:S(2)}, u32[]{:S(2)}) collective-permute-start(bf16[384,256]{1,0:T(8,128)(2,1)S(1)} %collective-permute-done.6.refs_9_), channel_id=1, source_target_pairs={{0,1},{1,2},{2,3},{3,4},{4,5},{5,6},{6,7},{7,8},{8,9},{9,10},{10,1... | collective-permute-start | bytes 589832 | tf_op jit(solution)/shard_map/ppermute | solution.py:131
  30.8 8.8 %collective-permute-start.2 = (bf16[384,256]{1,0:T(8,128)(2,1)S(1)}, bf16[384,256]{1,0:T(8,128)(2,1)S(1)}, u32[]{:S(2)}, u32[]{:S(2)}) collective-permute-start(bf16[384,256]{1,0:T(8,128)(2,1)S(1)} %collective-permute-done.1.refs_1_), channel_id=1, source_target_pairs={{0,11},{1,0},{2,1},{3,2},{4,3},{5,4},{6,5},{7,6},{8,7},{9,8},{10,9... | collective-permute-start | bytes 589832 | tf_op jit(solution)/shard_map/ppermute | solution.py:131
  37.6 8.8 %collective-permute-start.8 = (bf16[384,256]{1,0:T(8,128)(2,1)S(1)}, bf16[384,256]{1,0:T(8,128)(2,1)S(1)}, u32[]{:S(2)}, u32[]{:S(2)}) collective-permute-start(bf16[384,256]{1,0:T(8,128)(2,1)S(1)} %collective-permute-done.7.refs_8_), channel_id=1, source_target_pairs={{0,1},{1,2},{2,3},{3,4},{4,5},{5,6},{6,7},{7,8},{8,9},{9,10},{10,1... | collective-permute-start | bytes 589832 | tf_op jit(solution)/shard_map/ppermute | solution.py:131
  39.6 8.8 %collective-permute-start.3 = (bf16[384,256]{1,0:T(8,128)(2,1)S(1)}, bf16[384,256]{1,0:T(8,128)(2,1)S(1)}, u32[]{:S(2)}, u32[]{:S(2)}) collective-permute-start(bf16[384,256]{1,0:T(8,128)(2,1)S(1)} %collective-permute-done.2.refs_2_), channel_id=1, source_target_pairs={{0,11},{1,0},{2,1},{3,2},{4,3},{5,4},{6,5},{7,6},{8,7},{9,8},{10,9... | collective-permute-start | bytes 589832 | tf_op jit(solution)/shard_map/ppermute | solution.py:131
  46.4 8.8 %collective-permute-start.9 = (bf16[384,256]{1,0:T(8,128)(2,1)S(1)}, bf16[384,256]{1,0:T(8,128)(2,1)S(1)}, u32[]{:S(2)}, u32[]{:S(2)}) collective-permute-start(bf16[384,256]{1,0:T(8,128)(2,1)S(1)} %collective-permute-done.8.refs_7_), channel_id=1, source_target_pairs={{0,1},{1,2},{2,3},{3,4},{4,5},{5,6},{6,7},{7,8},{8,9},{9,10},{10,1... | collective-permute-start | bytes 589832 | tf_op jit(solution)/shard_map/ppermute | solution.py:131
  48.3 9.5 %collective-permute-start.4 = (bf16[384,256]{1,0:T(8,128)(2,1)S(1)}, bf16[384,256]{1,0:T(8,128)(2,1)S(1)}, u32[]{:S(2)}, u32[]{:S(2)}) collective-permute-start(bf16[384,256]{1,0:T(8,128)(2,1)S(1)} %collective-permute-done.3.refs_3_), channel_id=1, source_target_pairs={{0,11},{1,0},{2,1},{3,2},{4,3},{5,4},{6,5},{7,6},{8,7},{9,8},{10,9... | collective-permute-start | bytes 589832 | tf_op jit(solution)/shard_map/ppermute | solution.py:131
  55.2 8.8 %collective-permute-start.10 = (bf16[384,256]{1,0:T(8,128)(2,1)S(1)}, bf16[384,256]{1,0:T(8,128)(2,1)S(1)}, u32[]{:S(2)}, u32[]{:S(2)}) collective-permute-start(bf16[384,256]{1,0:T(8,128)(2,1)S(1)} %collective-permute-done.9.refs_6_), channel_id=1, source_target_pairs={{0,1},{1,2},{2,3},{3,4},{4,5},{5,6},{6,7},{7,8},{8,9},{9,10},{10,1... | collective-permute-start | bytes 589832 | tf_op jit(solution)/shard_map/ppermute | solution.py:131
  63.9 0.9 copy-start
  68.8 4.4 %collective-permute-start.11 = (bf16[32,56,256]{2,1,0:T(8,128)(2,1)S(1)}, bf16[32,56,256]{2,1,0:T(8,128)(2,1)S(1)}, u32[]{:S(2)}, u32[]{:S(2)}) collective-permute-start(bf16[32,56,256]{2,1,0:T(8,128)(2,1)S(1)} %get-tuple-element.12), channel_id=1, source_target_pairs={{0,12},{12,0},{1,13},{13,1},{2,14},{14,2},{3,15},{15,3},{4,16},{16... | collective-permute-start | bytes 2752520 | tf_op jit(solution)/shard_map/ppermute | solution.py:159
  73.9 10.5 %collective-permute-start.12 = (bf16[8,56,256]{2,1,0:T(8,128)(2,1)S(1)}, bf16[8,56,256]{2,1,0:T(8,128)(2,1)S(1)}, u32[]{:S(2)}, u32[]{:S(2)}) collective-permute-start(bf16[8,56,256]{2,1,0:T(8,128)(2,1)S(1)} %get-tuple-element.14), channel_id=1, source_target_pairs={{0,192},{192,384},{384,576},{576,0},{1,193},{193,385},{385,577},{5... | collective-permute-start | bytes 688136 | tf_op jit(solution)/shard_map/ppermute | solution.py:131
  77.3 11.9 %collective-permute-start.13 = (bf16[8,56,256]{2,1,0:T(8,128)(2,1)S(1)}, bf16[8,56,256]{2,1,0:T(8,128)(2,1)S(1)}, u32[]{:S(2)}, u32[]{:S(2)}) collective-permute-start(bf16[8,56,256]{2,1,0:T(8,128)(2,1)S(1)} %get-tuple-element.15), channel_id=1, source_target_pairs={{0,384},{192,576},{384,0},{576,192},{1,385},{193,577},{385,1},{577... | collective-permute-start | bytes 688136 | tf_op jit(solution)/shard_map/ppermute | solution.py:131
  80.4 12.6 %collective-permute-start.14 = (bf16[8,56,256]{2,1,0:T(8,128)(2,1)S(1)}, bf16[8,56,256]{2,1,0:T(8,128)(2,1)S(1)}, u32[]{:S(2)}, u32[]{:S(2)}) collective-permute-start(bf16[8,56,256]{2,1,0:T(8,128)(2,1)S(1)} %get-tuple-element.16), channel_id=1, source_target_pairs={{0,576},{192,0},{384,192},{576,384},{1,577},{193,1},{385,193},{577... | collective-permute-start | bytes 688136 | tf_op jit(solution)/shard_map/ppermute | solution.py:131

commit v3 on v1

v3 whole, which is shorter than its diff:
```python
import jax
import jax.numpy as jnp
from jax import lax
from jax.experimental import pallas as pl
from jax.experimental.pallas import tpu as pltpu
from jax.sharding import Mesh, PartitionSpec as P

X, Y, CORES, PANELS = 4, 8, 2, 12
SLOTS = X * Y
BLOCK = 64
ITEMS = 3072
SHARE = 48
SLOT_ROWS = SHARE + 8
HOPS = 4
CORE, RESIDUE, SLAB, COUNTS = 0, 1, 2, 3
UNITS = {
    (0, 0): (3, (4, 3)),
    (0, 1): (1, (2, 0)),
    (0, 2): (2, (3, 2)),
    (1, 0): (0, (-4, -3)),
    (1, 1): (1, (-1, 1)),
    (1, 2): (-1, (-1, 0)),
}


def split_rows(total):
    high = total.astype(jnp.bfloat16).astype(jnp.float32)
    first = lax.broadcasted_iota(jnp.int32, total.shape, 0) < 4
    return jnp.where(first, high, total - high)


def pair_kernel(place_ref, own_ref, other_ref, out_ref):
    core, rows = place_ref[CORE], own_ref.shape[0]
    out_ref[pl.ds(pl.multiple_of(core * rows, 64), rows), :] = own_ref[...]
    out_ref[pl.ds(pl.multiple_of((1 - core) * rows, 64), rows), :] = other_ref[...]


def partial_kernel(place_ref, near_ref, far_ref, *refs):
    panels, (out_ref, gram_ref, degree_ref) = refs[: 2 * HOPS], refs[2 * HOPS :]
    core, residue = place_ref[CORE], place_ref[RESIDUE]
    rows, width = panels[0].shape
    squares = jnp.zeros((rows, width), jnp.float32)
    for k in (3, 4, 6, 7):
        values = panels[k][...].astype(jnp.float32)
        squares = squares + values * values
    square_sum = jnp.sum(squares, axis=1, keepdims=True)
    chunk = near_ref.shape[1]
    corner = lax.broadcasted_iota(jnp.int32, (chunk, chunk), 0) == lax.broadcasted_iota(
        jnp.int32, (chunk, chunk), 1
    )
    upright = [
        jnp.sum(
            jnp.where(corner, near_ref[pl.ds(i, 1), :] + far_ref[pl.ds(i, 1), :], 0.0),
            axis=1,
            keepdims=True,
        )
        for i in range(rows // chunk)
    ]
    square_sum = square_sum + jnp.concatenate(upright, axis=0)
    position = lax.broadcasted_iota(jnp.int32, (BLOCK, 1), 0)
    blocks = rows // BLOCK // CORES
    live = []
    for i in range(CORES * blocks):
        own = core == i // blocks
        count = jnp.where(
            own, place_ref[COUNTS + i % blocks], place_ref[COUNTS + blocks + i % blocks]
        )
        live.append((position < count).astype(jnp.float32))
    scale = jnp.concatenate(live, axis=0) / jnp.sqrt(square_sum / ITEMS + 1e-05)

    for (its_core, its_residue), (at, columns) in UNITS.items():

        @pl.when((core == its_core) & (residue == its_residue))
        def _():
            def panel(offset):
                hop = -offset if its_core else offset
                return panels[hop if hop >= 0 else HOPS - hop]

            def degree(ref):
                values = ref[...].astype(jnp.float32)
                weighted = (scale * values).astype(jnp.bfloat16)
                total = jnp.sum(values * weighted.astype(jnp.float32), axis=0, keepdims=True)
                return weighted, total

            row_panels = [panel(i - at) for i in range(3)]
            for i, ref in enumerate(row_panels):
                total = degree(ref)[1]
                for unit in range(2):
                    degree_ref[pl.ds(4 * unit + 1 + i, 1), :] = total
            for unit, offset in enumerate(columns):
                weighted, total = degree(panel(offset))
                degree_ref[pl.ds(4 * unit, 1), :] = total
                for i, ref in enumerate(row_panels):
                    gram_ref[pl.ds((3 * unit + i) * width, width), :] = lax.dot_general(
                        ref[...],
                        weighted,
                        (((0,), (0,)), ((), ())),
                        preferred_element_type=jnp.float32,
                    )

    blank = jnp.zeros((1, width), jnp.float32)
    for x in range(X):
        for y in range(Y):
            unit, start = x // 2, (2 * y + x % 2) * SHARE
            low, high = start // width, (start + SHARE - 1) // width
            four = [degree_ref[pl.ds(4 * unit + i, 1), :] for i in (0, 1 + low, 1 + high)]
            four.append(blank)
            extra = split_rows(jnp.concatenate(four + four, axis=0))
            block = gram_ref[pl.ds(unit * 3 * width + start, SHARE), :]
            out_ref[x * Y + y] = jnp.concatenate([block, extra], axis=0).astype(jnp.bfloat16)


def finish_kernel(place_ref, got_ref, out_ref):
    start = place_ref[SLAB] * SHARE
    offset = start - lax.shift_left(lax.shift_right_logical(start, 8), 8)
    total = got_ref[0].astype(jnp.float32)
    for slot in range(1, SLOTS):
        total = total + got_ref[slot].astype(jnp.float32)
    extra = total[SHARE:]
    extra = extra + pltpu.roll(extra, 4, 0)
    width = total.shape[1]
    lane = lax.broadcasted_iota(jnp.int32, (SHARE, width), 1)
    row = lax.broadcasted_iota(jnp.int32, (SHARE, width), 0) + offset
    row_degree = jnp.sum(
        jnp.where(lane == row, extra[1:2], 0.0) + jnp.where(lane + width == row, extra[2:3], 0.0),
        axis=1,
        keepdims=True,
    )
    row_inverse = 1.0 / jnp.sqrt(row_degree)
    column_inverse = 1.0 / jnp.sqrt(extra[0:1])
    out_ref[...] = (total[:SHARE] * row_inverse * column_inverse).astype(jnp.bfloat16)


VMEM = pl.BlockSpec(memory_space=pltpu.VMEM)
SMEM = pl.BlockSpec(memory_space=pltpu.SMEM)
PARAMS = pltpu.CompilerParams(vmem_limit_bytes=48 * 1024 * 1024)


def homes():
    pairs = []
    for x in range(X):
        for y in range(Y):
            for core in range(CORES):
                for z in range(PANELS):
                    at, columns = UNITS[core, z % 3]
                    triple = (z - at) % PANELS // 3
                    user = 16 * triple + 2 * y + x % 2
                    column = (z + columns[x // 2]) % PANELS
                    source = ((x * Y + y) * CORES + core) * PANELS + z
                    pairs.append((source, user * PANELS + column))
    return pairs


def square_sum(panels):
    values = [panel.astype(jnp.float32) for panel in panels]
    return jnp.sum(sum(v * v for v in values), axis=1)


def per_device(ratings, counts):
    rows, width = CORES * ratings.shape[0], ratings.shape[1]
    x, y, core, me = (lax.axis_index(name) for name in ("x", "y", "core", "z"))
    place = jnp.stack([core, me % 3, 2 * y + x % 2]).astype(jnp.int32)

    def swap(array):
        return lax.ppermute(array, "core", [(0, 1), (1, 0)])

    def hop(array):
        return lax.ppermute(
            array,
            ("core", "z"),
            [
                (c * PANELS + z, c * PANELS + (z + (1 if c else -1)) % PANELS)
                for c in range(CORES)
                for z in range(PANELS)
            ],
        )

    both = jax.ShapeDtypeStruct((rows, width), ratings.dtype)
    own = pl.pallas_call(
        pair_kernel,
        out_shape=both,
        in_specs=[SMEM, VMEM, VMEM],
        out_specs=VMEM,
        compiler_params=PARAMS,
        name="pair",
    )(place, ratings, swap(ratings))
    ahead, behind = [own], []
    for step in range(HOPS):
        ahead.append(hop(ahead[-1]))
        if step == 0:
            later, ahead[1] = lax.optimization_barrier((counts, ahead[1]))
            other_counts = swap(later)
        if step < HOPS - 1:
            behind.append(swap(ahead[-1]))
    near = square_sum([ahead[0], ahead[1], ahead[2], behind[0]]).reshape(-1, 128)
    far = lax.ppermute(near, "z", [(z, (z + 6) % PANELS) for z in range(PANELS)])
    everything = jnp.concatenate([place, counts, other_counts])
    slots = jax.ShapeDtypeStruct((SLOTS, SLOT_ROWS, width), jnp.bfloat16)
    partial = pl.pallas_call(
        partial_kernel,
        out_shape=slots,
        in_specs=[SMEM] + [VMEM] * (2 + 2 * HOPS),
        out_specs=VMEM,
        scratch_shapes=[
            pltpu.VMEM((6 * width, width), jnp.float32),
            pltpu.VMEM((8, width), jnp.float32),
        ],
        compiler_params=PARAMS,
        name="partial",
    )(everything, near, far, *ahead, *behind)
    got = lax.all_to_all(partial, ("x", "y"), 0, 0, tiled=True)
    block = pl.pallas_call(
        finish_kernel,
        out_shape=jax.ShapeDtypeStruct((SHARE, width), jnp.bfloat16),
        in_specs=[SMEM, VMEM],
        out_specs=VMEM,
        compiler_params=PARAMS,
        name="finish",
    )(place, got)
    return lax.ppermute(block, ("x", "y", "core", "z"), homes())


def solution(mesh):
    fine = Mesh(mesh.devices.reshape(X, Y, CORES, PANELS), ("x", "y", "core", "z"))
    users = ("x", "y", "core")
    return jax.shard_map(
        per_device,
        mesh=fine,
        in_specs=(P(users, "z"), P(users)),
        out_specs=P(users, "z"),
        check_vma=False,
    )
```

time: 112 us -> 111 us (level)
  the two profiles are of different devices: /device:TPU:8 before, /device:TPU:14 now
where the time goes in v3:
time: 111 us
  starting transfers between devices  47.8 us (43%)
  blocking collectives  30.2 us (27%)
  waiting for transfers between devices  26.3 us (24%)
  Pallas kernels  3.98 us (4%)
  local copies, waits for them, and re-layouts  1.62 us (1%)
    ppermute x4, starting transfers between devices, hop(): lax.ppermute(array, ('core', 'z'), [(c * PANELS + z, c * PANELS + (z + (1...  31.4 us
    all_to_all x1, blocking collectives, per_device(): got = lax.all_to_all(partial, ('x', 'y'), 0, 0, tiled=True)  30.2 us
    ppermute x5, starting transfers between devices, swap(): return lax.ppermute(array, 'core', [(0, 1), (1, 0)])  12.6 us
    ppermute x4, waiting for transfers between devices, hop(): lax.ppermute(array, ('core', 'z'), [(c * PANELS + z, c * PANELS + (z + (1...  11.5 us
    ppermute x1, waiting for transfers between devices, per_device(): return lax.ppermute(block, ('x', 'y', 'core', 'z'), homes())  8.01 us
    ppermute x1, waiting for transfers between devices, per_device(): lax.ppermute(near, 'z', [(z, (z + 6) % PANELS) for z in range(PANELS)])  4.53 us
    pallas_call x1, Pallas kernels, per_device(): pl.pallas_call(partial_kernel, out_shape=slots, in_specs=[SMEM] + [VMEM]...  2.72 us
    ppermute x5, waiting for transfers between devices, swap(): return lax.ppermute(array, 'core', [(0, 1), (1, 0)])  2.31 us
  transfers between devices with their start and end apart: 11, of which 7 were waited for; matrix products, arithmetic and copies ran while one was open for 0% of the time, Pallas kernels for 0%

profile of v3, /device:TPU:14, one launch (start us, length us, event | category | flops | bytes accessed | tf_op | source)
XLA Modules:
  0.0 110.6 jit_solution(7658463031092107350)
XLA Ops:
  0.0 1.9 %collective-permute-start = (bf16[384,256]{1,0:T(8,128)(2,1)}, bf16[384,256]{1,0:T(8,128)(2,1)S(1)}, u32[]{:S(2)}, u32[]{:S(2)}) collective-permute-start(bf16[384,256]{1,0:T(8,128)(2,1)} %own_ref.1), channel_id=1, source_target_pairs={{0,12},{12,0},{1,13},{13,1},{2,14},{14,2},{3,15},{15,3},{4,16},{16... | collective-permute-start | bytes 589832 | tf_op jit(solution)/shard_map/ppermute | solution.py:165
  2.0 0.1 pad_add_fusion.place_ref
  2.0 1.5 %collective-permute-done.other_ref = bf16[384,256]{1,0:T(8,128)(2,1)S(1)} collective-permute-done((bf16[384,256]{1,0:T(8,128)(2,1)}, bf16[384,256]{1,0:T(8,128)(2,1)S(1)}, u32[]{:S(2)}, u32[]{:S(2)}) %collective-permute-start) | collective-permute-done | bytes 196640 | tf_op jit(solution)/shard_map/ppermute | solution.py:165
  3.5 0.0 copy-start
  3.5 0.9 copy-done
  4.5 0.6 pair.1.refs_0_
  5.0 14.6 %collective-permute-start.1 = (bf16[768,256]{1,0:T(8,128)(2,1)S(1)}, bf16[768,256]{1,0:T(8,128)(2,1)S(1)}, u32[]{:S(2)}, u32[]{:S(2)}) collective-permute-start(bf16[768,256]{1,0:T(8,128)(2,1)S(1)} %pair.1.refs_0_), channel_id=1, source_target_pairs={{0,11},{1,0},{2,1},{3,2},{4,3},{5,4},{6,5},{7,6},{8,7},{9,8},{10,9... | collective-permute-start | bytes 1179656 | tf_op jit(solution)/shard_map/ppermute | solution.py:168
  19.6 5.3 %collective-permute-done.1.refs_1_ = bf16[768,256]{1,0:T(8,128)(2,1)S(1)} collective-permute-done((bf16[768,256]{1,0:T(8,128)(2,1)S(1)}, bf16[768,256]{1,0:T(8,128)(2,1)S(1)}, u32[]{:S(2)}, u32[]{:S(2)}) %collective-permute-start.1) | collective-permute-done | bytes 393248 | tf_op jit(solution)/shard_map/ppermute | solution.py:168
  24.9 5.6 %collective-permute-start.3 = (bf16[768,256]{1,0:T(8,128)(2,1)S(1)}, bf16[768,256]{1,0:T(8,128)(2,1)S(1)}, u32[]{:S(2)}, u32[]{:S(2)}) collective-permute-start(bf16[768,256]{1,0:T(8,128)(2,1)S(1)} %collective-permute-done.1.refs_1_), channel_id=1, source_target_pairs={{0,11},{1,0},{2,1},{3,2},{4,3},{5,4},{6,5},{7,6},{8,7},{9,8},{10,9... | collective-permute-start | bytes 1179656 | tf_op jit(solution)/shard_map/ppermute | solution.py:168
  30.5 5.3 %collective-permute-done.3.refs_2_ = bf16[768,256]{1,0:T(8,128)(2,1)S(1)} collective-permute-done((bf16[768,256]{1,0:T(8,128)(2,1)S(1)}, bf16[768,256]{1,0:T(8,128)(2,1)S(1)}, u32[]{:S(2)}, u32[]{:S(2)}) %collective-permute-start.3) | collective-permute-done | bytes 393248 | tf_op jit(solution)/shard_map/ppermute | solution.py:168
  35.8 5.6 %collective-permute-start.6 = (bf16[768,256]{1,0:T(8,128)(2,1)S(1)}, bf16[768,256]{1,0:T(8,128)(2,1)S(1)}, u32[]{:S(2)}, u32[]{:S(2)}) collective-permute-start(bf16[768,256]{1,0:T(8,128)(2,1)S(1)} %collective-permute-done.3.refs_2_), channel_id=1, source_target_pairs={{0,11},{1,0},{2,1},{3,2},{4,3},{5,4},{6,5},{7,6},{8,7},{9,8},{10,9... | collective-permute-start | bytes 1179656 | tf_op jit(solution)/shard_map/ppermute | solution.py:168
  41.4 1.9 %collective-permute-start.4 = (bf16[768,256]{1,0:T(8,128)(2,1)S(1)}, bf16[768,256]{1,0:T(8,128)(2,1)S(1)}, u32[]{:S(2)}, u32[]{:S(2)}) collective-permute-start(bf16[768,256]{1,0:T(8,128)(2,1)S(1)} %collective-permute-done.1.refs_1_), channel_id=1, source_target_pairs={{0,12},{12,0},{1,13},{13,1},{2,14},{14,2},{3,15},{15,3},{4,16},{16... | collective-permute-start | bytes 1179656 | tf_op jit(solution)/shard_map/ppermute | solution.py:165
  43.3 2.4 %collective-permute-start.8 = (bf16[768,256]{1,0:T(8,128)(2,1)S(1)}, bf16[768,256]{1,0:T(8,128)(2,1)S(1)}, u32[]{:S(2)}, u32[]{:S(2)}) collective-permute-start(bf16[768,256]{1,0:T(8,128)(2,1)S(1)} %collective-permute-done.3.refs_2_), channel_id=1, source_target_pairs={{0,12},{12,0},{1,13},{13,1},{2,14},{14,2},{3,15},{15,3},{4,16},{16... | collective-permute-start | bytes 1179656 | tf_op jit(solution)/shard_map/ppermute | solution.py:165
  45.7 0.9 collective-permute-done.6.refs_3_
  46.7 1.9 %collective-permute-start.9 = (bf16[768,256]{1,0:T(8,128)(2,1)S(1)}, bf16[768,256]{1,0:T(8,128)(2,1)S(1)}, u32[]{:S(2)}, u32[]{:S(2)}) collective-permute-start(bf16[768,256]{1,0:T(8,128)(2,1)S(1)} %collective-permute-done.6.refs_3_), channel_id=1, source_target_pairs={{0,12},{12,0},{1,13},{13,1},{2,14},{14,2},{3,15},{15,3},{4,16},{16... | collective-permute-start | bytes 1179656 | tf_op jit(solution)/shard_map/ppermute | solution.py:165
  48.6 5.6 %collective-permute-start.7 = (bf16[768,256]{1,0:T(8,128)(2,1)S(1)}, bf16[768,256]{1,0:T(8,128)(2,1)S(1)}, u32[]{:S(2)}, u32[]{:S(2)}) collective-permute-start(bf16[768,256]{1,0:T(8,128)(2,1)S(1)} %collective-permute-done.6.refs_3_), channel_id=1, source_target_pairs={{0,11},{1,0},{2,1},{3,2},{4,3},{5,4},{6,5},{7,6},{8,7},{9,8},{10,9... | collective-permute-start | bytes 1179656 | tf_op jit(solution)/shard_map/ppermute | solution.py:168
  54.2 0.0 collective-permute-done.4.refs_5_
  54.2 0.4 add_reduce_fusion
  54.6 0.0 copy-start.1
  54.6 1.9 %collective-permute-start.5 = (f32[6,128]{1,0:T(8,128)S(1)}, f32[6,128]{1,0:T(8,128)S(1)}, u32[]{:S(2)}, u32[]{:S(2)}) collective-permute-start(f32[6,128]{1,0:T(8,128)S(1)} %bitcast.4), channel_id=1, source_target_pairs={{0,6},{1,7},{2,8},{3,9},{4,10},{5,11},{6,0},{7,1},{8,2},{9,3},{10,... | collective-permute-start | bytes 9224 | tf_op jit(solution)/shard_map/ppermute | solution.py:196
  56.5 0.0 copy-done.1
  56.5 4.5 %collective-permute-start.2 = (s32[6]{0:T(128)S(1)}, s32[6]{0:T(128)S(1)}, u32[]{:S(2)}, u32[]{:S(2)}) collective-permute-start(s32[6]{0:T(128)S(1)} %copy-done.1), channel_id=1, source_target_pairs={{0,12},{12,0},{1,13},{13,1},{2,14},{14,2},{3,15},{15,3},{4,16},{16... | collective-permute-start | bytes 80 | tf_op jit(solution)/shard_map/ppermute | solution.py:165
  61.0 0.8 collective-permute-done.2
  61.8 0.1 concatenate.4.place_ref
  61.9 4.5 %collective-permute-done.5.far_ref = f32[6,128]{1,0:T(8,128)S(1)} collective-permute-done((f32[6,128]{1,0:T(8,128)S(1)}, f32[6,128]{1,0:T(8,128)S(1)}, u32[]{:S(2)}, u32[]{:S(2)}) %collective-permute-start.5) | collective-permute-done | bytes 3104 | tf_op jit(solution)/shard_map/ppermute | solution.py:196
  66.4 0.0 collective-permute-done.8.refs_6_
  66.4 0.0 collective-permute-done.9.refs_7_
  66.4 0.0 collective-permute-done.7.refs_4_
  66.4 2.7 %partial.1 = bf16[32,56,256]{2,1,0:T(8,128)(2,1)S(1)} custom-call(s32[15]{0:T(128)S(1)} %concatenate.4.place_ref, f32[6,128]{1,0:T(8,128)S(1)} %bitcast.5, f32[6,128]{1,0:T(8,128)S(1)} %collective-permute-done.5.far_ref, bf16[768,256]{1,0:T(8,128)(2,1)S(1)} %pair.1.refs_0_, bf16[768,256]{1,0:T(8,128)(2,1)S(1)} %collective-permute-done.1.refs_1_, ...), custom_call_target="tpu_custom_call" | custom-call | tf_op jit(solution)/shard_map/partial/pallas_call | solution.py:199
  69.1 30.2 %all_to_all.5.got_ref = bf16[32,56,256]{2,1,0:T(8,128)(2,1)S(1)} all-to-all(bf16[32,56,256]{2,1,0:T(8,128)(2,1)S(1)} %partial.1), channel_id=1, replica_groups=mesh['x'=4,'y'=8,'core'=2,'z'=12] {'x','y'}, dimensions={0} | all-to-all | bytes 1835008 | tf_op jit(solution)/shard_map/all_to_all | solution.py:211
  99.3 0.7 finish.1
  100.0 1.9 %collective-permute-start.10 = (bf16[48,256]{1,0:T(8,128)(2,1)S(1)}, bf16[48,256]{1,0:T(8,128)(2,1)S(1)}, u32[]{:S(2)}, u32[]{:S(2)}) collective-permute-start(bf16[48,256]{1,0:T(8,128)(2,1)S(1)} %finish.1), channel_id=1, source_target_pairs={{0,580},{1,3},{2,5},{3,7},{4,198},{5,200},{6,202},{7,393},{8,395},... | collective-permute-start | bytes 73736 | tf_op jit(solution)/shard_map/ppermute | solution.py:220
  102.0 8.0 %collective-permute-done.10 = bf16[48,256]{1,0:T(8,128)(2,1)S(1)} collective-permute-done((bf16[48,256]{1,0:T(8,128)(2,1)S(1)}, bf16[48,256]{1,0:T(8,128)(2,1)S(1)}, u32[]{:S(2)}, u32[]{:S(2)}) %collective-permute-start.10) | collective-permute-done | bytes 24608 | tf_op jit(solution)/shard_map/ppermute | solution.py:220
  110.0 0.6 copy.4
Async XLA Ops:
  0.0 3.5 %collective-permute-start = (bf16[384,256]{1,0:T(8,128)(2,1)}, bf16[384,256]{1,0:T(8,128)(2,1)S(1)}, u32[]{:S(2)}, u32[]{:S(2)}) collective-permute-start(bf16[384,256]{1,0:T(8,128)(2,1)} %own_ref.1), channel_id=1, source_target_pairs={{0,12},{12,0},{1,13},{13,1},{2,14},{14,2},{3,15},{15,3},{4,16},{16... | collective-permute-start | bytes 589832 | tf_op jit(solution)/shard_map/ppermute | solution.py:165
  3.5 0.9 copy-start
  5.0 19.9 %collective-permute-start.1 = (bf16[768,256]{1,0:T(8,128)(2,1)S(1)}, bf16[768,256]{1,0:T(8,128)(2,1)S(1)}, u32[]{:S(2)}, u32[]{:S(2)}) collective-permute-start(bf16[768,256]{1,0:T(8,128)(2,1)S(1)} %pair.1.refs_0_), channel_id=1, source_target_pairs={{0,11},{1,0},{2,1},{3,2},{4,3},{5,4},{6,5},{7,6},{8,7},{9,8},{10,9... | collective-permute-start | bytes 1179656 | tf_op jit(solution)/shard_map/ppermute | solution.py:168
  24.9 10.9 %collective-permute-start.3 = (bf16[768,256]{1,0:T(8,128)(2,1)S(1)}, bf16[768,256]{1,0:T(8,128)(2,1)S(1)}, u32[]{:S(2)}, u32[]{:S(2)}) collective-permute-start(bf16[768,256]{1,0:T(8,128)(2,1)S(1)} %collective-permute-done.1.refs_1_), channel_id=1, source_target_pairs={{0,11},{1,0},{2,1},{3,2},{4,3},{5,4},{6,5},{7,6},{8,7},{9,8},{10,9... | collective-permute-start | bytes 1179656 | tf_op jit(solution)/shard_map/ppermute | solution.py:168
  35.8 10.9 %collective-permute-start.6 = (bf16[768,256]{1,0:T(8,128)(2,1)S(1)}, bf16[768,256]{1,0:T(8,128)(2,1)S(1)}, u32[]{:S(2)}, u32[]{:S(2)}) collective-permute-start(bf16[768,256]{1,0:T(8,128)(2,1)S(1)} %collective-permute-done.3.refs_2_), channel_id=1, source_target_pairs={{0,11},{1,0},{2,1},{3,2},{4,3},{5,4},{6,5},{7,6},{8,7},{9,8},{10,9... | collective-permute-start | bytes 1179656 | tf_op jit(solution)/shard_map/ppermute | solution.py:168
  41.4 12.8 %collective-permute-start.4 = (bf16[768,256]{1,0:T(8,128)(2,1)S(1)}, bf16[768,256]{1,0:T(8,128)(2,1)S(1)}, u32[]{:S(2)}, u32[]{:S(2)}) collective-permute-start(bf16[768,256]{1,0:T(8,128)(2,1)S(1)} %collective-permute-done.1.refs_1_), channel_id=1, source_target_pairs={{0,12},{12,0},{1,13},{13,1},{2,14},{14,2},{3,15},{15,3},{4,16},{16... | collective-permute-start | bytes 1179656 | tf_op jit(solution)/shard_map/ppermute | solution.py:165
  43.3 23.1 %collective-permute-start.8 = (bf16[768,256]{1,0:T(8,128)(2,1)S(1)}, bf16[768,256]{1,0:T(8,128)(2,1)S(1)}, u32[]{:S(2)}, u32[]{:S(2)}) collective-permute-start(bf16[768,256]{1,0:T(8,128)(2,1)S(1)} %collective-permute-done.3.refs_2_), channel_id=1, source_target_pairs={{0,12},{12,0},{1,13},{13,1},{2,14},{14,2},{3,15},{15,3},{4,16},{16... | collective-permute-start | bytes 1179656 | tf_op jit(solution)/shard_map/ppermute | solution.py:165
  46.7 19.7 %collective-permute-start.9 = (bf16[768,256]{1,0:T(8,128)(2,1)S(1)}, bf16[768,256]{1,0:T(8,128)(2,1)S(1)}, u32[]{:S(2)}, u32[]{:S(2)}) collective-permute-start(bf16[768,256]{1,0:T(8,128)(2,1)S(1)} %collective-permute-done.6.refs_3_), channel_id=1, source_target_pairs={{0,12},{12,0},{1,13},{13,1},{2,14},{14,2},{3,15},{15,3},{4,16},{16... | collective-permute-start | bytes 1179656 | tf_op jit(solution)/shard_map/ppermute | solution.py:165
  48.6 17.8 %collective-permute-start.7 = (bf16[768,256]{1,0:T(8,128)(2,1)S(1)}, bf16[768,256]{1,0:T(8,128)(2,1)S(1)}, u32[]{:S(2)}, u32[]{:S(2)}) collective-permute-start(bf16[768,256]{1,0:T(8,128)(2,1)S(1)} %collective-permute-done.6.refs_3_), channel_id=1, source_target_pairs={{0,11},{1,0},{2,1},{3,2},{4,3},{5,4},{6,5},{7,6},{8,7},{9,8},{10,9... | collective-permute-start | bytes 1179656 | tf_op jit(solution)/shard_map/ppermute | solution.py:168
  54.6 1.9 %copy-start.1 = (s32[6]{0:T(128)S(1)}, s32[6]{0:T(128)}, u32[]{:S(2)}) copy-start(s32[6]{0:T(128)} %param.3) | copy-start | bytes 76
  54.6 11.8 %collective-permute-start.5 = (f32[6,128]{1,0:T(8,128)S(1)}, f32[6,128]{1,0:T(8,128)S(1)}, u32[]{:S(2)}, u32[]{:S(2)}) collective-permute-start(f32[6,128]{1,0:T(8,128)S(1)} %bitcast.4), channel_id=1, source_target_pairs={{0,6},{1,7},{2,8},{3,9},{4,10},{5,11},{6,0},{7,1},{8,2},{9,3},{10,... | collective-permute-start | bytes 9224 | tf_op jit(solution)/shard_map/ppermute | solution.py:196
  56.5 5.3 %collective-permute-start.2 = (s32[6]{0:T(128)S(1)}, s32[6]{0:T(128)S(1)}, u32[]{:S(2)}, u32[]{:S(2)}) collective-permute-start(s32[6]{0:T(128)S(1)} %copy-done.1), channel_id=1, source_target_pairs={{0,12},{12,0},{1,13},{13,1},{2,14},{14,2},{3,15},{15,3},{4,16},{16... | collective-permute-start | bytes 80 | tf_op jit(solution)/shard_map/ppermute | solution.py:165
  100.0 9.9 %collective-permute-start.10 = (bf16[48,256]{1,0:T(8,128)(2,1)S(1)}, bf16[48,256]{1,0:T(8,128)(2,1)S(1)}, u32[]{:S(2)}, u32[]{:S(2)}) collective-permute-start(bf16[48,256]{1,0:T(8,128)(2,1)S(1)} %finish.1), channel_id=1, source_target_pairs={{0,580},{1,3},{2,5},{3,7},{4,198},{5,200},{6,202},{7,393},{8,395},... | collective-permute-start | bytes 73736 | tf_op jit(solution)/shard_map/ppermute | solution.py:220

commit v4 on v1

v4 whole, which is shorter than its diff:
```python
import jax
import jax.numpy as jnp
from jax import lax
from jax.experimental import pallas as pl
from jax.experimental.pallas import tpu as pltpu
from jax.sharding import Mesh, PartitionSpec as P

X, Y, CORES, PANELS = 4, 8, 2, 12
SLOTS = X * Y
BLOCK = 64
ITEMS = 3072
SHARE = 48
LANES = 128
SLOT_ROWS = 2 * SHARE + 8
CORE, RESIDUE, SLAB, COUNTS = 0, 1, 2, 3
COLUMNS = ((9, 10, 11), (7, 8, 6), (5, 3, 4))


def split_rows(total):
    high = total.astype(jnp.bfloat16).astype(jnp.float32)
    first = lax.broadcasted_iota(jnp.int32, total.shape, 0) < 4
    return jnp.where(first, high, total - high)


def join_rows(extra):
    return extra + pltpu.roll(extra, 4, 0)


def partial_kernel(place_ref, sums_ref, *refs):
    panels, (keep_ref, send_ref, gram_ref, row_ref, column_ref) = refs[:6], refs[6:]
    core, residue = place_ref[CORE], place_ref[RESIDUE]
    rows, width = panels[0].shape
    sums = sums_ref[0]
    for i in range(1, PANELS):
        sums = sums + sums_ref[i]
    corner = lax.broadcasted_iota(jnp.int32, (LANES, LANES), 0) == lax.broadcasted_iota(
        jnp.int32, (LANES, LANES), 1
    )
    square_sum = jnp.concatenate(
        [
            jnp.sum(jnp.where(corner, sums[i : i + 1], 0.0), axis=1, keepdims=True)
            for i in range(rows // LANES)
        ],
        axis=0,
    )
    position = lax.broadcasted_iota(jnp.int32, (BLOCK, 1), 0)
    live = jnp.concatenate(
        [
            (position < place_ref[COUNTS + i]).astype(jnp.float32)
            for i in range(rows // BLOCK)
        ],
        axis=0,
    )
    scale = live / jnp.sqrt(square_sum / ITEMS + 1e-05)

    weighted = []
    degrees = []
    for panel in panels:
        values = panel[...].astype(jnp.float32)
        one = (scale * values).astype(jnp.bfloat16)
        weighted.append(one)
        degrees.append(
            jnp.sum(values * one.astype(jnp.float32), axis=0, keepdims=True)
        )
    places = (residue, lax.rem(residue + 2, 3), lax.rem(residue + 1, 3))
    for panel, at, degree in zip(panels[:3], places, degrees[:3]):
        for half in range(2):
            row_ref[pl.ds(2 * at + half, 1), :] = degree[:, half * LANES : (half + 1) * LANES]
    for unit, column in enumerate((0, 3, 4, 5)):
        for half in range(2):
            column_ref[pl.ds(2 * unit + half, 1), :] = degrees[column][
                :, half * LANES : (half + 1) * LANES
            ]
        for panel, at in zip(panels[:3], places):
            start = pl.multiple_of((3 * unit + at) * width, width)
            gram_ref[pl.ds(start, width), :] = lax.dot_general(
                panel[...],
                weighted[column],
                (((0,), (0,)), ((), ())),
                preferred_element_type=jnp.float32,
            )
    for x in range(X):
        for y in range(Y):
            start = (2 * y + x % 2) * SHARE
            low, high = start // LANES, (start + SHARE - 1) // LANES
            for mine in (True, False):
                unit = 2 * (core if mine else 1 - core) + x // 2
                four = [column_ref[pl.ds(2 * unit + half, 1), :] for half in range(2)]
                four += [row_ref[pl.ds(i, 1), :] for i in (low, high)]
                extra = split_rows(jnp.concatenate(four + four, axis=0))
                first = pl.multiple_of(unit * 3 * width + start, 16)
                block = gram_ref[pl.ds(first, SHARE), :]
                whole = jnp.concatenate([block[:, :LANES], block[:, LANES:], extra], axis=0)
                ref = keep_ref if mine else send_ref
                ref[x * Y + y] = whole.astype(ref.dtype)


def add_kernel(keep_ref, got_ref, out_ref):
    for slot in range(SLOTS):
        total = keep_ref[slot] + got_ref[slot].astype(jnp.float32)
        extra = split_rows(join_rows(total[2 * SHARE :]))
        out_ref[slot] = jnp.concatenate([total[: 2 * SHARE], extra], axis=0).astype(
            jnp.bfloat16
        )


def finish_kernel(place_ref, got_ref, out_ref):
    offset = lax.rem(place_ref[SLAB] * SHARE, LANES)
    total = got_ref[0].astype(jnp.float32)
    for slot in range(1, SLOTS):
        total = total + got_ref[slot].astype(jnp.float32)
    extra = join_rows(total[2 * SHARE :])
    lane = lax.broadcasted_iota(jnp.int32, (SHARE, LANES), 1)
    row = lax.broadcasted_iota(jnp.int32, (SHARE, LANES), 0) + offset
    row_degree = jnp.sum(
        jnp.where(lane == row, extra[2:3], 0.0) + jnp.where(lane + LANES == row, extra[3:4], 0.0),
        axis=1,
        keepdims=True,
    )
    row_inverse = 1.0 / jnp.sqrt(row_degree)
    for half in range(2):
        block = total[half * SHARE : (half + 1) * SHARE]
        column_inverse = 1.0 / jnp.sqrt(extra[half : half + 1])
        out_ref[:, half * LANES : (half + 1) * LANES] = (
            block * row_inverse * column_inverse
        ).astype(jnp.bfloat16)


VMEM = pl.BlockSpec(memory_space=pltpu.VMEM)
SMEM = pl.BlockSpec(memory_space=pltpu.SMEM)
PARAMS = pltpu.CompilerParams(vmem_limit_bytes=48 * 1024 * 1024)


def homes():
    pairs = []
    for x in range(X):
        for y in range(Y):
            for core in range(CORES):
                for z in range(PANELS):
                    triple, residue = z // 3, z % 3
                    unit = 2 * core + x // 2
                    column = z
                    if unit:
                        column = (3 * triple + COLUMNS[residue][unit - 1]) % PANELS
                    user = 16 * triple + 2 * y + x % 2
                    source = ((x * Y + y) * CORES + core) * PANELS + z
                    pairs.append((source, user * PANELS + column))
    return pairs


def per_device(ratings, counts):
    rows, width = ratings.shape
    x, y, core, me = (lax.axis_index(name) for name in ("x", "y", "core", "z"))
    place = jnp.stack([core, me % 3, 2 * y + x % 2]).astype(jnp.int32)
    place = jnp.concatenate([place, counts])

    columns = [
        lax.ppermute(
            ratings,
            "z",
            [((z // 3 * 3 + COLUMNS[z % 3][i]) % PANELS, z) for z in range(PANELS)],
        )
        for i in range(3)
    ]
    triple = [ratings] + [
        lax.ppermute(
            ratings, "z", [(z // 3 * 3 + (z + by) % 3, z) for z in range(PANELS)]
        )
        for by in (2, 1)
    ]
    values = ratings.astype(jnp.float32)
    squares = jnp.sum(values * values, axis=1).reshape(rows // LANES, LANES)
    squares = jnp.pad(squares, ((0, 8 - rows // LANES), (0, 0)))
    squares = jnp.broadcast_to(squares[None], (PANELS, 8, LANES))
    squares = lax.all_to_all(squares, "z", 0, 0, tiled=True)

    slots = (SLOTS, SLOT_ROWS, LANES)
    keep, send = pl.pallas_call(
        partial_kernel,
        out_shape=(
            jax.ShapeDtypeStruct(slots, jnp.float32),
            jax.ShapeDtypeStruct(slots, jnp.bfloat16),
        ),
        in_specs=[SMEM] + [VMEM] * 7,
        out_specs=(VMEM, VMEM),
        scratch_shapes=[
            pltpu.VMEM((12 * width, width), jnp.float32),
            pltpu.VMEM((8, LANES), jnp.float32),
            pltpu.VMEM((8, LANES), jnp.float32),
        ],
        compiler_params=PARAMS,
        name="partial",
    )(place, squares, *triple, *columns)
    got = lax.ppermute(send, "core", [(0, 1), (1, 0)])
    total = pl.pallas_call(
        add_kernel,
        out_shape=jax.ShapeDtypeStruct(slots, jnp.bfloat16),
        in_specs=[VMEM, VMEM],
        out_specs=VMEM,
        compiler_params=PARAMS,
        name="add",
    )(keep, got)
    parts = lax.all_to_all(total, ("x", "y"), 0, 0, tiled=True)
    block = pl.pallas_call(
        finish_kernel,
        out_shape=jax.ShapeDtypeStruct((SHARE, width), jnp.bfloat16),
        in_specs=[SMEM, VMEM],
        out_specs=VMEM,
        compiler_params=PARAMS,
        name="finish",
    )(place, parts)
    return lax.ppermute(block, ("x", "y", "core", "z"), homes())


def solution(mesh):
    fine = Mesh(mesh.devices.reshape(X, Y, CORES, PANELS), ("x", "y", "core", "z"))
    users = ("x", "y", "core")
    return jax.shard_map(
        per_device,
        mesh=fine,
        in_specs=(P(users, "z"), P(users)),
        out_specs=P(users, "z"),
        check_vma=False,
    )
```

time: 112 us -> 103 us (0.920)
  the two profiles are of different devices: /device:TPU:8 before, /device:TPU:76 now
where the time goes in v4:
time: 103 us
  starting transfers between devices  45.3 us (44%)
  blocking collectives  33.3 us (32%)
  waiting for transfers between devices  17.2 us (17%)
  Pallas kernels  3.14 us (3%)
  local copies, waits for them, and re-layouts  2.16 us (2%)
  other arithmetic  1.81 us (2%)
    all_to_all x1, blocking collectives, per_device(): parts = lax.all_to_all(total, ('x', 'y'), 0, 0, tiled=True)  33.3 us
    ppermute x3, starting transfers between devices, per_device(): lax.ppermute(ratings, 'z', [((z // 3 * 3 + COLUMNS[z % 3][i]) % PANELS, z...  21.1 us
    all_to_all x1, waiting for transfers between devices, per_device(): squares = lax.all_to_all(squares, 'z', 0, 0, tiled=True)  9.74 us
    all_to_all x1, starting transfers between devices, per_device(): squares = lax.all_to_all(squares, 'z', 0, 0, tiled=True)  9.54 us
    ppermute x1, starting transfers between devices, per_device(): return lax.ppermute(block, ('x', 'y', 'core', 'z'), homes())  6.89 us
    ppermute x2, starting transfers between devices, per_device(): lax.ppermute(ratings, 'z', [(z // 3 * 3 + (z + by) % 3, z) for z in range...  5.85 us
    ppermute x1, waiting for transfers between devices, per_device(): return lax.ppermute(block, ('x', 'y', 'core', 'z'), homes())  5.14 us
    ppermute x1, waiting for transfers between devices, per_device(): got = lax.ppermute(send, 'core', [(0, 1), (1, 0)])  2.34 us
  transfers between devices with their start and end apart: 8, of which 3 were waited for; matrix products, arithmetic and copies ran while one was open for 2% of the time, Pallas kernels for 0%

profile of v4, /device:TPU:76, one launch (start us, length us, event | category | flops | bytes accessed | tf_op | source)
XLA Modules:
  0.0 103.0 jit_solution(17839882184026190777)
XLA Ops:
  0.0 6.1 %collective-permute-start.3 = (bf16[384,256]{1,0:T(8,128)(2,1)}, bf16[384,256]{1,0:T(8,128)(2,1)S(1)}, u32[]{:S(2)}, u32[]{:S(2)}) collective-permute-start(bf16[384,256]{1,0:T(8,128)(2,1)} %refs_0_.1), channel_id=1, source_target_pairs={{10,0},{8,1},{3,2},{1,3},{11,4},{6,5},{4,6},{2,7},{9,8},{7,9},{5,1... | collective-permute-start | bytes 589832 | tf_op jit(solution)/shard_map/ppermute | solution.py:158
  6.1 12.4 %collective-permute-start.2 = (bf16[384,256]{1,0:T(8,128)(2,1)}, bf16[384,256]{1,0:T(8,128)(2,1)S(1)}, u32[]{:S(2)}, u32[]{:S(2)}) collective-permute-start(bf16[384,256]{1,0:T(8,128)(2,1)} %refs_0_.1), channel_id=1, source_target_pairs={{9,0},{7,1},{5,2},{0,3},{10,4},{8,5},{3,6},{1,7},{11,8},{6,9},{4,1... | collective-permute-start | bytes 589832 | tf_op jit(solution)/shard_map/ppermute | solution.py:158
  18.5 1.9 %collective-permute-start.1 = (bf16[384,256]{1,0:T(8,128)(2,1)}, bf16[384,256]{1,0:T(8,128)(2,1)S(1)}, u32[]{:S(2)}, u32[]{:S(2)}) collective-permute-start(bf16[384,256]{1,0:T(8,128)(2,1)} %refs_0_.1), channel_id=1, source_target_pairs={{1,0},{2,1},{0,2},{4,3},{5,4},{3,5},{7,6},{8,7},{6,8},{10,9},{11,1... | collective-permute-start | bytes 589832 | tf_op jit(solution)/shard_map/ppermute | solution.py:166
  20.5 3.9 %collective-permute-start = (bf16[384,256]{1,0:T(8,128)(2,1)}, bf16[384,256]{1,0:T(8,128)(2,1)S(1)}, u32[]{:S(2)}, u32[]{:S(2)}) collective-permute-start(bf16[384,256]{1,0:T(8,128)(2,1)} %refs_0_.1), channel_id=1, source_target_pairs={{2,0},{0,1},{1,2},{5,3},{3,4},{4,5},{8,6},{6,7},{7,8},{11,9},{9,10... | collective-permute-start | bytes 589832 | tf_op jit(solution)/shard_map/ppermute | solution.py:166
  24.4 2.5 %collective-permute-start.4 = (bf16[384,256]{1,0:T(8,128)(2,1)}, bf16[384,256]{1,0:T(8,128)(2,1)S(1)}, u32[]{:S(2)}, u32[]{:S(2)}) collective-permute-start(bf16[384,256]{1,0:T(8,128)(2,1)} %refs_0_.1), channel_id=1, source_target_pairs={{11,0},{6,1},{4,2},{2,3},{9,4},{7,5},{5,6},{0,7},{10,8},{8,9},{3,1... | collective-permute-start | bytes 589832 | tf_op jit(solution)/shard_map/ppermute | solution.py:158
  27.0 1.1 %multiply_reduce_fusion = f32[384]{0:T(512)S(1)} fusion(bf16[384,256]{1,0:T(8,128)(2,1)} %refs_0_.1), kind=kLoop, calls=%fused_computation | loop fusion | flops 294528 | bytes 198144 | tf_op jit(solution)/shard_map/reduce_sum | solution.py:172
  28.0 0.6 broadcast_in_dim.2
  28.7 9.5 %all-to-all-start = ((f32[12,8,128]{2,1,0:T(8,128)}), f32[12,8,128]{2,1,0:T(8,128)S(1)}, u32[]{:S(2)}, u32[]{:S(2)}) async-start(f32[12,8,128]{2,1,0:T(8,128)} %broadcast_in_dim.2), calls=%async_computation | async-start | bytes 98304 | tf_op jit(solution)/shard_map/all_to_all | solution.py:175
  38.2 0.7 pad_add_fusion.place_ref
  38.9 9.7 %all-to-all-done.sums_ref = f32[12,8,128]{2,1,0:T(8,128)S(1)} async-done(((f32[12,8,128]{2,1,0:T(8,128)}), f32[12,8,128]{2,1,0:T(8,128)S(1)}, u32[]{:S(2)}, u32[]{:S(2)}) %all-to-all-start) | async-done | bytes 49184 | tf_op jit(solution)/shard_map/all_to_all | solution.py:175
  48.7 0.0 collective-permute-done.3.refs_4_
  48.7 0.0 collective-permute-done.2.refs_3_
  48.7 0.0 collective-permute-done.1.refs_2_
  48.7 0.0 collective-permute-done.refs_1_
  48.7 0.0 collective-permute-done.4.refs_5_
  48.7 0.0 copy-start
  48.7 0.9 copy-done
  49.7 2.3 %partial.1 = (f32[32,104,128]{2,1,0:T(8,128)S(1)}, bf16[32,104,128]{2,1,0:T(8,128)(2,1)S(1)}) custom-call(s32[9]{0:T(128)S(1)} %pad_add_fusion.place_ref, f32[12,8,128]{2,1,0:T(8,128)S(1)} %all-to-all-done.sums_ref, bf16[384,256]{1,0:T(8,128)(2,1)S(1)} %copy-done, bf16[384,256]{1,0:T(8,128)(2,1)S(1)} %collective-permute-done.refs_1_, ...), custom_call_target="tpu_custom_call" | custom-call | tf_op jit(solution)/shard_map/partial/pallas_call | solution.py:178
  51.9 1.9 %collective-permute-start.5 = (bf16[32,104,128]{2,1,0:T(8,128)(2,1)S(1)}, bf16[32,104,128]{2,1,0:T(8,128)(2,1)S(1)}, u32[]{:S(2)}, u32[]{:S(2)}) collective-permute-start(bf16[32,104,128]{2,1,0:T(8,128)(2,1)S(1)} %get-tuple-element.8), channel_id=1, source_target_pairs={{0,12},{12,0},{1,13},{13,1},{2,14},{14,2},{3,15},{15,3},{4,16},{16... | collective-permute-start | bytes 2555912 | tf_op jit(solution)/shard_map/ppermute | solution.py:194
  53.8 2.3 %collective-permute-done.5.got_ref = bf16[32,104,128]{2,1,0:T(8,128)(2,1)S(1)} collective-permute-done((bf16[32,104,128]{2,1,0:T(8,128)(2,1)S(1)}, bf16[32,104,128]{2,1,0:T(8,128)(2,1)S(1)}, u32[]{:S(2)}, u32[]{:S(2)}) %collective-permute-start.5) | collective-permute-done | bytes 852000 | tf_op jit(solution)/shard_map/ppermute | solution.py:194
  56.2 0.2 add.22
  56.4 33.3 %all_to_all.10.got_ref = bf16[32,104,128]{2,1,0:T(8,128)(2,1)S(1)} all-to-all(bf16[32,104,128]{2,1,0:T(8,128)(2,1)S(1)} %add.22), channel_id=1, replica_groups=mesh['x'=4,'y'=8,'core'=2,'z'=12] {'x','y'}, dimensions={0} | all-to-all | bytes 1703936 | tf_op jit(solution)/shard_map/all_to_all | solution.py:203
  89.6 0.7 finish.1
  90.3 6.9 %collective-permute-start.6 = (bf16[48,256]{1,0:T(8,128)(2,1)S(1)}, bf16[48,256]{1,0:T(8,128)(2,1)S(1)}, u32[]{:S(2)}, u32[]{:S(2)}) collective-permute-start(bf16[48,256]{1,0:T(8,128)(2,1)S(1)} %finish.1), channel_id=1, source_target_pairs={{0,0},{1,1},{2,2},{3,195},{4,196},{5,197},{6,390},{7,391},{8,392},... | collective-permute-start | bytes 73736 | tf_op jit(solution)/shard_map/ppermute | solution.py:212
  97.2 5.1 %collective-permute-done.6 = bf16[48,256]{1,0:T(8,128)(2,1)S(1)} collective-permute-done((bf16[48,256]{1,0:T(8,128)(2,1)S(1)}, bf16[48,256]{1,0:T(8,128)(2,1)S(1)}, u32[]{:S(2)}, u32[]{:S(2)}) %collective-permute-start.6) | collective-permute-done | bytes 24608 | tf_op jit(solution)/shard_map/ppermute | solution.py:212
  102.4 0.6 copy.4
  (1 shorter events, 0.0 us)
Async XLA Ops:
  0.0 48.7 %collective-permute-start.3 = (bf16[384,256]{1,0:T(8,128)(2,1)}, bf16[384,256]{1,0:T(8,128)(2,1)S(1)}, u32[]{:S(2)}, u32[]{:S(2)}) collective-permute-start(bf16[384,256]{1,0:T(8,128)(2,1)} %refs_0_.1), channel_id=1, source_target_pairs={{10,0},{8,1},{3,2},{1,3},{11,4},{6,5},{4,6},{2,7},{9,8},{7,9},{5,1... | collective-permute-start | bytes 589832 | tf_op jit(solution)/shard_map/ppermute | solution.py:158
  6.1 42.6 %collective-permute-start.2 = (bf16[384,256]{1,0:T(8,128)(2,1)}, bf16[384,256]{1,0:T(8,128)(2,1)S(1)}, u32[]{:S(2)}, u32[]{:S(2)}) collective-permute-start(bf16[384,256]{1,0:T(8,128)(2,1)} %refs_0_.1), channel_id=1, source_target_pairs={{9,0},{7,1},{5,2},{0,3},{10,4},{8,5},{3,6},{1,7},{11,8},{6,9},{4,1... | collective-permute-start | bytes 589832 | tf_op jit(solution)/shard_map/ppermute | solution.py:158
  18.5 30.2 %collective-permute-start.1 = (bf16[384,256]{1,0:T(8,128)(2,1)}, bf16[384,256]{1,0:T(8,128)(2,1)S(1)}, u32[]{:S(2)}, u32[]{:S(2)}) collective-permute-start(bf16[384,256]{1,0:T(8,128)(2,1)} %refs_0_.1), channel_id=1, source_target_pairs={{1,0},{2,1},{0,2},{4,3},{5,4},{3,5},{7,6},{8,7},{6,8},{10,9},{11,1... | collective-permute-start | bytes 589832 | tf_op jit(solution)/shard_map/ppermute | solution.py:166
  20.5 28.2 %collective-permute-start = (bf16[384,256]{1,0:T(8,128)(2,1)}, bf16[384,256]{1,0:T(8,128)(2,1)S(1)}, u32[]{:S(2)}, u32[]{:S(2)}) collective-permute-start(bf16[384,256]{1,0:T(8,128)(2,1)} %refs_0_.1), channel_id=1, source_target_pairs={{2,0},{0,1},{1,2},{5,3},{3,4},{4,5},{8,6},{6,7},{7,8},{11,9},{9,10... | collective-permute-start | bytes 589832 | tf_op jit(solution)/shard_map/ppermute | solution.py:166
  24.4 24.3 %collective-permute-start.4 = (bf16[384,256]{1,0:T(8,128)(2,1)}, bf16[384,256]{1,0:T(8,128)(2,1)S(1)}, u32[]{:S(2)}, u32[]{:S(2)}) collective-permute-start(bf16[384,256]{1,0:T(8,128)(2,1)} %refs_0_.1), channel_id=1, source_target_pairs={{11,0},{6,1},{4,2},{2,3},{9,4},{7,5},{5,6},{0,7},{10,8},{8,9},{3,1... | collective-permute-start | bytes 589832 | tf_op jit(solution)/shard_map/ppermute | solution.py:158
  28.7 20.0 %all-to-all-start = ((f32[12,8,128]{2,1,0:T(8,128)}), f32[12,8,128]{2,1,0:T(8,128)S(1)}, u32[]{:S(2)}, u32[]{:S(2)}) async-start(f32[12,8,128]{2,1,0:T(8,128)} %broadcast_in_dim.2), calls=%async_computation | async-start | bytes 98304 | tf_op jit(solution)/shard_map/all_to_all | solution.py:175
  48.7 0.9 copy-start
  51.9 4.3 %collective-permute-start.5 = (bf16[32,104,128]{2,1,0:T(8,128)(2,1)S(1)}, bf16[32,104,128]{2,1,0:T(8,128)(2,1)S(1)}, u32[]{:S(2)}, u32[]{:S(2)}) collective-permute-start(bf16[32,104,128]{2,1,0:T(8,128)(2,1)S(1)} %get-tuple-element.8), channel_id=1, source_target_pairs={{0,12},{12,0},{1,13},{13,1},{2,14},{14,2},{3,15},{15,3},{4,16},{16... | collective-permute-start | bytes 2555912 | tf_op jit(solution)/shard_map/ppermute | solution.py:194
  90.3 12.0 %collective-permute-start.6 = (bf16[48,256]{1,0:T(8,128)(2,1)S(1)}, bf16[48,256]{1,0:T(8,128)(2,1)S(1)}, u32[]{:S(2)}, u32[]{:S(2)}) collective-permute-start(bf16[48,256]{1,0:T(8,128)(2,1)S(1)} %finish.1), channel_id=1, source_target_pairs={{0,0},{1,1},{2,2},{3,195},{4,196},{5,197},{6,390},{7,391},{8,392},... | collective-permute-start | bytes 73736 | tf_op jit(solution)/shard_map/ppermute | solution.py:212

commit v5 on v4

--- a/solution.py
+++ b/solution.py
@@ -12,8 +12,43 @@
 SHARE = 48
 LANES = 128
 SLOT_ROWS = 2 * SHARE + 8
+AXES = ("x", "y", "core", "triple", "member")
 CORE, RESIDUE, SLAB, COUNTS = 0, 1, 2, 3
-COLUMNS = ((9, 10, 11), (7, 8, 6), (5, 3, 4))
+TRIPLES, MEMBERS = 4, 3
+FAR = ((9, 10, 11), (5, 6, 8), (3, 4, 7))
+
+
+def far_columns():
+    wanted = []
+    for z in range(PANELS):
+        triple, member = divmod(z, MEMBERS)
+        offsets = FAR[member]
+        if triple % 2:
+            offsets = [2 - offset for offset in FAR[2 - member]]
+        wanted.append([(3 * triple + offset) % PANELS for offset in offsets])
+    rounds = []
+    for _ in range(3):
+        taken = {}
+
+        def place(z, seen):
+            for panel in wanted[z]:
+                if panel not in seen:
+                    seen.add(panel)
+                    if panel not in taken or place(taken[panel], seen):
+                        taken[panel] = z
+                        return True
+            return False
+
+        for z in range(PANELS):
+            place(z, set())
+        chosen = {z: panel for panel, z in taken.items()}
+        rounds.append([chosen[z] for z in range(PANELS)])
+        for z in range(PANELS):
+            wanted[z].remove(chosen[z])
+    return rounds
+
+
+COLUMNS = far_columns()
 
 
 def split_rows(total):
@@ -24,6 +59,26 @@
 
 def join_rows(extra):
     return extra + pltpu.roll(extra, 4, 0)
+
+
+def sums_kernel(ratings_ref, before_ref, after_ref, sums_ref, own_ref):
+    own_ref[...] = ratings_ref[...]
+    squares = jnp.zeros(ratings_ref.shape, jnp.float32)
+    for ref in (ratings_ref, before_ref, after_ref):
+        values = ref[...].astype(jnp.float32)
+        squares = squares + values * values
+    upright = jnp.sum(squares, axis=1, keepdims=True)
+    corner = lax.broadcasted_iota(jnp.int32, (LANES, LANES), 0) == lax.broadcasted_iota(
+        jnp.int32, (LANES, LANES), 1
+    )
+    lying = [
+        jnp.sum(jnp.where(corner, upright[i : i + LANES], 0.0), axis=0, keepdims=True)
+        for i in range(0, upright.shape[0], LANES)
+    ]
+    lying.append(jnp.zeros((8 - len(lying), LANES), jnp.float32))
+    sums = jnp.concatenate(lying, axis=0)
+    for i in range(TRIPLES):
+        sums_ref[i] = sums
 
 
 def partial_kernel(place_ref, sums_ref, *refs):
@@ -31,7 +86,7 @@
     core, residue = place_ref[CORE], place_ref[RESIDUE]
     rows, width = panels[0].shape
     sums = sums_ref[0]
-    for i in range(1, PANELS):
+    for i in range(1, TRIPLES):
         sums = sums + sums_ref[i]
     corner = lax.broadcasted_iota(jnp.int32, (LANES, LANES), 0) == lax.broadcasted_iota(
         jnp.int32, (LANES, LANES), 1
@@ -137,12 +192,9 @@
         for y in range(Y):
             for core in range(CORES):
                 for z in range(PANELS):
-                    triple, residue = z // 3, z % 3
                     unit = 2 * core + x // 2
-                    column = z
-                    if unit:
-                        column = (3 * triple + COLUMNS[residue][unit - 1]) % PANELS
-                    user = 16 * triple + 2 * y + x % 2
+                    column = COLUMNS[unit - 1][z] if unit else z
+                    user = 16 * (z // MEMBERS) + 2 * y + x % 2
                     source = ((x * Y + y) * CORES + core) * PANELS + z
                     pairs.append((source, user * PANELS + column))
     return pairs
@@ -150,29 +202,28 @@
 
 def per_device(ratings, counts):
     rows, width = ratings.shape
-    x, y, core, me = (lax.axis_index(name) for name in ("x", "y", "core", "z"))
-    place = jnp.stack([core, me % 3, 2 * y + x % 2]).astype(jnp.int32)
+    x, y, core, member = (lax.axis_index(name) for name in ("x", "y", "core", "member"))
+    place = jnp.stack([core, member, 2 * y + x % 2]).astype(jnp.int32)
     place = jnp.concatenate([place, counts])
 
-    columns = [
-        lax.ppermute(
-            ratings,
-            "z",
-            [((z // 3 * 3 + COLUMNS[z % 3][i]) % PANELS, z) for z in range(PANELS)],
-        )
-        for i in range(3)
-    ]
-    triple = [ratings] + [
-        lax.ppermute(
-            ratings, "z", [(z // 3 * 3 + (z + by) % 3, z) for z in range(PANELS)]
-        )
-        for by in (2, 1)
-    ]
-    values = ratings.astype(jnp.float32)
-    squares = jnp.sum(values * values, axis=1).reshape(rows // LANES, LANES)
-    squares = jnp.pad(squares, ((0, 8 - rows // LANES), (0, 0)))
-    squares = jnp.broadcast_to(squares[None], (PANELS, 8, LANES))
-    squares = lax.all_to_all(squares, "z", 0, 0, tiled=True)
+    def fetch(sources):
+        pairs = [(source, z) for z, source in enumerate(sources)]
+        return lax.ppermute(ratings, ("triple", "member"), pairs)
+
+    triple = [fetch([z // 3 * 3 + (z + by) % 3 for z in range(PANELS)]) for by in (2, 1)]
+    columns = [fetch(sources) for sources in COLUMNS]
+    sums, own = pl.pallas_call(
+        sums_kernel,
+        out_shape=(
+            jax.ShapeDtypeStruct((TRIPLES, 8, LANES), jnp.float32),
+            jax.ShapeDtypeStruct((rows, width), ratings.dtype),
+        ),
+        in_specs=[VMEM] * 3,
+        out_specs=(VMEM, VMEM),
+        compiler_params=PARAMS,
+        name="sums",
+    )(ratings, *triple)
+    sums = lax.all_to_all(sums, "triple", 0, 0, tiled=True)
 
     slots = (SLOTS, SLOT_ROWS, LANES)
     keep, send = pl.pallas_call(
@@ -190,7 +241,7 @@
         ],
         compiler_params=PARAMS,
         name="partial",
-    )(place, squares, *triple, *columns)
+    )(place, sums, own, *triple, *columns)
     got = lax.ppermute(send, "core", [(0, 1), (1, 0)])
     total = pl.pallas_call(
         add_kernel,
@@ -209,16 +260,16 @@
         compiler_params=PARAMS,
         name="finish",
     )(place, parts)
-    return lax.ppermute(block, ("x", "y", "core", "z"), homes())
+    return lax.ppermute(block, AXES, homes())
 
 
 def solution(mesh):
-    fine = Mesh(mesh.devices.reshape(X, Y, CORES, PANELS), ("x", "y", "core", "z"))
-    users = ("x", "y", "core")
+    fine = Mesh(mesh.devices.reshape(X, Y, CORES, TRIPLES, MEMBERS), AXES)
+    users, items = AXES[:3], AXES[3:]
     return jax.shard_map(
         per_device,
         mesh=fine,
-        in_specs=(P(users, "z"), P(users)),
-        out_specs=P(users, "z"),
+        in_specs=(P(users, items), P(users)),
+        out_specs=P(users, items),
         check_vma=False,
     )

time: 103 us -> 105 us (1.019)
  the two profiles are of different devices: /device:TPU:76 before, /device:TPU:12 now
where the time goes in v5:
time: 105 us
  starting transfers between devices  47.4 us (45%)
  blocking collectives  33.3 us (32%)
  waiting for transfers between devices  17.7 us (17%)
  Pallas kernels  3.93 us (4%)
  local copies, waits for them, and re-layouts  1.53 us (1%)
    ppermute x5, starting transfers between devices, fetch(): return lax.ppermute(ratings, ('triple', 'member'), pairs)  33.5 us
    all_to_all x1, blocking collectives, per_device(): parts = lax.all_to_all(total, ('x', 'y'), 0, 0, tiled=True)  33.3 us
    ppermute x5, waiting for transfers between devices, fetch(): return lax.ppermute(ratings, ('triple', 'member'), pairs)  10.5 us
    ppermute x1, starting transfers between devices, per_device(): return lax.ppermute(block, AXES, homes())  8.75 us
    ppermute x1, waiting for transfers between devices, per_device(): return lax.ppermute(block, AXES, homes())  4.83 us
    all_to_all x1, starting transfers between devices, per_device(): sums = lax.all_to_all(sums, 'triple', 0, 0, tiled=True)  3.25 us
    ppermute x1, waiting for transfers between devices, per_device(): got = lax.ppermute(send, 'core', [(0, 1), (1, 0)])  2.34 us
    pallas_call x1, Pallas kernels, per_device(): pl.pallas_call(partial_kernel, out_shape=(jax.ShapeDtypeStruct(slots, jnp...  2.23 us
  transfers between devices with their start and end apart: 8, of which 4 were waited for; matrix products, arithmetic and copies ran while one was open for 1% of the time, Pallas kernels for 1%

profile of v5, /device:TPU:12, one launch (start us, length us, event | category | flops | bytes accessed | tf_op | source)
XLA Modules:
  0.0 104.7 jit_solution(11423262042974100697)
XLA Ops:
  0.0 6.1 %collective-permute-start.1 = (bf16[384,256]{1,0:T(8,128)(2,1)}, bf16[384,256]{1,0:T(8,128)(2,1)S(1)}, u32[]{:S(2)}, u32[]{:S(2)}) collective-permute-start(bf16[384,256]{1,0:T(8,128)(2,1)} %ratings_ref.1), channel_id=1, source_target_pairs={{1,0},{2,1},{0,2},{4,3},{5,4},{3,5},{7,6},{8,7},{6,8},{10,9},{11,1... | collective-permute-start | bytes 589832 | tf_op jit(solution)/shard_map/ppermute | solution.py:211
  6.1 1.9 %collective-permute-start = (bf16[384,256]{1,0:T(8,128)(2,1)}, bf16[384,256]{1,0:T(8,128)(2,1)S(1)}, u32[]{:S(2)}, u32[]{:S(2)}) collective-permute-start(bf16[384,256]{1,0:T(8,128)(2,1)} %ratings_ref.1), channel_id=1, source_target_pairs={{2,0},{0,1},{1,2},{5,3},{3,4},{4,5},{8,6},{6,7},{7,8},{11,9},{9,10... | collective-permute-start | bytes 589832 | tf_op jit(solution)/shard_map/ppermute | solution.py:211
  8.0 9.1 %collective-permute-start.2 = (bf16[384,256]{1,0:T(8,128)(2,1)}, bf16[384,256]{1,0:T(8,128)(2,1)S(1)}, u32[]{:S(2)}, u32[]{:S(2)}) collective-permute-start(bf16[384,256]{1,0:T(8,128)(2,1)} %ratings_ref.1), channel_id=1, source_target_pairs={{10,0},{5,1},{4,2},{1,3},{0,4},{7,5},{3,6},{11,7},{9,8},{8,9},{6,1... | collective-permute-start | bytes 589832 | tf_op jit(solution)/shard_map/ppermute | solution.py:211
  17.1 8.2 %collective-permute-start.4 = (bf16[384,256]{1,0:T(8,128)(2,1)}, bf16[384,256]{1,0:T(8,128)(2,1)S(1)}, u32[]{:S(2)}, u32[]{:S(2)}) collective-permute-start(bf16[384,256]{1,0:T(8,128)(2,1)} %ratings_ref.1), channel_id=1, source_target_pairs={{11,0},{8,1},{7,2},{10,3},{9,4},{6,5},{5,6},{2,7},{1,8},{4,9},{3,1... | collective-permute-start | bytes 589832 | tf_op jit(solution)/shard_map/ppermute | solution.py:211
  25.3 8.2 %collective-permute-start.3 = (bf16[384,256]{1,0:T(8,128)(2,1)}, bf16[384,256]{1,0:T(8,128)(2,1)S(1)}, u32[]{:S(2)}, u32[]{:S(2)}) collective-permute-start(bf16[384,256]{1,0:T(8,128)(2,1)} %ratings_ref.1), channel_id=1, source_target_pairs={{9,0},{6,1},{3,2},{2,3},{11,4},{8,5},{4,6},{0,7},{10,8},{7,9},{5,1... | collective-permute-start | bytes 589832 | tf_op jit(solution)/shard_map/ppermute | solution.py:211
  33.5 0.0 collective-permute-done.1.after_ref.refs_2_
  33.5 0.0 collective-permute-done.before_ref.refs_1_
  33.6 0.0 copy-start
  33.6 0.9 copy-done
  34.5 0.8 sums.1
  35.3 3.3 %all-to-all-start = ((f32[4,8,128]{2,1,0:T(8,128)}), f32[4,8,128]{2,1,0:T(8,128)S(1)}, u32[]{:S(2)}, u32[]{:S(2)}) async-start(f32[4,8,128]{2,1,0:T(8,128)} %get-tuple-element.9), calls=%async_computation | async-start | bytes 32768 | tf_op jit(solution)/shard_map/all_to_all | solution.py:226
  38.5 0.7 pad_add_fusion.place_ref
  39.3 0.0 collective-permute-done.2.refs_3_
  39.3 8.3 %collective-permute-done.4.refs_5_ = bf16[384,256]{1,0:T(8,128)(2,1)S(1)} collective-permute-done((bf16[384,256]{1,0:T(8,128)(2,1)}, bf16[384,256]{1,0:T(8,128)(2,1)S(1)}, u32[]{:S(2)}, u32[]{:S(2)}) %collective-permute-start.4) | collective-permute-done | bytes 196640 | tf_op jit(solution)/shard_map/ppermute | solution.py:211
  47.5 2.3 %collective-permute-done.3.refs_4_ = bf16[384,256]{1,0:T(8,128)(2,1)S(1)} collective-permute-done((bf16[384,256]{1,0:T(8,128)(2,1)}, bf16[384,256]{1,0:T(8,128)(2,1)S(1)}, u32[]{:S(2)}, u32[]{:S(2)}) %collective-permute-start.3) | collective-permute-done | bytes 196640 | tf_op jit(solution)/shard_map/ppermute | solution.py:211
  49.8 0.0 all-to-all-done.sums_ref
  49.8 2.2 %partial.1 = (f32[32,104,128]{2,1,0:T(8,128)S(1)}, bf16[32,104,128]{2,1,0:T(8,128)(2,1)S(1)}) custom-call(s32[9]{0:T(128)S(1)} %pad_add_fusion.place_ref, f32[4,8,128]{2,1,0:T(8,128)S(1)} %all-to-all-done.sums_ref, bf16[384,256]{1,0:T(8,128)(2,1)S(1)} %get-tuple-element.10.refs_0_, bf16[384,256]{1,0:T(8,128)(2,1)S(1)} %collective-permute-done.before_ref.refs_1_, ...), custom_call_target="tpu_custom_call" | custom-call | tf_op jit(solution)/shard_map/partial/pallas_call | solution.py:229
  52.1 1.9 %collective-permute-start.5 = (bf16[32,104,128]{2,1,0:T(8,128)(2,1)S(1)}, bf16[32,104,128]{2,1,0:T(8,128)(2,1)S(1)}, u32[]{:S(2)}, u32[]{:S(2)}) collective-permute-start(bf16[32,104,128]{2,1,0:T(8,128)(2,1)S(1)} %get-tuple-element.12), channel_id=1, source_target_pairs={{0,12},{12,0},{1,13},{13,1},{2,14},{14,2},{3,15},{15,3},{4,16},{16... | collective-permute-start | bytes 2555912 | tf_op jit(solution)/shard_map/ppermute | solution.py:245
  54.0 2.3 %collective-permute-done.5.got_ref = bf16[32,104,128]{2,1,0:T(8,128)(2,1)S(1)} collective-permute-done((bf16[32,104,128]{2,1,0:T(8,128)(2,1)S(1)}, bf16[32,104,128]{2,1,0:T(8,128)(2,1)S(1)}, u32[]{:S(2)}, u32[]{:S(2)}) %collective-permute-start.5) | collective-permute-done | bytes 852000 | tf_op jit(solution)/shard_map/ppermute | solution.py:245
  56.3 0.2 add.16
  56.5 33.3 %all_to_all.10.got_ref = bf16[32,104,128]{2,1,0:T(8,128)(2,1)S(1)} all-to-all(bf16[32,104,128]{2,1,0:T(8,128)(2,1)S(1)} %add.16), channel_id=1, replica_groups=mesh['x'=4,'y'=8,'core'=2,'triple'=4,'member'=3] {'x','y'}, dimensions={0} | all-to-all | bytes 1703936 | tf_op jit(solution)/shard_map/all_to_all | solution.py:254
  89.8 0.7 finish.1
  90.5 8.8 %collective-permute-start.6 = (bf16[48,256]{1,0:T(8,128)(2,1)S(1)}, bf16[48,256]{1,0:T(8,128)(2,1)S(1)}, u32[]{:S(2)}, u32[]{:S(2)}) collective-permute-start(bf16[48,256]{1,0:T(8,128)(2,1)S(1)} %finish.1), channel_id=1, source_target_pairs={{0,0},{1,1},{2,2},{3,195},{4,196},{5,197},{6,390},{7,391},{8,392},... | collective-permute-start | bytes 73736 | tf_op jit(solution)/shard_map/ppermute | solution.py:263
  99.2 4.8 %collective-permute-done.6 = bf16[48,256]{1,0:T(8,128)(2,1)S(1)} collective-permute-done((bf16[48,256]{1,0:T(8,128)(2,1)S(1)}, bf16[48,256]{1,0:T(8,128)(2,1)S(1)}, u32[]{:S(2)}, u32[]{:S(2)}) %collective-permute-start.6) | collective-permute-done | bytes 24608 | tf_op jit(solution)/shard_map/ppermute | solution.py:263
  104.1 0.6 copy.4
Async XLA Ops:
  0.0 33.5 %collective-permute-start.1 = (bf16[384,256]{1,0:T(8,128)(2,1)}, bf16[384,256]{1,0:T(8,128)(2,1)S(1)}, u32[]{:S(2)}, u32[]{:S(2)}) collective-permute-start(bf16[384,256]{1,0:T(8,128)(2,1)} %ratings_ref.1), channel_id=1, source_target_pairs={{1,0},{2,1},{0,2},{4,3},{5,4},{3,5},{7,6},{8,7},{6,8},{10,9},{11,1... | collective-permute-start | bytes 589832 | tf_op jit(solution)/shard_map/ppermute | solution.py:211
  6.1 27.5 %collective-permute-start = (bf16[384,256]{1,0:T(8,128)(2,1)}, bf16[384,256]{1,0:T(8,128)(2,1)S(1)}, u32[]{:S(2)}, u32[]{:S(2)}) collective-permute-start(bf16[384,256]{1,0:T(8,128)(2,1)} %ratings_ref.1), channel_id=1, source_target_pairs={{2,0},{0,1},{1,2},{5,3},{3,4},{4,5},{8,6},{6,7},{7,8},{11,9},{9,10... | collective-permute-start | bytes 589832 | tf_op jit(solution)/shard_map/ppermute | solution.py:211
  8.0 31.3 %collective-permute-start.2 = (bf16[384,256]{1,0:T(8,128)(2,1)}, bf16[384,256]{1,0:T(8,128)(2,1)S(1)}, u32[]{:S(2)}, u32[]{:S(2)}) collective-permute-start(bf16[384,256]{1,0:T(8,128)(2,1)} %ratings_ref.1), channel_id=1, source_target_pairs={{10,0},{5,1},{4,2},{1,3},{0,4},{7,5},{3,6},{11,7},{9,8},{8,9},{6,1... | collective-permute-start | bytes 589832 | tf_op jit(solution)/shard_map/ppermute | solution.py:211
  17.1 30.4 %collective-permute-start.4 = (bf16[384,256]{1,0:T(8,128)(2,1)}, bf16[384,256]{1,0:T(8,128)(2,1)S(1)}, u32[]{:S(2)}, u32[]{:S(2)}) collective-permute-start(bf16[384,256]{1,0:T(8,128)(2,1)} %ratings_ref.1), channel_id=1, source_target_pairs={{11,0},{8,1},{7,2},{10,3},{9,4},{6,5},{5,6},{2,7},{1,8},{4,9},{3,1... | collective-permute-start | bytes 589832 | tf_op jit(solution)/shard_map/ppermute | solution.py:211
  25.3 24.5 %collective-permute-start.3 = (bf16[384,256]{1,0:T(8,128)(2,1)}, bf16[384,256]{1,0:T(8,128)(2,1)S(1)}, u32[]{:S(2)}, u32[]{:S(2)}) collective-permute-start(bf16[384,256]{1,0:T(8,128)(2,1)} %ratings_ref.1), channel_id=1, source_target_pairs={{9,0},{6,1},{3,2},{2,3},{11,4},{8,5},{4,6},{0,7},{10,8},{7,9},{5,1... | collective-permute-start | bytes 589832 | tf_op jit(solution)/shard_map/ppermute | solution.py:211
  33.6 0.9 copy-start
  35.3 14.5 %all-to-all-start = ((f32[4,8,128]{2,1,0:T(8,128)}), f32[4,8,128]{2,1,0:T(8,128)S(1)}, u32[]{:S(2)}, u32[]{:S(2)}) async-start(f32[4,8,128]{2,1,0:T(8,128)} %get-tuple-element.9), calls=%async_computation | async-start | bytes 32768 | tf_op jit(solution)/shard_map/all_to_all | solution.py:226
  52.1 4.3 %collective-permute-start.5 = (bf16[32,104,128]{2,1,0:T(8,128)(2,1)S(1)}, bf16[32,104,128]{2,1,0:T(8,128)(2,1)S(1)}, u32[]{:S(2)}, u32[]{:S(2)}) collective-permute-start(bf16[32,104,128]{2,1,0:T(8,128)(2,1)S(1)} %get-tuple-element.12), channel_id=1, source_target_pairs={{0,12},{12,0},{1,13},{13,1},{2,14},{14,2},{3,15},{15,3},{4,16},{16... | collective-permute-start | bytes 2555912 | tf_op jit(solution)/shard_map/ppermute | solution.py:245
  90.5 13.6 %collective-permute-start.6 = (bf16[48,256]{1,0:T(8,128)(2,1)S(1)}, bf16[48,256]{1,0:T(8,128)(2,1)S(1)}, u32[]{:S(2)}, u32[]{:S(2)}) collective-permute-start(bf16[48,256]{1,0:T(8,128)(2,1)S(1)} %finish.1), channel_id=1, source_target_pairs={{0,0},{1,1},{2,2},{3,195},{4,196},{5,197},{6,390},{7,391},{8,392},... | collective-permute-start | bytes 73736 | tf_op jit(solution)/shard_map/ppermute | solution.py:263

commit v6 on v4

v6 whole, which is shorter than its diff:
```python
import jax
import jax.numpy as jnp
from jax import lax
from jax.experimental import pallas as pl
from jax.experimental.pallas import tpu as pltpu
from jax.sharding import Mesh, PartitionSpec as P

X, Y, CORES, PANELS = 4, 8, 2, 12
SLOTS = X * Y
BLOCK = 64
ITEMS = 3072
SHARE = 48
LANES = 128
SLOT_ROWS = 2 * SHARE + 8
AXES = ("x", "y", "core", "triple", "member")
COUNTS = 4
AXES = ("x", "y", "core", "z")
MEMBERS = 3
REACH = 3
UNITS = ((-3, (4, 1, 3, 2)), (-1, (2, 0, 1, -1)), (1, (-3, 0, -2, -1)))


def split_rows(total):
    high = total.astype(jnp.bfloat16).astype(jnp.float32)
    first = lax.broadcasted_iota(jnp.int32, total.shape, 0) < 4
    return jnp.where(first, high, total - high)


def join_rows(extra):
    return extra + pltpu.roll(extra, 4, 0)


def held(place_ref):
    member = lax.rem(place_ref[3], MEMBERS)
    first = sum(jnp.where(member == i, UNITS[i][0], 0) for i in range(MEMBERS))
    return member, lax.div(lax.rem(place_ref[3] + first + PANELS, PANELS), MEMBERS)


def diagonal():
    shape = (LANES, LANES)
    rows = lax.broadcasted_iota(jnp.int32, shape, 0)
    return rows == lax.broadcasted_iota(jnp.int32, shape, 1)


def sums_kernel(*refs):
    panels, (sums_ref, own_ref) = refs[:-2], refs[-2:]
    own_ref[...] = panels[0][...]
    squares = jnp.zeros(own_ref.shape, jnp.float32)
    for ref in panels:
        values = ref[...].astype(jnp.float32)
        squares = squares + values * values
    upright = jnp.sum(squares, axis=1, keepdims=True)
    corner = diagonal()
    lying = [
        jnp.sum(jnp.where(corner, upright[i : i + LANES], 0.0), axis=0, keepdims=True)
        for i in range(0, upright.shape[0], LANES)
    ]
    lying.append(jnp.zeros((8 - len(lying), LANES), jnp.float32))
    sums_ref[...] = jnp.concatenate(lying, axis=0)


def partial_kernel(place_ref, near_ref, far_ref, *refs):
    panels, (keep_ref, send_ref, gram_ref, row_ref, column_ref) = refs[:8], refs[8:]
    core = place_ref[2]
    member, triple = held(place_ref)
    rows, width = panels[0].shape
    squares = jnp.zeros((rows, width), jnp.float32)
    for ref in (panels[0], panels[2 * REACH]):
        values = ref[...].astype(jnp.float32)
        squares = squares + values * values
    sums = near_ref[...] + far_ref[...]
    corner = diagonal()
    square_sum = jnp.sum(squares, axis=1, keepdims=True) + jnp.concatenate(
        [
            jnp.sum(jnp.where(corner, sums[i : i + 1], 0.0), axis=1, keepdims=True)
            for i in range(rows // LANES)
        ],
        axis=0,
    )
    position = lax.broadcasted_iota(jnp.int32, (BLOCK, 1), 0)
    live = jnp.concatenate(
        [
            (position < place_ref[COUNTS + i]).astype(jnp.float32)
            for i in range(rows // BLOCK)
        ],
        axis=0,
    )
    scale = live / jnp.sqrt(square_sum / ITEMS + 1e-05)

    def degree(ref):
        values = ref[...].astype(jnp.float32)
        weighted = (scale * values).astype(jnp.bfloat16)
        total = values * weighted.astype(jnp.float32)
        return weighted, jnp.sum(total, axis=0, keepdims=True)

    def keep_degree(target, at, total):
        for half in range(2):
            lanes = total[:, half * LANES : (half + 1) * LANES]
            target[pl.ds(2 * at + half, 1), :] = lanes

    for its_member, (first, columns) in enumerate(UNITS):

        @pl.when(member == its_member)
        def _():
            row_panels = [panels[REACH + first + i] for i in range(MEMBERS)]
            for i, ref in enumerate(row_panels):
                keep_degree(row_ref, i, degree(ref)[1])
            for unit, offset in enumerate(columns):
                weighted, total = degree(panels[REACH + offset])
                keep_degree(column_ref, unit, total)
                for i, ref in enumerate(row_panels):
                    gram_ref[pl.ds((3 * unit + i) * width, width), :] = lax.dot_general(
                        ref[...],
                        weighted,
                        (((0,), (0,)), ((), ())),
                        preferred_element_type=jnp.float32,
                    )

    for x in range(X):
        slot = lax.rem(triple + x, X) * Y
        for y in range(Y):
            start = (2 * y + x % 2) * SHARE
            low, high = start // LANES, (start + SHARE - 1) // LANES
            for mine in (True, False):
                unit = 2 * (core if mine else 1 - core) + x // 2
                four = [column_ref[pl.ds(2 * unit + half, 1), :] for half in range(2)]
                four += [row_ref[pl.ds(i, 1), :] for i in (low, high)]
                extra = split_rows(jnp.concatenate(four + four, axis=0))
                at = pl.multiple_of(unit * 3 * width + start, 16)
                block = gram_ref[pl.ds(at, SHARE), :]
                whole = jnp.concatenate([block[:, :LANES], block[:, LANES:], extra], axis=0)
                ref = keep_ref if mine else send_ref
                ref[slot + y] = whole.astype(ref.dtype)


def add_kernel(keep_ref, got_ref, out_ref):
    for slot in range(SLOTS):
        total = keep_ref[slot] + got_ref[slot].astype(jnp.float32)
        extra = split_rows(join_rows(total[2 * SHARE :]))
        out_ref[slot] = jnp.concatenate([total[: 2 * SHARE], extra], axis=0).astype(
            jnp.bfloat16
        )


def finish_kernel(place_ref, got_ref, out_ref):
    by = lax.rem(place_ref[0] - held(place_ref)[1] + X, X)
    offset = lax.rem((2 * place_ref[1] + lax.rem(by, 2)) * SHARE, LANES)
    total = got_ref[0].astype(jnp.float32)
    for slot in range(1, SLOTS):
        total = total + got_ref[slot].astype(jnp.float32)
    extra = join_rows(total[2 * SHARE :])
    lane = lax.broadcasted_iota(jnp.int32, (SHARE, LANES), 1)
    row = lax.broadcasted_iota(jnp.int32, (SHARE, LANES), 0) + offset
    row_degree = jnp.sum(
        jnp.where(lane == row, extra[2:3], 0.0) + jnp.where(lane + LANES == row, extra[3:4], 0.0),
        axis=1,
        keepdims=True,
    )
    row_inverse = 1.0 / jnp.sqrt(row_degree)
    for half in range(2):
        block = total[half * SHARE : (half + 1) * SHARE]
        column_inverse = 1.0 / jnp.sqrt(extra[half : half + 1])
        out_ref[:, half * LANES : (half + 1) * LANES] = (
            block * row_inverse * column_inverse
        ).astype(jnp.bfloat16)


VMEM = pl.BlockSpec(memory_space=pltpu.VMEM)
SMEM = pl.BlockSpec(memory_space=pltpu.SMEM)
PARAMS = pltpu.CompilerParams(vmem_limit_bytes=48 * 1024 * 1024)


def homes():
    pairs = []
    for x in range(X):
        for y in range(Y):
            for core in range(CORES):
                for z in range(PANELS):
                    first, columns = UNITS[z % MEMBERS]
                    triple = (z + first) % PANELS // MEMBERS
                    by = (x - triple) % X
                    column = (z + columns[2 * core + by // 2]) % PANELS
                    user = 16 * triple + 2 * y + by % 2
                    source = ((x * Y + y) * CORES + core) * PANELS + z
                    pairs.append((source, user * PANELS + column))
    return pairs


def per_device(ratings, counts):
    rows, width = ratings.shape
    x, y, core, me = (lax.axis_index(name) for name in AXES)
    place = jnp.concatenate([jnp.stack([x, y, core, me]).astype(jnp.int32), counts])

    def fetch(array, by, at=range(PANELS)):
        return lax.ppermute(array, "z", [((z + by) % PANELS, z) for z in at])

    above, below = [ratings], [ratings]
    for _ in range(REACH):
        above.append(fetch(above[-1], 1))
        below.append(fetch(below[-1], -1))
    last = fetch(ratings, REACH + 1, range(0, PANELS, MEMBERS))
    near, own = pl.pallas_call(
        sums_kernel,
        out_shape=(
            jax.ShapeDtypeStruct((8, LANES), jnp.float32),
            jax.ShapeDtypeStruct((rows, width), ratings.dtype),
        ),
        in_specs=[VMEM] * 5,
        out_specs=(VMEM, VMEM),
        compiler_params=PARAMS,
        name="sums",
    )(*above[:3], *below[1:3])
    far = fetch(near, PANELS // 2)
    panels = below[:0:-1] + [own] + above[1:] + [last]

    slots = (SLOTS, SLOT_ROWS, LANES)
    keep, send = pl.pallas_call(
        partial_kernel,
        out_shape=(
            jax.ShapeDtypeStruct(slots, jnp.float32),
            jax.ShapeDtypeStruct(slots, jnp.bfloat16),
        ),
        in_specs=[SMEM] + [VMEM] * 10,
        out_specs=(VMEM, VMEM),
        scratch_shapes=[
            pltpu.VMEM((12 * width, width), jnp.float32),
            pltpu.VMEM((8, LANES), jnp.float32),
            pltpu.VMEM((8, LANES), jnp.float32),
        ],
        compiler_params=PARAMS,
        name="partial",
    )(place, near, far, *panels)
    got = lax.ppermute(send, "core", [(0, 1), (1, 0)])
    total = pl.pallas_call(
        add_kernel,
        out_shape=jax.ShapeDtypeStruct(slots, jnp.bfloat16),
        in_specs=[VMEM, VMEM],
        out_specs=VMEM,
        compiler_params=PARAMS,
        name="add",
    )(keep, got)
    parts = lax.all_to_all(total, ("x", "y"), 0, 0, tiled=True)
    block = pl.pallas_call(
        finish_kernel,
        out_shape=jax.ShapeDtypeStruct((SHARE, width), jnp.bfloat16),
        in_specs=[SMEM, VMEM],
        out_specs=VMEM,
        compiler_params=PARAMS,
        name="finish",
    )(place, parts)
    return lax.ppermute(block, AXES, homes())


def solution(mesh):
    fine = Mesh(mesh.devices.reshape(X, Y, CORES, PANELS), AXES)
    users = AXES[:3]
    return jax.shard_map(
        per_device,
        mesh=fine,
        in_specs=(P(users, "z"), P(users)),
        out_specs=P(users, "z"),
        check_vma=False,
    )
```

time: 103 us -> 104 us (level)
  the two profiles are of different devices: /device:TPU:76 before, /device:TPU:8 now
where the time goes in v6:
time: 104 us; the launch traced here: 103 us
  starting transfers between devices  40.6 us (39%)
  blocking collectives  34.7 us (33%)
  waiting for transfers between devices  22 us (21%)
  Pallas kernels  3.58 us (3%)
  local copies, waits for them, and re-layouts  2.26 us (2%)
    ppermute x8, starting transfers between devices, fetch(): return lax.ppermute(array, 'z', [((z + by) % PANELS, z) for z in at])  36.6 us
    all_to_all x1, blocking collectives, per_device(): parts = lax.all_to_all(total, ('x', 'y'), 0, 0, tiled=True)  34.7 us
    ppermute x8, waiting for transfers between devices, fetch(): return lax.ppermute(array, 'z', [((z + by) % PANELS, z) for z in at])  14.2 us
    ppermute x1, waiting for transfers between devices, per_device(): return lax.ppermute(block, AXES, homes())  5.47 us
    pallas_call x1, Pallas kernels, per_device(): pl.pallas_call(partial_kernel, out_shape=(jax.ShapeDtypeStruct(slots, jnp...  2.42 us
    ppermute x1, waiting for transfers between devices, per_device(): got = lax.ppermute(send, 'core', [(0, 1), (1, 0)])  2.34 us
  transfers between devices with their start and end apart: 10, of which 6 were waited for; matrix products, arithmetic and copies ran while one was open for 1% of the time, Pallas kernels for 0%

profile of v6, /device:TPU:8, one launch (start us, length us, event | category | flops | bytes accessed | tf_op | source)
XLA Modules:
  0.0 103.2 jit_solution(1018332654277809891)
XLA Ops:
  0.0 4.3 %collective-permute-start.2 = (bf16[384,256]{1,0:T(8,128)(2,1)}, bf16[384,256]{1,0:T(8,128)(2,1)S(1)}, u32[]{:S(2)}, u32[]{:S(2)}) collective-permute-start(bf16[384,256]{1,0:T(8,128)(2,1)} %refs_0_.1), channel_id=1, source_target_pairs={{11,0},{0,1},{1,2},{2,3},{3,4},{4,5},{5,6},{6,7},{7,8},{8,9},{9,10... | collective-permute-start | bytes 589832 | tf_op jit(solution)/shard_map/ppermute | solution.py:195
  4.3 12.2 %collective-permute-start = (bf16[384,256]{1,0:T(8,128)(2,1)}, bf16[384,256]{1,0:T(8,128)(2,1)S(1)}, u32[]{:S(2)}, u32[]{:S(2)}) collective-permute-start(bf16[384,256]{1,0:T(8,128)(2,1)} %refs_0_.1), channel_id=1, source_target_pairs={{1,0},{2,1},{3,2},{4,3},{5,4},{6,5},{7,6},{8,7},{9,8},{10,9},{11,1... | collective-permute-start | bytes 589832 | tf_op jit(solution)/shard_map/ppermute | solution.py:195
  16.5 3.2 %collective-permute-done.2.refs_3_.refs_2_ = bf16[384,256]{1,0:T(8,128)(2,1)S(1)} collective-permute-done((bf16[384,256]{1,0:T(8,128)(2,1)}, bf16[384,256]{1,0:T(8,128)(2,1)S(1)}, u32[]{:S(2)}, u32[]{:S(2)}) %collective-permute-start.2) | collective-permute-done | bytes 196640 | tf_op jit(solution)/shard_map/ppermute | solution.py:195
  19.7 1.9 %collective-permute-start.3 = (bf16[384,256]{1,0:T(8,128)(2,1)S(1)}, bf16[384,256]{1,0:T(8,128)(2,1)S(1)}, u32[]{:S(2)}, u32[]{:S(2)}) collective-permute-start(bf16[384,256]{1,0:T(8,128)(2,1)S(1)} %collective-permute-done.2.refs_3_.refs_2_), channel_id=1, source_target_pairs={{11,0},{0,1},{1,2},{2,3},{3,4},{4,5},{5,6},{6,7},{7,8},{8,9},{9,10... | collective-permute-start | bytes 589832 | tf_op jit(solution)/shard_map/ppermute | solution.py:195
  21.6 0.0 collective-permute-done.refs_1_.refs_4_
  21.6 5.1 %collective-permute-start.1 = (bf16[384,256]{1,0:T(8,128)(2,1)S(1)}, bf16[384,256]{1,0:T(8,128)(2,1)S(1)}, u32[]{:S(2)}, u32[]{:S(2)}) collective-permute-start(bf16[384,256]{1,0:T(8,128)(2,1)S(1)} %collective-permute-done.refs_1_.refs_4_), channel_id=1, source_target_pairs={{1,0},{2,1},{3,2},{4,3},{5,4},{6,5},{7,6},{8,7},{9,8},{10,9},{11,1... | collective-permute-start | bytes 589832 | tf_op jit(solution)/shard_map/ppermute | solution.py:195
  26.7 1.3 %collective-permute-start.7 = (bf16[384,256]{1,0:T(8,128)(2,1)}, bf16[384,256]{1,0:T(8,128)(2,1)S(1)}, u32[]{:S(2)}, u32[]{:S(2)}) collective-permute-start(bf16[384,256]{1,0:T(8,128)(2,1)} %refs_0_.1), channel_id=1, source_target_pairs={{4,0},{7,3},{10,6},{1,9},{16,12},{19,15},{22,18},{13,21},{28,24},{... | collective-permute-start | bytes 589832 | tf_op jit(solution)/shard_map/ppermute | solution.py:195
  28.0 0.8 collective-permute-done.3.refs_4_.refs_1_
  28.9 3.7 %collective-permute-start.5 = (bf16[384,256]{1,0:T(8,128)(2,1)S(1)}, bf16[384,256]{1,0:T(8,128)(2,1)S(1)}, u32[]{:S(2)}, u32[]{:S(2)}) collective-permute-start(bf16[384,256]{1,0:T(8,128)(2,1)S(1)} %collective-permute-done.3.refs_4_.refs_1_), channel_id=1, source_target_pairs={{11,0},{0,1},{1,2},{2,3},{3,4},{4,5},{5,6},{6,7},{7,8},{8,9},{9,10... | collective-permute-start | bytes 589832 | tf_op jit(solution)/shard_map/ppermute | solution.py:195
  32.6 1.6 %collective-permute-done.1.refs_2_.refs_5_ = bf16[384,256]{1,0:T(8,128)(2,1)S(1)} collective-permute-done((bf16[384,256]{1,0:T(8,128)(2,1)S(1)}, bf16[384,256]{1,0:T(8,128)(2,1)S(1)}, u32[]{:S(2)}, u32[]{:S(2)}) %collective-permute-start.1) | collective-permute-done | bytes 196640 | tf_op jit(solution)/shard_map/ppermute | solution.py:195
  34.2 5.6 %collective-permute-start.6 = (bf16[384,256]{1,0:T(8,128)(2,1)S(1)}, bf16[384,256]{1,0:T(8,128)(2,1)S(1)}, u32[]{:S(2)}, u32[]{:S(2)}) collective-permute-start(bf16[384,256]{1,0:T(8,128)(2,1)S(1)} %collective-permute-done.1.refs_2_.refs_5_), channel_id=1, source_target_pairs={{1,0},{2,1},{3,2},{4,3},{5,4},{6,5},{7,6},{8,7},{9,8},{10,9},{11,1... | collective-permute-start | bytes 589832 | tf_op jit(solution)/shard_map/ppermute | solution.py:195
  39.8 0.0 copy-start
  39.8 0.9 copy-done
  40.7 0.3 sums.1
  40.9 2.5 %collective-permute-start.4 = (f32[8,128]{1,0:T(8,128)S(1)}, f32[8,128]{1,0:T(8,128)S(1)}, u32[]{:S(2)}, u32[]{:S(2)}) collective-permute-start(f32[8,128]{1,0:T(8,128)S(1)} %get-tuple-element.9.near_ref), channel_id=1, source_target_pairs={{6,0},{7,1},{8,2},{9,3},{10,4},{11,5},{0,6},{1,7},{2,8},{3,9},{4,1... | collective-permute-start | bytes 12296 | tf_op jit(solution)/shard_map/ppermute | solution.py:195
  43.4 0.7 concatenate.3.place_ref
  44.2 0.0 collective-permute-done.7.refs_7_
  44.2 8.6 %collective-permute-done.4.far_ref = f32[8,128]{1,0:T(8,128)S(1)} collective-permute-done((f32[8,128]{1,0:T(8,128)S(1)}, f32[8,128]{1,0:T(8,128)S(1)}, u32[]{:S(2)}, u32[]{:S(2)}) %collective-permute-start.4) | collective-permute-done | bytes 4128 | tf_op jit(solution)/shard_map/ppermute | solution.py:195
  52.8 0.0 collective-permute-done.5.refs_0_
  52.8 0.0 collective-permute-done.6.refs_6_
  52.8 2.4 %partial.1 = (f32[32,104,128]{2,1,0:T(8,128)S(1)}, bf16[32,104,128]{2,1,0:T(8,128)(2,1)S(1)}) custom-call(s32[10]{0:T(128)S(1)} %concatenate.3.place_ref, f32[8,128]{1,0:T(8,128)S(1)} %get-tuple-element.9.near_ref, f32[8,128]{1,0:T(8,128)S(1)} %collective-permute-done.4.far_ref, bf16[384,256]{1,0:T(8,128)(2,1)S(1)} %collective-permute-done.5.refs_0_, ...), custom_call_target="tpu_custom_call" | custom-call | tf_op jit(solution)/shard_map/partial/pallas_call | solution.py:217
  55.2 1.9 %collective-permute-start.8 = (bf16[32,104,128]{2,1,0:T(8,128)(2,1)S(1)}, bf16[32,104,128]{2,1,0:T(8,128)(2,1)S(1)}, u32[]{:S(2)}, u32[]{:S(2)}) collective-permute-start(bf16[32,104,128]{2,1,0:T(8,128)(2,1)S(1)} %get-tuple-element.12), channel_id=1, source_target_pairs={{0,12},{12,0},{1,13},{13,1},{2,14},{14,2},{3,15},{15,3},{4,16},{16... | collective-permute-start | bytes 2555912 | tf_op jit(solution)/shard_map/ppermute | solution.py:233
  57.1 2.3 %collective-permute-done.8.got_ref = bf16[32,104,128]{2,1,0:T(8,128)(2,1)S(1)} collective-permute-done((bf16[32,104,128]{2,1,0:T(8,128)(2,1)S(1)}, bf16[32,104,128]{2,1,0:T(8,128)(2,1)S(1)}, u32[]{:S(2)}, u32[]{:S(2)}) %collective-permute-start.8) | collective-permute-done | bytes 852000 | tf_op jit(solution)/shard_map/ppermute | solution.py:233
  59.5 0.2 add.1
  59.7 34.7 %all_to_all.5.got_ref = bf16[32,104,128]{2,1,0:T(8,128)(2,1)S(1)} all-to-all(bf16[32,104,128]{2,1,0:T(8,128)(2,1)S(1)} %add.1), channel_id=1, replica_groups=mesh['x'=4,'y'=8,'core'=2,'z'=12] {'x','y'}, dimensions={0} | all-to-all | bytes 1703936 | tf_op jit(solution)/shard_map/all_to_all | solution.py:242
  94.4 0.7 finish.1
  95.1 2.1 %collective-permute-start.9 = (bf16[48,256]{1,0:T(8,128)(2,1)S(1)}, bf16[48,256]{1,0:T(8,128)(2,1)S(1)}, u32[]{:S(2)}, u32[]{:S(2)}) collective-permute-start(bf16[48,256]{1,0:T(8,128)(2,1)S(1)} %finish.1), channel_id=1, source_target_pairs={{0,592},{1,3},{2,206},{3,7},{4,208},{5,389},{6,211},{7,391},{8,593... | collective-permute-start | bytes 73736 | tf_op jit(solution)/shard_map/ppermute | solution.py:251
  97.2 5.5 %collective-permute-done.9 = bf16[48,256]{1,0:T(8,128)(2,1)S(1)} collective-permute-done((bf16[48,256]{1,0:T(8,128)(2,1)S(1)}, bf16[48,256]{1,0:T(8,128)(2,1)S(1)}, u32[]{:S(2)}, u32[]{:S(2)}) %collective-permute-start.9) | collective-permute-done | bytes 24608 | tf_op jit(solution)/shard_map/ppermute | solution.py:251
  102.6 0.6 copy.4
Async XLA Ops:
  0.0 19.7 %collective-permute-start.2 = (bf16[384,256]{1,0:T(8,128)(2,1)}, bf16[384,256]{1,0:T(8,128)(2,1)S(1)}, u32[]{:S(2)}, u32[]{:S(2)}) collective-permute-start(bf16[384,256]{1,0:T(8,128)(2,1)} %refs_0_.1), channel_id=1, source_target_pairs={{11,0},{0,1},{1,2},{2,3},{3,4},{4,5},{5,6},{6,7},{7,8},{8,9},{9,10... | collective-permute-start | bytes 589832 | tf_op jit(solution)/shard_map/ppermute | solution.py:195
  4.3 17.3 %collective-permute-start = (bf16[384,256]{1,0:T(8,128)(2,1)}, bf16[384,256]{1,0:T(8,128)(2,1)S(1)}, u32[]{:S(2)}, u32[]{:S(2)}) collective-permute-start(bf16[384,256]{1,0:T(8,128)(2,1)} %refs_0_.1), channel_id=1, source_target_pairs={{1,0},{2,1},{3,2},{4,3},{5,4},{6,5},{7,6},{8,7},{9,8},{10,9},{11,1... | collective-permute-start | bytes 589832 | tf_op jit(solution)/shard_map/ppermute | solution.py:195
  19.7 9.2 %collective-permute-start.3 = (bf16[384,256]{1,0:T(8,128)(2,1)S(1)}, bf16[384,256]{1,0:T(8,128)(2,1)S(1)}, u32[]{:S(2)}, u32[]{:S(2)}) collective-permute-start(bf16[384,256]{1,0:T(8,128)(2,1)S(1)} %collective-permute-done.2.refs_3_.refs_2_), channel_id=1, source_target_pairs={{11,0},{0,1},{1,2},{2,3},{3,4},{4,5},{5,6},{6,7},{7,8},{8,9},{9,10... | collective-permute-start | bytes 589832 | tf_op jit(solution)/shard_map/ppermute | solution.py:195
  21.6 12.6 %collective-permute-start.1 = (bf16[384,256]{1,0:T(8,128)(2,1)S(1)}, bf16[384,256]{1,0:T(8,128)(2,1)S(1)}, u32[]{:S(2)}, u32[]{:S(2)}) collective-permute-start(bf16[384,256]{1,0:T(8,128)(2,1)S(1)} %collective-permute-done.refs_1_.refs_4_), channel_id=1, source_target_pairs={{1,0},{2,1},{3,2},{4,3},{5,4},{6,5},{7,6},{8,7},{9,8},{10,9},{11,1... | collective-permute-start | bytes 589832 | tf_op jit(solution)/shard_map/ppermute | solution.py:195
  26.7 17.4 %collective-permute-start.7 = (bf16[384,256]{1,0:T(8,128)(2,1)}, bf16[384,256]{1,0:T(8,128)(2,1)S(1)}, u32[]{:S(2)}, u32[]{:S(2)}) collective-permute-start(bf16[384,256]{1,0:T(8,128)(2,1)} %refs_0_.1), channel_id=1, source_target_pairs={{4,0},{7,3},{10,6},{1,9},{16,12},{19,15},{22,18},{13,21},{28,24},{... | collective-permute-start | bytes 589832 | tf_op jit(solution)/shard_map/ppermute | solution.py:195
  28.9 23.9 %collective-permute-start.5 = (bf16[384,256]{1,0:T(8,128)(2,1)S(1)}, bf16[384,256]{1,0:T(8,128)(2,1)S(1)}, u32[]{:S(2)}, u32[]{:S(2)}) collective-permute-start(bf16[384,256]{1,0:T(8,128)(2,1)S(1)} %collective-permute-done.3.refs_4_.refs_1_), channel_id=1, source_target_pairs={{11,0},{0,1},{1,2},{2,3},{3,4},{4,5},{5,6},{6,7},{7,8},{8,9},{9,10... | collective-permute-start | bytes 589832 | tf_op jit(solution)/shard_map/ppermute | solution.py:195
  34.2 18.6 %collective-permute-start.6 = (bf16[384,256]{1,0:T(8,128)(2,1)S(1)}, bf16[384,256]{1,0:T(8,128)(2,1)S(1)}, u32[]{:S(2)}, u32[]{:S(2)}) collective-permute-start(bf16[384,256]{1,0:T(8,128)(2,1)S(1)} %collective-permute-done.1.refs_2_.refs_5_), channel_id=1, source_target_pairs={{1,0},{2,1},{3,2},{4,3},{5,4},{6,5},{7,6},{8,7},{9,8},{10,9},{11,1... | collective-permute-start | bytes 589832 | tf_op jit(solution)/shard_map/ppermute | solution.py:195
  39.8 0.9 copy-start
  40.9 11.8 %collective-permute-start.4 = (f32[8,128]{1,0:T(8,128)S(1)}, f32[8,128]{1,0:T(8,128)S(1)}, u32[]{:S(2)}, u32[]{:S(2)}) collective-permute-start(f32[8,128]{1,0:T(8,128)S(1)} %get-tuple-element.9.near_ref), channel_id=1, source_target_pairs={{6,0},{7,1},{8,2},{9,3},{10,4},{11,5},{0,6},{1,7},{2,8},{3,9},{4,1... | collective-permute-start | bytes 12296 | tf_op jit(solution)/shard_map/ppermute | solution.py:195
  55.2 4.3 %collective-permute-start.8 = (bf16[32,104,128]{2,1,0:T(8,128)(2,1)S(1)}, bf16[32,104,128]{2,1,0:T(8,128)(2,1)S(1)}, u32[]{:S(2)}, u32[]{:S(2)}) collective-permute-start(bf16[32,104,128]{2,1,0:T(8,128)(2,1)S(1)} %get-tuple-element.12), channel_id=1, source_target_pairs={{0,12},{12,0},{1,13},{13,1},{2,14},{14,2},{3,15},{15,3},{4,16},{16... | collective-permute-start | bytes 2555912 | tf_op jit(solution)/shard_map/ppermute | solution.py:233
  95.1 7.5 %collective-permute-start.9 = (bf16[48,256]{1,0:T(8,128)(2,1)S(1)}, bf16[48,256]{1,0:T(8,128)(2,1)S(1)}, u32[]{:S(2)}, u32[]{:S(2)}) collective-permute-start(bf16[48,256]{1,0:T(8,128)(2,1)S(1)} %finish.1), channel_id=1, source_target_pairs={{0,592},{1,3},{2,206},{3,7},{4,208},{5,389},{6,211},{7,391},{8,593... | collective-permute-start | bytes 73736 | tf_op jit(solution)/shard_map/ppermute | solution.py:251

commit v7 on v6

--- a/solution.py
+++ b/solution.py
@@ -1,3 +1,5 @@
+import itertools
+
 import jax
 import jax.numpy as jnp
 from jax import lax
@@ -42,10 +44,15 @@
     return rows == lax.broadcasted_iota(jnp.int32, shape, 1)
 
 
+def own_kernel(place_ref, ratings_ref, own_ref, out_ref):
+    own_ref[...] = ratings_ref[...]
+    for i in range(place_ref.shape[0]):
+        out_ref[i] = place_ref[i]
+
+
 def sums_kernel(*refs):
-    panels, (sums_ref, own_ref) = refs[:-2], refs[-2:]
-    own_ref[...] = panels[0][...]
-    squares = jnp.zeros(own_ref.shape, jnp.float32)
+    panels, sums_ref = refs[:-1], refs[-1]
+    squares = jnp.zeros(panels[0].shape, jnp.float32)
     for ref in panels:
         values = ref[...].astype(jnp.float32)
         squares = squares + values * values
@@ -98,15 +105,21 @@
             lanes = total[:, half * LANES : (half + 1) * LANES]
             target[pl.ds(2 * at + half, 1), :] = lanes
 
-    for its_member, (first, columns) in enumerate(UNITS):
-
-        @pl.when(member == its_member)
-        def _():
-            row_panels = [panels[REACH + first + i] for i in range(MEMBERS)]
+    for its_core, its_member in itertools.product(range(CORES), range(MEMBERS)):
+        first, columns = UNITS[its_member]
+
+        def panel(offset, its_core=its_core):
+            if offset > REACH:
+                return panels[-1]
+            return panels[REACH - offset if its_core else REACH + offset]
+
+        @pl.when((core == its_core) & (member == its_member))
+        def _(first=first, columns=columns, panel=panel):
+            row_panels = [panel(first + i) for i in range(MEMBERS)]
             for i, ref in enumerate(row_panels):
                 keep_degree(row_ref, i, degree(ref)[1])
             for unit, offset in enumerate(columns):
-                weighted, total = degree(panels[REACH + offset])
+                weighted, total = degree(panel(offset))
                 keep_degree(column_ref, unit, total)
                 for i, ref in enumerate(row_panels):
                     gram_ref[pl.ds((3 * unit + i) * width, width), :] = lax.dot_general(
@@ -194,24 +207,41 @@
     def fetch(array, by, at=range(PANELS)):
         return lax.ppermute(array, "z", [((z + by) % PANELS, z) for z in at])
 
-    above, below = [ratings], [ratings]
-    for _ in range(REACH):
-        above.append(fetch(above[-1], 1))
-        below.append(fetch(below[-1], -1))
+    def relay(array, by):
+        pairs = []
+        for c in range(CORES):
+            shift = -by if c else by
+            pairs += [(c * PANELS + (z + shift) % PANELS, c * PANELS + z) for z in range(PANELS)]
+        return lax.ppermute(array, ("core", "z"), pairs)
+
+    first, second = [ratings], [ratings]
+    own, place = pl.pallas_call(
+        own_kernel,
+        out_shape=(
+            jax.ShapeDtypeStruct((rows, width), ratings.dtype),
+            jax.ShapeDtypeStruct(place.shape, jnp.int32),
+        ),
+        in_specs=[SMEM, VMEM],
+        out_specs=(VMEM, SMEM),
+        compiler_params=PARAMS,
+        name="own",
+    )(place, ratings)
+    for i in range(REACH):
+        first.append(relay(first[-1], 1))
+        second.append(relay(second[-1], -1))
+        if i == 0:
+            first[1], own, place = lax.optimization_barrier((first[1], own, place))
     last = fetch(ratings, REACH + 1, range(0, PANELS, MEMBERS))
-    near, own = pl.pallas_call(
+    near = pl.pallas_call(
         sums_kernel,
-        out_shape=(
-            jax.ShapeDtypeStruct((8, LANES), jnp.float32),
-            jax.ShapeDtypeStruct((rows, width), ratings.dtype),
-        ),
+        out_shape=jax.ShapeDtypeStruct((8, LANES), jnp.float32),
         in_specs=[VMEM] * 5,
-        out_specs=(VMEM, VMEM),
+        out_specs=VMEM,
         compiler_params=PARAMS,
         name="sums",
-    )(*above[:3], *below[1:3])
+    )(own, *first[1:3], *second[1:3])
     far = fetch(near, PANELS // 2)
-    panels = below[:0:-1] + [own] + above[1:] + [last]
+    panels = second[:0:-1] + [own] + first[1:] + [last]
 
     slots = (SLOTS, SLOT_ROWS, LANES)
     keep, send = pl.pallas_call(

time: 104 us -> 105 us (level)
  starting transfers between devices: 40.6 us -> 38.4 us
  waiting for transfers between devices: 22 us -> 23.9 us
  Pallas kernels: 3.58 us -> 4.71 us
    ppermute x8 -> x2, starting transfers between devices: 36.6 us -> 3.21 us  [fetch(): return lax.ppermute(array, 'z', [((z + by) % PANELS, z) for z in at])]
    ppermute x0 -> x6, starting transfers between devices: none -> 31.4 us  [relay(): return lax.ppermute(array, ('core', 'z'), pairs)]
    ppermute x0 -> x6, waiting for transfers between devices: none -> 6.05 us  [relay(): return lax.ppermute(array, ('core', 'z'), pairs)]
    ppermute x8 -> x2, waiting for transfers between devices: 14.2 us -> 9.88 us  [fetch(): return lax.ppermute(array, 'z', [((z + by) % PANELS, z) for z in at])]
    pallas_call x1 -> x2, Pallas kernels: 0.26 us -> 1.41 us  [the longest x1 1.14 us: per_device(): pl.pallas_call(own_kernel, out_shape=(jax.ShapeDtypeStruct((rows, width),...]
  transfers between devices with their start and end apart: 10 -> 10, of which waited for: 6 -> 5; matrix products, arithmetic and copies ran while one was open for 1% -> 1% of each run, Pallas kernels for 0% -> 1%
where the time goes in v7:
time: 105 us; the launch traced here: 104 us
  starting transfers between devices  38.4 us (37%)
  blocking collectives  34.7 us (33%)
  waiting for transfers between devices  23.9 us (23%)
  Pallas kernels  4.71 us (4%)
  local copies, waits for them, and re-layouts  2.27 us (2%)
    all_to_all x1, blocking collectives, per_device(): parts = lax.all_to_all(total, ('x', 'y'), 0, 0, tiled=True)  34.7 us
    ppermute x6, starting transfers between devices, relay(): return lax.ppermute(array, ('core', 'z'), pairs)  31.4 us
    ppermute x2, waiting for transfers between devices, fetch(): return lax.ppermute(array, 'z', [((z + by) % PANELS, z) for z in at])  9.88 us
    ppermute x6, waiting for transfers between devices, relay(): return lax.ppermute(array, ('core', 'z'), pairs)  6.05 us
    ppermute x1, waiting for transfers between devices, per_device(): return lax.ppermute(block, AXES, homes())  5.62 us
    ppermute x2, starting transfers between devices, fetch(): return lax.ppermute(array, 'z', [((z + by) % PANELS, z) for z in at])  3.21 us
    pallas_call x1, Pallas kernels, per_device(): pl.pallas_call(partial_kernel, out_shape=(jax.ShapeDtypeStruct(slots, jnp...  2.43 us
    ppermute x1, waiting for transfers between devices, per_device(): got = lax.ppermute(send, 'core', [(0, 1), (1, 0)])  2.34 us
  transfers between devices with their start and end apart: 10, of which 5 were waited for; matrix products, arithmetic and copies ran while one was open for 1% of the time, Pallas kernels for 1%

profile of v7, /device:TPU:8, one launch (start us, length us, event | category | flops | bytes accessed | tf_op | source)
XLA Modules:
  0.0 104.2 jit_solution(17719839905571977595)
XLA Ops:
  0.0 14.6 %collective-permute-start = (bf16[384,256]{1,0:T(8,128)(2,1)}, bf16[384,256]{1,0:T(8,128)(2,1)S(1)}, u32[]{:S(2)}, u32[]{:S(2)}) collective-permute-start(bf16[384,256]{1,0:T(8,128)(2,1)} %ratings_ref.1), channel_id=1, source_target_pairs={{1,0},{2,1},{3,2},{4,3},{5,4},{6,5},{7,6},{8,7},{9,8},{10,9},{11,1... | collective-permute-start | bytes 589832 | tf_op jit(solution)/shard_map/ppermute | solution.py:215
  14.6 1.9 %collective-permute-start.2 = (bf16[384,256]{1,0:T(8,128)(2,1)}, bf16[384,256]{1,0:T(8,128)(2,1)S(1)}, u32[]{:S(2)}, u32[]{:S(2)}) collective-permute-start(bf16[384,256]{1,0:T(8,128)(2,1)} %ratings_ref.1), channel_id=1, source_target_pairs={{11,0},{0,1},{1,2},{2,3},{3,4},{4,5},{5,6},{6,7},{7,8},{8,9},{9,10... | collective-permute-start | bytes 589832 | tf_op jit(solution)/shard_map/ppermute | solution.py:215
  16.5 0.7 concatenate.3.place_ref
  17.3 0.0 copy-start
  17.3 0.9 copy-done
  18.2 1.1 %own.1 = (bf16[384,256]{1,0:T(8,128)(2,1)S(1)}, s32[10]{0:T(128)S(1)}) custom-call(s32[10]{0:T(128)S(1)} %concatenate.3.place_ref, bf16[384,256]{1,0:T(8,128)(2,1)S(1)} %copy-done), custom_call_target="tpu_custom_call" | custom-call | tf_op jit(solution)/shard_map/own/pallas_call | solution.py:218
  19.3 0.1 collective-permute-done.refs_1_.refs_4_
  19.4 5.5 %collective-permute-start.1 = (bf16[384,256]{1,0:T(8,128)(2,1)S(1)}, bf16[384,256]{1,0:T(8,128)(2,1)S(1)}, u32[]{:S(2)}, u32[]{:S(2)}) collective-permute-start(bf16[384,256]{1,0:T(8,128)(2,1)S(1)} %collective-permute-done.refs_1_.refs_4_), channel_id=1, source_target_pairs={{1,0},{2,1},{3,2},{4,3},{5,4},{6,5},{7,6},{8,7},{9,8},{10,9},{11,1... | collective-permute-start | bytes 589832 | tf_op jit(solution)/shard_map/ppermute | solution.py:215
  24.9 0.0 collective-permute-done.2.refs_3_.refs_2_
  24.9 1.9 %collective-permute-start.3 = (bf16[384,256]{1,0:T(8,128)(2,1)S(1)}, bf16[384,256]{1,0:T(8,128)(2,1)S(1)}, u32[]{:S(2)}, u32[]{:S(2)}) collective-permute-start(bf16[384,256]{1,0:T(8,128)(2,1)S(1)} %collective-permute-done.2.refs_3_.refs_2_), channel_id=1, source_target_pairs={{11,0},{0,1},{1,2},{2,3},{3,4},{4,5},{5,6},{6,7},{7,8},{8,9},{9,10... | collective-permute-start | bytes 589832 | tf_op jit(solution)/shard_map/ppermute | solution.py:215
  26.8 1.3 %collective-permute-start.7 = (bf16[384,256]{1,0:T(8,128)(2,1)}, bf16[384,256]{1,0:T(8,128)(2,1)S(1)}, u32[]{:S(2)}, u32[]{:S(2)}) collective-permute-start(bf16[384,256]{1,0:T(8,128)(2,1)} %ratings_ref.1), channel_id=1, source_target_pairs={{4,0},{7,3},{10,6},{1,9},{16,12},{19,15},{22,18},{13,21},{28,24},{... | collective-permute-start | bytes 589832 | tf_op jit(solution)/shard_map/ppermute | solution.py:208
  28.1 6.0 %collective-permute-done.1.refs_2_.refs_5_ = bf16[384,256]{1,0:T(8,128)(2,1)S(1)} collective-permute-done((bf16[384,256]{1,0:T(8,128)(2,1)S(1)}, bf16[384,256]{1,0:T(8,128)(2,1)S(1)}, u32[]{:S(2)}, u32[]{:S(2)}) %collective-permute-start.1) | collective-permute-done | bytes 196640 | tf_op jit(solution)/shard_map/ppermute | solution.py:215
  34.1 5.6 %collective-permute-start.6 = (bf16[384,256]{1,0:T(8,128)(2,1)S(1)}, bf16[384,256]{1,0:T(8,128)(2,1)S(1)}, u32[]{:S(2)}, u32[]{:S(2)}) collective-permute-start(bf16[384,256]{1,0:T(8,128)(2,1)S(1)} %collective-permute-done.1.refs_2_.refs_5_), channel_id=1, source_target_pairs={{1,0},{2,1},{3,2},{4,3},{5,4},{6,5},{7,6},{8,7},{9,8},{10,9},{11,1... | collective-permute-start | bytes 589832 | tf_op jit(solution)/shard_map/ppermute | solution.py:215
  39.7 0.0 collective-permute-done.3.refs_4_.refs_1_
  39.7 1.9 %collective-permute-start.5 = (bf16[384,256]{1,0:T(8,128)(2,1)S(1)}, bf16[384,256]{1,0:T(8,128)(2,1)S(1)}, u32[]{:S(2)}, u32[]{:S(2)}) collective-permute-start(bf16[384,256]{1,0:T(8,128)(2,1)S(1)} %collective-permute-done.3.refs_4_.refs_1_), channel_id=1, source_target_pairs={{11,0},{0,1},{1,2},{2,3},{3,4},{4,5},{5,6},{6,7},{7,8},{8,9},{9,10... | collective-permute-start | bytes 589832 | tf_op jit(solution)/shard_map/ppermute | solution.py:215
  41.6 0.3 sums.1.near_ref
  41.9 1.9 %collective-permute-start.4 = (f32[8,128]{1,0:T(8,128)S(1)}, f32[8,128]{1,0:T(8,128)S(1)}, u32[]{:S(2)}, u32[]{:S(2)}) collective-permute-start(f32[8,128]{1,0:T(8,128)S(1)} %sums.1.near_ref), channel_id=1, source_target_pairs={{6,0},{7,1},{8,2},{9,3},{10,4},{11,5},{0,6},{1,7},{2,8},{3,9},{4,1... | collective-permute-start | bytes 12296 | tf_op jit(solution)/shard_map/ppermute | solution.py:208
  43.8 0.0 collective-permute-done.7.refs_7_
  43.8 9.9 %collective-permute-done.4.far_ref = f32[8,128]{1,0:T(8,128)S(1)} collective-permute-done((f32[8,128]{1,0:T(8,128)S(1)}, f32[8,128]{1,0:T(8,128)S(1)}, u32[]{:S(2)}, u32[]{:S(2)}) %collective-permute-start.4) | collective-permute-done | bytes 4128 | tf_op jit(solution)/shard_map/ppermute | solution.py:208
  53.7 0.0 collective-permute-done.6.refs_6_
  53.7 0.0 collective-permute-done.5.refs_0_
  53.7 2.4 %partial.1 = (f32[32,104,128]{2,1,0:T(8,128)S(1)}, bf16[32,104,128]{2,1,0:T(8,128)(2,1)S(1)}) custom-call(s32[10]{0:T(128)S(1)} %get-tuple-element.14.place_ref, f32[8,128]{1,0:T(8,128)S(1)} %sums.1.near_ref, f32[8,128]{1,0:T(8,128)S(1)} %collective-permute-done.4.far_ref, bf16[384,256]{1,0:T(8,128)(2,1)S(1)} %collective-permute-done.5.refs_0_, ...), custom_call_target="tpu_custom_call" | custom-call | tf_op jit(solution)/shard_map/partial/pallas_call | solution.py:247
  56.1 1.9 %collective-permute-start.8 = (bf16[32,104,128]{2,1,0:T(8,128)(2,1)S(1)}, bf16[32,104,128]{2,1,0:T(8,128)(2,1)S(1)}, u32[]{:S(2)}, u32[]{:S(2)}) collective-permute-start(bf16[32,104,128]{2,1,0:T(8,128)(2,1)S(1)} %get-tuple-element.18), channel_id=1, source_target_pairs={{0,12},{12,0},{1,13},{13,1},{2,14},{14,2},{3,15},{15,3},{4,16},{16... | collective-permute-start | bytes 2555912 | tf_op jit(solution)/shard_map/ppermute | solution.py:263
  58.1 2.3 %collective-permute-done.8.got_ref = bf16[32,104,128]{2,1,0:T(8,128)(2,1)S(1)} collective-permute-done((bf16[32,104,128]{2,1,0:T(8,128)(2,1)S(1)}, bf16[32,104,128]{2,1,0:T(8,128)(2,1)S(1)}, u32[]{:S(2)}, u32[]{:S(2)}) %collective-permute-start.8) | collective-permute-done | bytes 852000 | tf_op jit(solution)/shard_map/ppermute | solution.py:263
  60.4 0.2 add.1
  60.6 34.7 %all_to_all.5.got_ref = bf16[32,104,128]{2,1,0:T(8,128)(2,1)S(1)} all-to-all(bf16[32,104,128]{2,1,0:T(8,128)(2,1)S(1)} %add.1), channel_id=1, replica_groups=mesh['x'=4,'y'=8,'core'=2,'z'=12] {'x','y'}, dimensions={0} | all-to-all | bytes 1703936 | tf_op jit(solution)/shard_map/all_to_all | solution.py:272
  95.3 0.7 finish.1
  96.0 1.9 %collective-permute-start.9 = (bf16[48,256]{1,0:T(8,128)(2,1)S(1)}, bf16[48,256]{1,0:T(8,128)(2,1)S(1)}, u32[]{:S(2)}, u32[]{:S(2)}) collective-permute-start(bf16[48,256]{1,0:T(8,128)(2,1)S(1)} %finish.1), channel_id=1, source_target_pairs={{0,592},{1,3},{2,206},{3,7},{4,208},{5,389},{6,211},{7,391},{8,593... | collective-permute-start | bytes 73736 | tf_op jit(solution)/shard_map/ppermute | solution.py:281
  97.9 5.6 %collective-permute-done.9 = bf16[48,256]{1,0:T(8,128)(2,1)S(1)} collective-permute-done((bf16[48,256]{1,0:T(8,128)(2,1)S(1)}, bf16[48,256]{1,0:T(8,128)(2,1)S(1)}, u32[]{:S(2)}, u32[]{:S(2)}) %collective-permute-start.9) | collective-permute-done | bytes 24608 | tf_op jit(solution)/shard_map/ppermute | solution.py:281
  103.6 0.6 copy.4
Async XLA Ops:
  0.0 19.4 %collective-permute-start = (bf16[384,256]{1,0:T(8,128)(2,1)}, bf16[384,256]{1,0:T(8,128)(2,1)S(1)}, u32[]{:S(2)}, u32[]{:S(2)}) collective-permute-start(bf16[384,256]{1,0:T(8,128)(2,1)} %ratings_ref.1), channel_id=1, source_target_pairs={{1,0},{2,1},{3,2},{4,3},{5,4},{6,5},{7,6},{8,7},{9,8},{10,9},{11,1... | collective-permute-start | bytes 589832 | tf_op jit(solution)/shard_map/ppermute | solution.py:215
  14.6 10.3 %collective-permute-start.2 = (bf16[384,256]{1,0:T(8,128)(2,1)}, bf16[384,256]{1,0:T(8,128)(2,1)S(1)}, u32[]{:S(2)}, u32[]{:S(2)}) collective-permute-start(bf16[384,256]{1,0:T(8,128)(2,1)} %ratings_ref.1), channel_id=1, source_target_pairs={{11,0},{0,1},{1,2},{2,3},{3,4},{4,5},{5,6},{6,7},{7,8},{8,9},{9,10... | collective-permute-start | bytes 589832 | tf_op jit(solution)/shard_map/ppermute | solution.py:215
  17.3 0.9 copy-start
  19.4 14.7 %collective-permute-start.1 = (bf16[384,256]{1,0:T(8,128)(2,1)S(1)}, bf16[384,256]{1,0:T(8,128)(2,1)S(1)}, u32[]{:S(2)}, u32[]{:S(2)}) collective-permute-start(bf16[384,256]{1,0:T(8,128)(2,1)S(1)} %collective-permute-done.refs_1_.refs_4_), channel_id=1, source_target_pairs={{1,0},{2,1},{3,2},{4,3},{5,4},{6,5},{7,6},{8,7},{9,8},{10,9},{11,1... | collective-permute-start | bytes 589832 | tf_op jit(solution)/shard_map/ppermute | solution.py:215
  24.9 14.8 %collective-permute-start.3 = (bf16[384,256]{1,0:T(8,128)(2,1)S(1)}, bf16[384,256]{1,0:T(8,128)(2,1)S(1)}, u32[]{:S(2)}, u32[]{:S(2)}) collective-permute-start(bf16[384,256]{1,0:T(8,128)(2,1)S(1)} %collective-permute-done.2.refs_3_.refs_2_), channel_id=1, source_target_pairs={{11,0},{0,1},{1,2},{2,3},{3,4},{4,5},{5,6},{6,7},{7,8},{8,9},{9,10... | collective-permute-start | bytes 589832 | tf_op jit(solution)/shard_map/ppermute | solution.py:215
  26.8 17.0 %collective-permute-start.7 = (bf16[384,256]{1,0:T(8,128)(2,1)}, bf16[384,256]{1,0:T(8,128)(2,1)S(1)}, u32[]{:S(2)}, u32[]{:S(2)}) collective-permute-start(bf16[384,256]{1,0:T(8,128)(2,1)} %ratings_ref.1), channel_id=1, source_target_pairs={{4,0},{7,3},{10,6},{1,9},{16,12},{19,15},{22,18},{13,21},{28,24},{... | collective-permute-start | bytes 589832 | tf_op jit(solution)/shard_map/ppermute | solution.py:208
  34.1 19.6 %collective-permute-start.6 = (bf16[384,256]{1,0:T(8,128)(2,1)S(1)}, bf16[384,256]{1,0:T(8,128)(2,1)S(1)}, u32[]{:S(2)}, u32[]{:S(2)}) collective-permute-start(bf16[384,256]{1,0:T(8,128)(2,1)S(1)} %collective-permute-done.1.refs_2_.refs_5_), channel_id=1, source_target_pairs={{1,0},{2,1},{3,2},{4,3},{5,4},{6,5},{7,6},{8,7},{9,8},{10,9},{11,1... | collective-permute-start | bytes 589832 | tf_op jit(solution)/shard_map/ppermute | solution.py:215
  39.7 14.0 %collective-permute-start.5 = (bf16[384,256]{1,0:T(8,128)(2,1)S(1)}, bf16[384,256]{1,0:T(8,128)(2,1)S(1)}, u32[]{:S(2)}, u32[]{:S(2)}) collective-permute-start(bf16[384,256]{1,0:T(8,128)(2,1)S(1)} %collective-permute-done.3.refs_4_.refs_1_), channel_id=1, source_target_pairs={{11,0},{0,1},{1,2},{2,3},{3,4},{4,5},{5,6},{6,7},{7,8},{8,9},{9,10... | collective-permute-start | bytes 589832 | tf_op jit(solution)/shard_map/ppermute | solution.py:215
  41.9 11.8 %collective-permute-start.4 = (f32[8,128]{1,0:T(8,128)S(1)}, f32[8,128]{1,0:T(8,128)S(1)}, u32[]{:S(2)}, u32[]{:S(2)}) collective-permute-start(f32[8,128]{1,0:T(8,128)S(1)} %sums.1.near_ref), channel_id=1, source_target_pairs={{6,0},{7,1},{8,2},{9,3},{10,4},{11,5},{0,6},{1,7},{2,8},{3,9},{4,1... | collective-permute-start | bytes 12296 | tf_op jit(solution)/shard_map/ppermute | solution.py:208
  56.1 4.3 %collective-permute-start.8 = (bf16[32,104,128]{2,1,0:T(8,128)(2,1)S(1)}, bf16[32,104,128]{2,1,0:T(8,128)(2,1)S(1)}, u32[]{:S(2)}, u32[]{:S(2)}) collective-permute-start(bf16[32,104,128]{2,1,0:T(8,128)(2,1)S(1)} %get-tuple-element.18), channel_id=1, source_target_pairs={{0,12},{12,0},{1,13},{13,1},{2,14},{14,2},{3,15},{15,3},{4,16},{16... | collective-permute-start | bytes 2555912 | tf_op jit(solution)/shard_map/ppermute | solution.py:263
  96.0 7.5 %collective-permute-start.9 = (bf16[48,256]{1,0:T(8,128)(2,1)S(1)}, bf16[48,256]{1,0:T(8,128)(2,1)S(1)}, u32[]{:S(2)}, u32[]{:S(2)}) collective-permute-start(bf16[48,256]{1,0:T(8,128)(2,1)S(1)} %finish.1), channel_id=1, source_target_pairs={{0,592},{1,3},{2,206},{3,7},{4,208},{5,389},{6,211},{7,391},{8,593... | collective-permute-start | bytes 73736 | tf_op jit(solution)/shard_map/ppermute | solution.py:281

commit v8 on v1

v8 whole, which is shorter than its diff:
```python
import jax
import jax.numpy as jnp
from jax import lax
from jax.experimental import pallas as pl
from jax.experimental.pallas import tpu as pltpu
from jax.sharding import Mesh, PartitionSpec as P

X, Y, CORES, PANELS = 4, 8, 2, 12
SLOTS = X * Y
BLOCK = 64
ITEMS = 3072
SHARE = 48
LANES = 128
SLOT_ROWS = 2 * SHARE + 8
AXES = ("x", "y", "core", "triple", "member")
COUNTS = 4
AXES = ("x", "y", "core", "z")
UP, DOWN = 6, 5


def split_rows(total):
    high = total.astype(jnp.bfloat16).astype(jnp.float32)
    first = lax.broadcasted_iota(jnp.int32, total.shape, 0) < 4
    return jnp.where(first, high, total - high)


def join_rows(extra):
    return extra + pltpu.roll(extra, 4, 0)


def partial_kernel(place_ref, *refs):
    panels, (keep_ref, send_ref, gram_ref, degree_ref) = refs[:PANELS], refs[PANELS:]
    core, me = place_ref[2], place_ref[3]
    rows, width = panels[0].shape
    squares = jnp.zeros((rows, width), jnp.float32)
    for panel in panels:
        values = panel[...].astype(jnp.float32)
        squares = squares + values * values
    square_sum = jnp.sum(squares, axis=1, keepdims=True)
    position = lax.broadcasted_iota(jnp.int32, (BLOCK, 1), 0)
    live = jnp.concatenate(
        [
            (position < place_ref[COUNTS + i]).astype(jnp.float32)
            for i in range(rows // BLOCK)
        ],
        axis=0,
    )
    scale = live / jnp.sqrt(square_sum / ITEMS + 1e-05)
    column = (scale * panels[0][...].astype(jnp.float32)).astype(jnp.bfloat16)
    hops = list(range(UP + 1)) + list(range(-1, -DOWN - 1, -1))
    for panel, hop in zip(panels, hops):
        owner = lax.rem(me + PANELS + jnp.where(core == 0, hop, -hop), PANELS)
        gram_ref[pl.ds(pl.multiple_of(owner * width, width), width), :] = lax.dot_general(
            panel[...], column, (((0,), (0,)), ((), ())), preferred_element_type=jnp.float32
        )
        values = panel[...].astype(jnp.float32)
        weighted = (scale * values).astype(jnp.bfloat16).astype(jnp.float32)
        degree = jnp.sum(values * weighted, axis=0, keepdims=True)
        for half in range(2):
            lanes = degree[:, half * LANES : (half + 1) * LANES]
            degree_ref[pl.ds(2 * owner + half, 1), :] = lanes

    for slot in range(SLOTS):
        for mine in (True, False):
            start = (2 * slot + (core if mine else 1 - core)) * SHARE
            low = lax.shift_right_logical(start, 7)
            high = lax.shift_right_logical(start + SHARE - 1, 7)
            four = [degree_ref[pl.ds(i, 1), :] for i in (2 * me, 2 * me + 1, low, high)]
            extra = split_rows(jnp.concatenate(four + four, axis=0))
            block = gram_ref[pl.ds(pl.multiple_of(start, 16), SHARE), :]
            whole = jnp.concatenate([block[:, :LANES], block[:, LANES:], extra], axis=0)
            ref = keep_ref if mine else send_ref
            ref[slot] = whole.astype(ref.dtype)


def add_kernel(keep_ref, got_ref, out_ref):
    for slot in range(SLOTS):
        total = keep_ref[slot] + got_ref[slot].astype(jnp.float32)
        extra = split_rows(join_rows(total[2 * SHARE :]))
        out_ref[slot] = jnp.concatenate([total[: 2 * SHARE], extra], axis=0).astype(
            jnp.bfloat16
        )


def finish_kernel(place_ref, got_ref, out_ref):
    user = (place_ref[0] * Y + place_ref[1]) * CORES + place_ref[2]
    offset = lax.rem(user * SHARE, LANES)
    total = got_ref[0].astype(jnp.float32)
    for slot in range(1, SLOTS):
        total = total + got_ref[slot].astype(jnp.float32)
    extra = join_rows(total[2 * SHARE :])
    lane = lax.broadcasted_iota(jnp.int32, (SHARE, LANES), 1)
    row = lax.broadcasted_iota(jnp.int32, (SHARE, LANES), 0) + offset
    row_degree = jnp.sum(
        jnp.where(lane == row, extra[2:3], 0.0) + jnp.where(lane + LANES == row, extra[3:4], 0.0),
        axis=1,
        keepdims=True,
    )
    row_inverse = 1.0 / jnp.sqrt(row_degree)
    for half in range(2):
        block = total[half * SHARE : (half + 1) * SHARE]
        column_inverse = 1.0 / jnp.sqrt(extra[half : half + 1])
        out_ref[:, half * LANES : (half + 1) * LANES] = (
            block * row_inverse * column_inverse
        ).astype(jnp.bfloat16)


VMEM = pl.BlockSpec(memory_space=pltpu.VMEM)
SMEM = pl.BlockSpec(memory_space=pltpu.SMEM)
PARAMS = pltpu.CompilerParams(vmem_limit_bytes=48 * 1024 * 1024)


def per_device(ratings, counts):
    rows, width = ratings.shape
    x, y, core, me = (lax.axis_index(name) for name in AXES)
    place = jnp.concatenate([jnp.stack([x, y, core, me]).astype(jnp.int32), counts])

    def relay(array, by):
        pairs = []
        for c in range(CORES):
            shift = -by if c else by
            pairs += [(c * PANELS + (z + shift) % PANELS, c * PANELS + z) for z in range(PANELS)]
        return lax.ppermute(array, ("core", "z"), pairs)

    first, second = [ratings], [ratings]
    for hop in range(UP):
        first.append(relay(first[-1], 1))
        if hop < DOWN:
            second.append(relay(second[-1], -1))
    panels = first + second[1:]

    slots = (SLOTS, SLOT_ROWS, LANES)
    keep, send = pl.pallas_call(
        partial_kernel,
        out_shape=(
            jax.ShapeDtypeStruct(slots, jnp.float32),
            jax.ShapeDtypeStruct(slots, jnp.bfloat16),
        ),
        in_specs=[SMEM] + [VMEM] * PANELS,
        out_specs=(VMEM, VMEM),
        scratch_shapes=[
            pltpu.VMEM((ITEMS, width), jnp.float32),
            pltpu.VMEM((ITEMS // LANES, LANES), jnp.float32),
        ],
        compiler_params=PARAMS,
        name="partial",
    )(place, *panels)
    got = lax.ppermute(send, "core", [(0, 1), (1, 0)])
    total = pl.pallas_call(
        add_kernel,
        out_shape=jax.ShapeDtypeStruct(slots, jnp.bfloat16),
        in_specs=[VMEM, VMEM],
        out_specs=VMEM,
        compiler_params=PARAMS,
        name="add",
    )(keep, got)
    parts = lax.all_to_all(total, ("x", "y"), 0, 0, tiled=True)
    return pl.pallas_call(
        finish_kernel,
        out_shape=jax.ShapeDtypeStruct((SHARE, width), jnp.bfloat16),
        in_specs=[SMEM, VMEM],
        out_specs=VMEM,
        compiler_params=PARAMS,
        name="finish",
    )(place, parts)


def solution(mesh):
    fine = Mesh(mesh.devices.reshape(X, Y, CORES, PANELS), AXES)
    users = AXES[:3]
    return jax.shard_map(
        per_device,
        mesh=fine,
        in_specs=(P(users, "z"), P(users)),
        out_specs=P(users, "z"),
        check_vma=False,
    )
```

time: 112 us -> 111 us (level)
  starting transfers between devices: 48.5 us -> 53.9 us
  waiting for transfers between devices: 19.6 us -> 15.3 us
  blocking collectives: 36.1 us -> 34.7 us
    ppermute x11, starting transfers between devices: 46.6 us -> 52 us  [relay(): return lax.ppermute(array, ('core', 'z'), pairs)]
    ppermute x11, waiting for transfers between devices: 17.1 us -> 13 us  [relay(): return lax.ppermute(array, ('core', 'z'), pairs)]
    all_to_all x1, blocking collectives: 36.1 us -> 34.7 us  [per_device(): parts = lax.all_to_all(total, ('x', 'y'), 0, 0, tiled=True)]
  transfers between devices with their start and end apart: 12 -> 12, of which waited for: 7 -> 7; matrix products, arithmetic and copies ran while one was open for 0% -> 1% of each run, Pallas kernels for 0% -> 0%
where the time goes in v8:
time: 111 us
  starting transfers between devices  53.9 us (49%)
  blocking collectives  34.7 us (31%)
  waiting for transfers between devices  15.3 us (14%)
  Pallas kernels  4.97 us (4%)
  local copies, waits for them, and re-layouts  1.66 us (1%)
    ppermute x11, starting transfers between devices, relay(): return lax.ppermute(array, ('core', 'z'), pairs)  52 us
    all_to_all x1, blocking collectives, per_device(): parts = lax.all_to_all(total, ('x', 'y'), 0, 0, tiled=True)  34.7 us
    ppermute x11, waiting for transfers between devices, relay(): return lax.ppermute(array, ('core', 'z'), pairs)  13 us
    pallas_call x1, Pallas kernels, per_device(): pl.pallas_call(partial_kernel, out_shape=(jax.ShapeDtypeStruct(slots, jnp...  3.46 us
    ppermute x1, waiting for transfers between devices, per_device(): got = lax.ppermute(send, 'core', [(0, 1), (1, 0)])  2.34 us
  transfers between devices with their start and end apart: 12, of which 7 were waited for; matrix products, arithmetic and copies ran while one was open for 1% of the time, Pallas kernels for 0%

profile of v8, /device:TPU:8, one launch (start us, length us, event | category | flops | bytes accessed | tf_op | source)
XLA Modules:
  0.0 110.8 jit_solution(6064977668356825477)
XLA Ops:
  0.0 14.6 %collective-permute-start = (bf16[384,256]{1,0:T(8,128)(2,1)}, bf16[384,256]{1,0:T(8,128)(2,1)S(1)}, u32[]{:S(2)}, u32[]{:S(2)}) collective-permute-start(bf16[384,256]{1,0:T(8,128)(2,1)} %refs_0_.1), channel_id=1, source_target_pairs={{1,0},{2,1},{3,2},{4,3},{5,4},{6,5},{7,6},{8,7},{9,8},{10,9},{11,1... | collective-permute-start | bytes 589832 | tf_op jit(solution)/shard_map/ppermute | solution.py:123
  14.6 1.9 %collective-permute-start.6 = (bf16[384,256]{1,0:T(8,128)(2,1)}, bf16[384,256]{1,0:T(8,128)(2,1)S(1)}, u32[]{:S(2)}, u32[]{:S(2)}) collective-permute-start(bf16[384,256]{1,0:T(8,128)(2,1)} %refs_0_.1), channel_id=1, source_target_pairs={{11,0},{0,1},{1,2},{2,3},{3,4},{4,5},{5,6},{6,7},{7,8},{8,9},{9,10... | collective-permute-start | bytes 589832 | tf_op jit(solution)/shard_map/ppermute | solution.py:123
  16.5 2.9 %collective-permute-done.refs_1_ = bf16[384,256]{1,0:T(8,128)(2,1)S(1)} collective-permute-done((bf16[384,256]{1,0:T(8,128)(2,1)}, bf16[384,256]{1,0:T(8,128)(2,1)S(1)}, u32[]{:S(2)}, u32[]{:S(2)}) %collective-permute-start) | collective-permute-done | bytes 196640 | tf_op jit(solution)/shard_map/ppermute | solution.py:123
  19.4 5.5 %collective-permute-start.1 = (bf16[384,256]{1,0:T(8,128)(2,1)S(1)}, bf16[384,256]{1,0:T(8,128)(2,1)S(1)}, u32[]{:S(2)}, u32[]{:S(2)}) collective-permute-start(bf16[384,256]{1,0:T(8,128)(2,1)S(1)} %collective-permute-done.refs_1_), channel_id=1, source_target_pairs={{1,0},{2,1},{3,2},{4,3},{5,4},{6,5},{7,6},{8,7},{9,8},{10,9},{11,1... | collective-permute-start | bytes 589832 | tf_op jit(solution)/shard_map/ppermute | solution.py:123
  24.9 0.0 collective-permute-done.6.refs_7_
  24.9 1.9 %collective-permute-start.7 = (bf16[384,256]{1,0:T(8,128)(2,1)S(1)}, bf16[384,256]{1,0:T(8,128)(2,1)S(1)}, u32[]{:S(2)}, u32[]{:S(2)}) collective-permute-start(bf16[384,256]{1,0:T(8,128)(2,1)S(1)} %collective-permute-done.6.refs_7_), channel_id=1, source_target_pairs={{11,0},{0,1},{1,2},{2,3},{3,4},{4,5},{5,6},{6,7},{7,8},{8,9},{9,10... | collective-permute-start | bytes 589832 | tf_op jit(solution)/shard_map/ppermute | solution.py:123
  26.8 2.9 %collective-permute-done.1.refs_2_ = bf16[384,256]{1,0:T(8,128)(2,1)S(1)} collective-permute-done((bf16[384,256]{1,0:T(8,128)(2,1)S(1)}, bf16[384,256]{1,0:T(8,128)(2,1)S(1)}, u32[]{:S(2)}, u32[]{:S(2)}) %collective-permute-start.1) | collective-permute-done | bytes 196640 | tf_op jit(solution)/shard_map/ppermute | solution.py:123
  29.8 5.6 %collective-permute-start.2 = (bf16[384,256]{1,0:T(8,128)(2,1)S(1)}, bf16[384,256]{1,0:T(8,128)(2,1)S(1)}, u32[]{:S(2)}, u32[]{:S(2)}) collective-permute-start(bf16[384,256]{1,0:T(8,128)(2,1)S(1)} %collective-permute-done.1.refs_2_), channel_id=1, source_target_pairs={{1,0},{2,1},{3,2},{4,3},{5,4},{6,5},{7,6},{8,7},{9,8},{10,9},{11,1... | collective-permute-start | bytes 589832 | tf_op jit(solution)/shard_map/ppermute | solution.py:123
  35.4 0.0 collective-permute-done.7.refs_8_
  35.4 1.9 %collective-permute-start.8 = (bf16[384,256]{1,0:T(8,128)(2,1)S(1)}, bf16[384,256]{1,0:T(8,128)(2,1)S(1)}, u32[]{:S(2)}, u32[]{:S(2)}) collective-permute-start(bf16[384,256]{1,0:T(8,128)(2,1)S(1)} %collective-permute-done.7.refs_8_), channel_id=1, source_target_pairs={{11,0},{0,1},{1,2},{2,3},{3,4},{4,5},{5,6},{6,7},{7,8},{8,9},{9,10... | collective-permute-start | bytes 589832 | tf_op jit(solution)/shard_map/ppermute | solution.py:123
  37.3 2.2 %collective-permute-done.2.refs_3_ = bf16[384,256]{1,0:T(8,128)(2,1)S(1)} collective-permute-done((bf16[384,256]{1,0:T(8,128)(2,1)S(1)}, bf16[384,256]{1,0:T(8,128)(2,1)S(1)}, u32[]{:S(2)}, u32[]{:S(2)}) %collective-permute-start.2) | collective-permute-done | bytes 196640 | tf_op jit(solution)/shard_map/ppermute | solution.py:123
  39.5 5.6 %collective-permute-start.3 = (bf16[384,256]{1,0:T(8,128)(2,1)S(1)}, bf16[384,256]{1,0:T(8,128)(2,1)S(1)}, u32[]{:S(2)}, u32[]{:S(2)}) collective-permute-start(bf16[384,256]{1,0:T(8,128)(2,1)S(1)} %collective-permute-done.2.refs_3_), channel_id=1, source_target_pairs={{1,0},{2,1},{3,2},{4,3},{5,4},{6,5},{7,6},{8,7},{9,8},{10,9},{11,1... | collective-permute-start | bytes 589832 | tf_op jit(solution)/shard_map/ppermute | solution.py:123
  45.1 0.0 collective-permute-done.8.refs_9_
  45.1 1.9 %collective-permute-start.9 = (bf16[384,256]{1,0:T(8,128)(2,1)S(1)}, bf16[384,256]{1,0:T(8,128)(2,1)S(1)}, u32[]{:S(2)}, u32[]{:S(2)}) collective-permute-start(bf16[384,256]{1,0:T(8,128)(2,1)S(1)} %collective-permute-done.8.refs_9_), channel_id=1, source_target_pairs={{11,0},{0,1},{1,2},{2,3},{3,4},{4,5},{5,6},{6,7},{7,8},{8,9},{9,10... | collective-permute-start | bytes 589832 | tf_op jit(solution)/shard_map/ppermute | solution.py:123
  47.0 1.3 %collective-permute-done.3.refs_4_ = bf16[384,256]{1,0:T(8,128)(2,1)S(1)} collective-permute-done((bf16[384,256]{1,0:T(8,128)(2,1)S(1)}, bf16[384,256]{1,0:T(8,128)(2,1)S(1)}, u32[]{:S(2)}, u32[]{:S(2)}) %collective-permute-start.3) | collective-permute-done | bytes 196640 | tf_op jit(solution)/shard_map/ppermute | solution.py:123
  48.3 5.6 %collective-permute-start.4 = (bf16[384,256]{1,0:T(8,128)(2,1)S(1)}, bf16[384,256]{1,0:T(8,128)(2,1)S(1)}, u32[]{:S(2)}, u32[]{:S(2)}) collective-permute-start(bf16[384,256]{1,0:T(8,128)(2,1)S(1)} %collective-permute-done.3.refs_4_), channel_id=1, source_target_pairs={{1,0},{2,1},{3,2},{4,3},{5,4},{6,5},{7,6},{8,7},{9,8},{10,9},{11,1... | collective-permute-start | bytes 589832 | tf_op jit(solution)/shard_map/ppermute | solution.py:123
  53.9 0.0 collective-permute-done.9.refs_10_
  53.9 1.9 %collective-permute-start.10 = (bf16[384,256]{1,0:T(8,128)(2,1)S(1)}, bf16[384,256]{1,0:T(8,128)(2,1)S(1)}, u32[]{:S(2)}, u32[]{:S(2)}) collective-permute-start(bf16[384,256]{1,0:T(8,128)(2,1)S(1)} %collective-permute-done.9.refs_10_), channel_id=1, source_target_pairs={{11,0},{0,1},{1,2},{2,3},{3,4},{4,5},{5,6},{6,7},{7,8},{8,9},{9,10... | collective-permute-start | bytes 589832 | tf_op jit(solution)/shard_map/ppermute | solution.py:123
  55.9 1.2 %collective-permute-done.4.refs_5_ = bf16[384,256]{1,0:T(8,128)(2,1)S(1)} collective-permute-done((bf16[384,256]{1,0:T(8,128)(2,1)S(1)}, bf16[384,256]{1,0:T(8,128)(2,1)S(1)}, u32[]{:S(2)}, u32[]{:S(2)}) %collective-permute-start.4) | collective-permute-done | bytes 196640 | tf_op jit(solution)/shard_map/ppermute | solution.py:123
  57.1 5.6 %collective-permute-start.5 = (bf16[384,256]{1,0:T(8,128)(2,1)S(1)}, bf16[384,256]{1,0:T(8,128)(2,1)S(1)}, u32[]{:S(2)}, u32[]{:S(2)}) collective-permute-start(bf16[384,256]{1,0:T(8,128)(2,1)S(1)} %collective-permute-done.4.refs_5_), channel_id=1, source_target_pairs={{1,0},{2,1},{3,2},{4,3},{5,4},{6,5},{7,6},{8,7},{9,8},{10,9},{11,1... | collective-permute-start | bytes 589832 | tf_op jit(solution)/shard_map/ppermute | solution.py:123
  62.7 0.7 concatenate.3.place_ref
  63.4 0.0 collective-permute-done.10.refs_11_
  63.5 2.4 %collective-permute-done.5.refs_6_ = bf16[384,256]{1,0:T(8,128)(2,1)S(1)} collective-permute-done((bf16[384,256]{1,0:T(8,128)(2,1)S(1)}, bf16[384,256]{1,0:T(8,128)(2,1)S(1)}, u32[]{:S(2)}, u32[]{:S(2)}) %collective-permute-start.5) | collective-permute-done | bytes 196640 | tf_op jit(solution)/shard_map/ppermute | solution.py:123
  65.9 0.0 copy-start
  65.9 0.9 copy-done
  66.8 3.5 %partial.1 = (f32[32,104,128]{2,1,0:T(8,128)S(1)}, bf16[32,104,128]{2,1,0:T(8,128)(2,1)S(1)}) custom-call(s32[10]{0:T(128)S(1)} %concatenate.3.place_ref, bf16[384,256]{1,0:T(8,128)(2,1)S(1)} %copy-done, bf16[384,256]{1,0:T(8,128)(2,1)S(1)} %collective-permute-done.refs_1_, bf16[384,256]{1,0:T(8,128)(2,1)S(1)} %collective-permute-done.1.refs_2_, ...), custom_call_target="tpu_custom_call" | custom-call | tf_op jit(solution)/shard_map/partial/pallas_call | solution.py:133
  70.3 1.9 %collective-permute-start.11 = (bf16[32,104,128]{2,1,0:T(8,128)(2,1)S(1)}, bf16[32,104,128]{2,1,0:T(8,128)(2,1)S(1)}, u32[]{:S(2)}, u32[]{:S(2)}) collective-permute-start(bf16[32,104,128]{2,1,0:T(8,128)(2,1)S(1)} %get-tuple-element.8), channel_id=1, source_target_pairs={{0,12},{12,0},{1,13},{13,1},{2,14},{14,2},{3,15},{15,3},{4,16},{16... | collective-permute-start | bytes 2555912 | tf_op jit(solution)/shard_map/ppermute | solution.py:148
  72.2 2.3 %collective-permute-done.11.got_ref = bf16[32,104,128]{2,1,0:T(8,128)(2,1)S(1)} collective-permute-done((bf16[32,104,128]{2,1,0:T(8,128)(2,1)S(1)}, bf16[32,104,128]{2,1,0:T(8,128)(2,1)S(1)}, u32[]{:S(2)}, u32[]{:S(2)}) %collective-permute-start.11) | collective-permute-done | bytes 852000 | tf_op jit(solution)/shard_map/ppermute | solution.py:148
  74.5 0.2 add.1
  74.7 34.7 %all_to_all.5.got_ref = bf16[32,104,128]{2,1,0:T(8,128)(2,1)S(1)} all-to-all(bf16[32,104,128]{2,1,0:T(8,128)(2,1)S(1)} %add.1), channel_id=1, replica_groups=mesh['x'=4,'y'=8,'core'=2,'z'=12] {'x','y'}, dimensions={0} | all-to-all | bytes 1703936 | tf_op jit(solution)/shard_map/all_to_all | solution.py:157
  109.5 1.3 %finish.1 = bf16[48,256]{1,0:T(8,128)(2,1)} custom-call(s32[10]{0:T(128)S(1)} %concatenate.3.place_ref, bf16[32,104,128]{2,1,0:T(8,128)(2,1)S(1)} %all_to_all.5.got_ref), custom_call_target="tpu_custom_call" | custom-call | tf_op jit(solution)/shard_map/finish/pallas_call | solution.py:158
Async XLA Ops:
  0.0 19.4 %collective-permute-start = (bf16[384,256]{1,0:T(8,128)(2,1)}, bf16[384,256]{1,0:T(8,128)(2,1)S(1)}, u32[]{:S(2)}, u32[]{:S(2)}) collective-permute-start(bf16[384,256]{1,0:T(8,128)(2,1)} %refs_0_.1), channel_id=1, source_target_pairs={{1,0},{2,1},{3,2},{4,3},{5,4},{6,5},{7,6},{8,7},{9,8},{10,9},{11,1... | collective-permute-start | bytes 589832 | tf_op jit(solution)/shard_map/ppermute | solution.py:123
  14.6 10.3 %collective-permute-start.6 = (bf16[384,256]{1,0:T(8,128)(2,1)}, bf16[384,256]{1,0:T(8,128)(2,1)S(1)}, u32[]{:S(2)}, u32[]{:S(2)}) collective-permute-start(bf16[384,256]{1,0:T(8,128)(2,1)} %refs_0_.1), channel_id=1, source_target_pairs={{11,0},{0,1},{1,2},{2,3},{3,4},{4,5},{5,6},{6,7},{7,8},{8,9},{9,10... | collective-permute-start | bytes 589832 | tf_op jit(solution)/shard_map/ppermute | solution.py:123
  19.4 10.4 %collective-permute-start.1 = (bf16[384,256]{1,0:T(8,128)(2,1)S(1)}, bf16[384,256]{1,0:T(8,128)(2,1)S(1)}, u32[]{:S(2)}, u32[]{:S(2)}) collective-permute-start(bf16[384,256]{1,0:T(8,128)(2,1)S(1)} %collective-permute-done.refs_1_), channel_id=1, source_target_pairs={{1,0},{2,1},{3,2},{4,3},{5,4},{6,5},{7,6},{8,7},{9,8},{10,9},{11,1... | collective-permute-start | bytes 589832 | tf_op jit(solution)/shard_map/ppermute | solution.py:123
  24.9 10.5 %collective-permute-start.7 = (bf16[384,256]{1,0:T(8,128)(2,1)S(1)}, bf16[384,256]{1,0:T(8,128)(2,1)S(1)}, u32[]{:S(2)}, u32[]{:S(2)}) collective-permute-start(bf16[384,256]{1,0:T(8,128)(2,1)S(1)} %collective-permute-done.6.refs_7_), channel_id=1, source_target_pairs={{11,0},{0,1},{1,2},{2,3},{3,4},{4,5},{5,6},{6,7},{7,8},{8,9},{9,10... | collective-permute-start | bytes 589832 | tf_op jit(solution)/shard_map/ppermute | solution.py:123
  29.8 9.7 %collective-permute-start.2 = (bf16[384,256]{1,0:T(8,128)(2,1)S(1)}, bf16[384,256]{1,0:T(8,128)(2,1)S(1)}, u32[]{:S(2)}, u32[]{:S(2)}) collective-permute-start(bf16[384,256]{1,0:T(8,128)(2,1)S(1)} %collective-permute-done.1.refs_2_), channel_id=1, source_target_pairs={{1,0},{2,1},{3,2},{4,3},{5,4},{6,5},{7,6},{8,7},{9,8},{10,9},{11,1... | collective-permute-start | bytes 589832 | tf_op jit(solution)/shard_map/ppermute | solution.py:123
  35.4 9.7 %collective-permute-start.8 = (bf16[384,256]{1,0:T(8,128)(2,1)S(1)}, bf16[384,256]{1,0:T(8,128)(2,1)S(1)}, u32[]{:S(2)}, u32[]{:S(2)}) collective-permute-start(bf16[384,256]{1,0:T(8,128)(2,1)S(1)} %collective-permute-done.7.refs_8_), channel_id=1, source_target_pairs={{11,0},{0,1},{1,2},{2,3},{3,4},{4,5},{5,6},{6,7},{7,8},{8,9},{9,10... | collective-permute-start | bytes 589832 | tf_op jit(solution)/shard_map/ppermute | solution.py:123
  39.5 8.8 %collective-permute-start.3 = (bf16[384,256]{1,0:T(8,128)(2,1)S(1)}, bf16[384,256]{1,0:T(8,128)(2,1)S(1)}, u32[]{:S(2)}, u32[]{:S(2)}) collective-permute-start(bf16[384,256]{1,0:T(8,128)(2,1)S(1)} %collective-permute-done.2.refs_3_), channel_id=1, source_target_pairs={{1,0},{2,1},{3,2},{4,3},{5,4},{6,5},{7,6},{8,7},{9,8},{10,9},{11,1... | collective-permute-start | bytes 589832 | tf_op jit(solution)/shard_map/ppermute | solution.py:123
  45.1 8.8 %collective-permute-start.9 = (bf16[384,256]{1,0:T(8,128)(2,1)S(1)}, bf16[384,256]{1,0:T(8,128)(2,1)S(1)}, u32[]{:S(2)}, u32[]{:S(2)}) collective-permute-start(bf16[384,256]{1,0:T(8,128)(2,1)S(1)} %collective-permute-done.8.refs_9_), channel_id=1, source_target_pairs={{11,0},{0,1},{1,2},{2,3},{3,4},{4,5},{5,6},{6,7},{7,8},{8,9},{9,10... | collective-permute-start | bytes 589832 | tf_op jit(solution)/shard_map/ppermute | solution.py:123
  48.3 8.8 %collective-permute-start.4 = (bf16[384,256]{1,0:T(8,128)(2,1)S(1)}, bf16[384,256]{1,0:T(8,128)(2,1)S(1)}, u32[]{:S(2)}, u32[]{:S(2)}) collective-permute-start(bf16[384,256]{1,0:T(8,128)(2,1)S(1)} %collective-permute-done.3.refs_4_), channel_id=1, source_target_pairs={{1,0},{2,1},{3,2},{4,3},{5,4},{6,5},{7,6},{8,7},{9,8},{10,9},{11,1... | collective-permute-start | bytes 589832 | tf_op jit(solution)/shard_map/ppermute | solution.py:123
  53.9 9.5 %collective-permute-start.10 = (bf16[384,256]{1,0:T(8,128)(2,1)S(1)}, bf16[384,256]{1,0:T(8,128)(2,1)S(1)}, u32[]{:S(2)}, u32[]{:S(2)}) collective-permute-start(bf16[384,256]{1,0:T(8,128)(2,1)S(1)} %collective-permute-done.9.refs_10_), channel_id=1, source_target_pairs={{11,0},{0,1},{1,2},{2,3},{3,4},{4,5},{5,6},{6,7},{7,8},{8,9},{9,10... | collective-permute-start | bytes 589832 | tf_op jit(solution)/shard_map/ppermute | solution.py:123
  57.1 8.8 %collective-permute-start.5 = (bf16[384,256]{1,0:T(8,128)(2,1)S(1)}, bf16[384,256]{1,0:T(8,128)(2,1)S(1)}, u32[]{:S(2)}, u32[]{:S(2)}) collective-permute-start(bf16[384,256]{1,0:T(8,128)(2,1)S(1)} %collective-permute-done.4.refs_5_), channel_id=1, source_target_pairs={{1,0},{2,1},{3,2},{4,3},{5,4},{6,5},{7,6},{8,7},{9,8},{10,9},{11,1... | collective-permute-start | bytes 589832 | tf_op jit(solution)/shard_map/ppermute | solution.py:123
  65.9 0.9 copy-start
  70.3 4.3 %collective-permute-start.11 = (bf16[32,104,128]{2,1,0:T(8,128)(2,1)S(1)}, bf16[32,104,128]{2,1,0:T(8,128)(2,1)S(1)}, u32[]{:S(2)}, u32[]{:S(2)}) collective-permute-start(bf16[32,104,128]{2,1,0:T(8,128)(2,1)S(1)} %get-tuple-element.8), channel_id=1, source_target_pairs={{0,12},{12,0},{1,13},{13,1},{2,14},{14,2},{3,15},{15,3},{4,16},{16... | collective-permute-start | bytes 2555912 | tf_op jit(solution)/shard_map/ppermute | solution.py:148

commit v9 on v5

--- a/solution.py
+++ b/solution.py
@@ -13,7 +13,7 @@
 LANES = 128
 SLOT_ROWS = 2 * SHARE + 8
 AXES = ("x", "y", "core", "triple", "member")
-CORE, RESIDUE, SLAB, COUNTS = 0, 1, 2, 3
+CORE, RESIDUE, SLAB, TRIPLE, COUNTS = 0, 1, 2, 3, 4
 TRIPLES, MEMBERS = 4, 3
 FAR = ((9, 10, 11), (5, 6, 8), (3, 4, 7))
 
@@ -61,13 +61,10 @@
     return extra + pltpu.roll(extra, 4, 0)
 
 
-def sums_kernel(ratings_ref, before_ref, after_ref, sums_ref, own_ref):
+def sums_kernel(ratings_ref, sums_ref, own_ref):
     own_ref[...] = ratings_ref[...]
-    squares = jnp.zeros(ratings_ref.shape, jnp.float32)
-    for ref in (ratings_ref, before_ref, after_ref):
-        values = ref[...].astype(jnp.float32)
-        squares = squares + values * values
-    upright = jnp.sum(squares, axis=1, keepdims=True)
+    values = ratings_ref[...].astype(jnp.float32)
+    upright = jnp.sum(values * values, axis=1, keepdims=True)
     corner = lax.broadcasted_iota(jnp.int32, (LANES, LANES), 0) == lax.broadcasted_iota(
         jnp.int32, (LANES, LANES), 1
     )
@@ -77,7 +74,7 @@
     ]
     lying.append(jnp.zeros((8 - len(lying), LANES), jnp.float32))
     sums = jnp.concatenate(lying, axis=0)
-    for i in range(TRIPLES):
+    for i in range(PANELS):
         sums_ref[i] = sums
 
 
@@ -86,7 +83,7 @@
     core, residue = place_ref[CORE], place_ref[RESIDUE]
     rows, width = panels[0].shape
     sums = sums_ref[0]
-    for i in range(1, TRIPLES):
+    for i in range(1, PANELS):
         sums = sums + sums_ref[i]
     corner = lax.broadcasted_iota(jnp.int32, (LANES, LANES), 0) == lax.broadcasted_iota(
         jnp.int32, (LANES, LANES), 1
@@ -135,11 +132,12 @@
                 preferred_element_type=jnp.float32,
             )
     for x in range(X):
+        slot = lax.rem(place_ref[TRIPLE] + x, X) * Y
         for y in range(Y):
             start = (2 * y + x % 2) * SHARE
             low, high = start // LANES, (start + SHARE - 1) // LANES
             for mine in (True, False):
-                unit = 2 * (core if mine else 1 - core) + x // 2
+                unit = 2 * (core if mine else 1 - core) + 1 - x // 2
                 four = [column_ref[pl.ds(2 * unit + half, 1), :] for half in range(2)]
                 four += [row_ref[pl.ds(i, 1), :] for i in (low, high)]
                 extra = split_rows(jnp.concatenate(four + four, axis=0))
@@ -147,7 +145,7 @@
                 block = gram_ref[pl.ds(first, SHARE), :]
                 whole = jnp.concatenate([block[:, :LANES], block[:, LANES:], extra], axis=0)
                 ref = keep_ref if mine else send_ref
-                ref[x * Y + y] = whole.astype(ref.dtype)
+                ref[slot + y] = whole.astype(ref.dtype)
 
 
 def add_kernel(keep_ref, got_ref, out_ref):
@@ -192,9 +190,10 @@
         for y in range(Y):
             for core in range(CORES):
                 for z in range(PANELS):
-                    unit = 2 * core + x // 2
+                    by = (x - z // MEMBERS) % X
+                    unit = 2 * core + 1 - by // 2
                     column = COLUMNS[unit - 1][z] if unit else z
-                    user = 16 * (z // MEMBERS) + 2 * y + x % 2
+                    user = 16 * (z // MEMBERS) + 2 * y + by % 2
                     source = ((x * Y + y) * CORES + core) * PANELS + z
                     pairs.append((source, user * PANELS + column))
     return pairs
@@ -202,28 +201,28 @@
 
 def per_device(ratings, counts):
     rows, width = ratings.shape
-    x, y, core, member = (lax.axis_index(name) for name in ("x", "y", "core", "member"))
-    place = jnp.stack([core, member, 2 * y + x % 2]).astype(jnp.int32)
+    x, y, core, group, member = (lax.axis_index(name) for name in AXES)
+    place = jnp.stack([core, member, 2 * y + (x + group) % 2, group]).astype(jnp.int32)
     place = jnp.concatenate([place, counts])
 
-    def fetch(sources):
+    def fetch(array, sources):
         pairs = [(source, z) for z, source in enumerate(sources)]
-        return lax.ppermute(ratings, ("triple", "member"), pairs)
-
-    triple = [fetch([z // 3 * 3 + (z + by) % 3 for z in range(PANELS)]) for by in (2, 1)]
-    columns = [fetch(sources) for sources in COLUMNS]
+        return lax.ppermute(array, AXES[3:], pairs)
+
+    columns = [fetch(ratings, sources) for sources in COLUMNS]
     sums, own = pl.pallas_call(
         sums_kernel,
         out_shape=(
-            jax.ShapeDtypeStruct((TRIPLES, 8, LANES), jnp.float32),
+            jax.ShapeDtypeStruct((PANELS, 8, LANES), jnp.float32),
             jax.ShapeDtypeStruct((rows, width), ratings.dtype),
         ),
-        in_specs=[VMEM] * 3,
+        in_specs=[VMEM],
         out_specs=(VMEM, VMEM),
         compiler_params=PARAMS,
         name="sums",
-    )(ratings, *triple)
-    sums = lax.all_to_all(sums, "triple", 0, 0, tiled=True)
+    )(ratings)
+    sums = lax.all_to_all(sums, AXES[3:], 0, 0, tiled=True)
+    triple = [fetch(own, [z // 3 * 3 + (z + by) % 3 for z in range(PANELS)]) for by in (2, 1)]
 
     slots = (SLOTS, SLOT_ROWS, LANES)
     keep, send = pl.pallas_call(

time: 105 us -> 106 us (level)
  waiting for transfers between devices: 17.7 us -> 23.4 us
  starting transfers between devices: 47.4 us -> 42.4 us
    all_to_all x1, waiting for transfers between devices: 0.01 us -> 11.5 us  [per_device(): sums = lax.all_to_all(sums, AXES[3:], 0, 0, tiled=True)]
    ppermute x5, waiting for transfers between devices: 10.5 us -> 0.01 us  [fetch(): return lax.ppermute(array, AXES[3:], pairs)]
    ppermute x1, starting transfers between devices: 8.75 us -> 3.87 us  [per_device(): return lax.ppermute(block, AXES, homes())]
    ppermute x1, waiting for transfers between devices: 4.83 us -> 9.68 us  [per_device(): return lax.ppermute(block, AXES, homes())]
  transfers between devices with their start and end apart: 8 -> 8, of which waited for: 4 -> 3; matrix products, arithmetic and copies ran while one was open for 1% -> 1% of each run, Pallas kernels for 1% -> 1%
where the time goes in v9:
time: 106 us; the launch traced here: 105 us
  starting transfers between devices  42.4 us (40%)
  blocking collectives  33.3 us (31%)
  waiting for transfers between devices  23.4 us (22%)
  Pallas kernels  3.89 us (4%)
  local copies, waits for them, and re-layouts  2.27 us (2%)
    all_to_all x1, blocking collectives, per_device(): parts = lax.all_to_all(total, ('x', 'y'), 0, 0, tiled=True)  33.3 us
    ppermute x5, starting transfers between devices, fetch(): return lax.ppermute(array, AXES[3:], pairs)  32.6 us
    all_to_all x1, waiting for transfers between devices, per_device(): sums = lax.all_to_all(sums, AXES[3:], 0, 0, tiled=True)  11.5 us
    ppermute x1, waiting for transfers between devices, per_device(): return lax.ppermute(block, AXES, homes())  9.68 us
    all_to_all x1, starting transfers between devices, per_device(): sums = lax.all_to_all(sums, AXES[3:], 0, 0, tiled=True)  3.94 us
    ppermute x1, starting transfers between devices, per_device(): return lax.ppermute(block, AXES, homes())  3.87 us
    ppermute x1, waiting for transfers between devices, per_device(): got = lax.ppermute(send, 'core', [(0, 1), (1, 0)])  2.24 us
    pallas_call x1, Pallas kernels, per_device(): pl.pallas_call(partial_kernel, out_shape=(jax.ShapeDtypeStruct(slots, jnp...  2.24 us
  transfers between devices with their start and end apart: 8, of which 3 were waited for; matrix products, arithmetic and copies ran while one was open for 1% of the time, Pallas kernels for 1%

profile of v9, /device:TPU:12, one launch (start us, length us, event | category | flops | bytes accessed | tf_op | source)
XLA Modules:
  0.0 105.4 jit_solution(344749275416101074)
XLA Ops:
  0.0 10.9 %collective-permute-start.2 = (bf16[384,256]{1,0:T(8,128)(2,1)}, bf16[384,256]{1,0:T(8,128)(2,1)S(1)}, u32[]{:S(2)}, u32[]{:S(2)}) collective-permute-start(bf16[384,256]{1,0:T(8,128)(2,1)} %ratings_ref.1), channel_id=1, source_target_pairs={{10,0},{5,1},{4,2},{1,3},{0,4},{7,5},{3,6},{11,7},{9,8},{8,9},{6,1... | collective-permute-start | bytes 589832 | tf_op jit(solution)/shard_map/ppermute | solution.py:210
  10.9 7.3 %collective-permute-start.4 = (bf16[384,256]{1,0:T(8,128)(2,1)}, bf16[384,256]{1,0:T(8,128)(2,1)S(1)}, u32[]{:S(2)}, u32[]{:S(2)}) collective-permute-start(bf16[384,256]{1,0:T(8,128)(2,1)} %ratings_ref.1), channel_id=1, source_target_pairs={{11,0},{8,1},{7,2},{10,3},{9,4},{6,5},{5,6},{2,7},{1,8},{4,9},{3,1... | collective-permute-start | bytes 589832 | tf_op jit(solution)/shard_map/ppermute | solution.py:210
  18.2 8.5 %collective-permute-start.3 = (bf16[384,256]{1,0:T(8,128)(2,1)}, bf16[384,256]{1,0:T(8,128)(2,1)S(1)}, u32[]{:S(2)}, u32[]{:S(2)}) collective-permute-start(bf16[384,256]{1,0:T(8,128)(2,1)} %ratings_ref.1), channel_id=1, source_target_pairs={{9,0},{6,1},{3,2},{2,3},{11,4},{8,5},{4,6},{0,7},{10,8},{7,9},{5,1... | collective-permute-start | bytes 589832 | tf_op jit(solution)/shard_map/ppermute | solution.py:210
  26.7 0.0 copy-start
  26.8 0.9 copy-done
  27.7 0.8 sums.1
  28.4 1.9 %collective-permute-start.1 = (bf16[384,256]{1,0:T(8,128)(2,1)S(1)}, bf16[384,256]{1,0:T(8,128)(2,1)S(1)}, u32[]{:S(2)}, u32[]{:S(2)}) collective-permute-start(bf16[384,256]{1,0:T(8,128)(2,1)S(1)} %get-tuple-element.10.refs_0_), channel_id=1, source_target_pairs={{1,0},{2,1},{0,2},{4,3},{5,4},{3,5},{7,6},{8,7},{6,8},{10,9},{11,1... | collective-permute-start | bytes 589832 | tf_op jit(solution)/shard_map/ppermute | solution.py:210
  30.4 3.9 %collective-permute-start = (bf16[384,256]{1,0:T(8,128)(2,1)S(1)}, bf16[384,256]{1,0:T(8,128)(2,1)S(1)}, u32[]{:S(2)}, u32[]{:S(2)}) collective-permute-start(bf16[384,256]{1,0:T(8,128)(2,1)S(1)} %get-tuple-element.10.refs_0_), channel_id=1, source_target_pairs={{2,0},{0,1},{1,2},{5,3},{3,4},{4,5},{8,6},{6,7},{7,8},{11,9},{9,10... | collective-permute-start | bytes 589832 | tf_op jit(solution)/shard_map/ppermute | solution.py:210
  34.3 3.9 %all-to-all-start = ((f32[12,8,128]{2,1,0:T(8,128)}), f32[12,8,128]{2,1,0:T(8,128)S(1)}, u32[]{:S(2)}, u32[]{:S(2)}) async-start(f32[12,8,128]{2,1,0:T(8,128)} %get-tuple-element.9), calls=%async_computation | async-start | bytes 98304 | tf_op jit(solution)/shard_map/all_to_all | solution.py:224
  38.3 0.7 concatenate.3.place_ref
  39.0 11.5 %all-to-all-done.sums_ref = f32[12,8,128]{2,1,0:T(8,128)S(1)} async-done(((f32[12,8,128]{2,1,0:T(8,128)}), f32[12,8,128]{2,1,0:T(8,128)S(1)}, u32[]{:S(2)}, u32[]{:S(2)}) %all-to-all-start) | async-done | bytes 49184 | tf_op jit(solution)/shard_map/all_to_all | solution.py:224
  50.5 0.0 collective-permute-done.2.refs_3_
  50.5 0.0 collective-permute-done.4.refs_5_
  50.5 0.0 collective-permute-done.3.refs_4_
  50.5 0.0 collective-permute-done.1.refs_2_
  50.5 0.0 collective-permute-done.refs_1_
  50.5 2.2 %partial.1 = (f32[32,104,128]{2,1,0:T(8,128)S(1)}, bf16[32,104,128]{2,1,0:T(8,128)(2,1)S(1)}) custom-call(s32[10]{0:T(128)S(1)} %concatenate.3.place_ref, f32[12,8,128]{2,1,0:T(8,128)S(1)} %all-to-all-done.sums_ref, bf16[384,256]{1,0:T(8,128)(2,1)S(1)} %get-tuple-element.10.refs_0_, bf16[384,256]{1,0:T(8,128)(2,1)S(1)} %collective-permute-done.refs_1_, ...), custom_call_target="tpu_custom_call" | custom-call | tf_op jit(solution)/shard_map/partial/pallas_call | solution.py:228
  52.8 2.0 %collective-permute-start.5 = (bf16[32,104,128]{2,1,0:T(8,128)(2,1)S(1)}, bf16[32,104,128]{2,1,0:T(8,128)(2,1)S(1)}, u32[]{:S(2)}, u32[]{:S(2)}) collective-permute-start(bf16[32,104,128]{2,1,0:T(8,128)(2,1)S(1)} %get-tuple-element.12), channel_id=1, source_target_pairs={{0,12},{12,0},{1,13},{13,1},{2,14},{14,2},{3,15},{15,3},{4,16},{16... | collective-permute-start | bytes 2555912 | tf_op jit(solution)/shard_map/ppermute | solution.py:244
  54.8 2.2 %collective-permute-done.5.got_ref = bf16[32,104,128]{2,1,0:T(8,128)(2,1)S(1)} collective-permute-done((bf16[32,104,128]{2,1,0:T(8,128)(2,1)S(1)}, bf16[32,104,128]{2,1,0:T(8,128)(2,1)S(1)}, u32[]{:S(2)}, u32[]{:S(2)}) %collective-permute-start.5) | collective-permute-done | bytes 852000 | tf_op jit(solution)/shard_map/ppermute | solution.py:244
  57.0 0.2 add.14
  57.2 33.3 %all_to_all.10.got_ref = bf16[32,104,128]{2,1,0:T(8,128)(2,1)S(1)} all-to-all(bf16[32,104,128]{2,1,0:T(8,128)(2,1)S(1)} %add.14), channel_id=1, replica_groups=mesh['x'=4,'y'=8,'core'=2,'triple'=4,'member'=3] {'x','y'}, dimensions={0} | all-to-all | bytes 1703936 | tf_op jit(solution)/shard_map/all_to_all | solution.py:253
  90.5 0.7 finish.1
  91.2 3.9 %collective-permute-start.6 = (bf16[48,256]{1,0:T(8,128)(2,1)S(1)}, bf16[48,256]{1,0:T(8,128)(2,1)S(1)}, u32[]{:S(2)}, u32[]{:S(2)}) collective-permute-start(bf16[48,256]{1,0:T(8,128)(2,1)S(1)} %finish.1), channel_id=1, source_target_pairs={{0,10},{1,5},{2,4},{3,207},{4,208},{5,209},{6,390},{7,391},{8,392}... | collective-permute-start | bytes 73736 | tf_op jit(solution)/shard_map/ppermute | solution.py:262
  95.1 9.7 %collective-permute-done.6 = bf16[48,256]{1,0:T(8,128)(2,1)S(1)} collective-permute-done((bf16[48,256]{1,0:T(8,128)(2,1)S(1)}, bf16[48,256]{1,0:T(8,128)(2,1)S(1)}, u32[]{:S(2)}, u32[]{:S(2)}) %collective-permute-start.6) | collective-permute-done | bytes 24608 | tf_op jit(solution)/shard_map/ppermute | solution.py:262
  104.8 0.6 copy.4
Async XLA Ops:
  0.0 50.5 %collective-permute-start.2 = (bf16[384,256]{1,0:T(8,128)(2,1)}, bf16[384,256]{1,0:T(8,128)(2,1)S(1)}, u32[]{:S(2)}, u32[]{:S(2)}) collective-permute-start(bf16[384,256]{1,0:T(8,128)(2,1)} %ratings_ref.1), channel_id=1, source_target_pairs={{10,0},{5,1},{4,2},{1,3},{0,4},{7,5},{3,6},{11,7},{9,8},{8,9},{6,1... | collective-permute-start | bytes 589832 | tf_op jit(solution)/shard_map/ppermute | solution.py:210
  10.9 39.6 %collective-permute-start.4 = (bf16[384,256]{1,0:T(8,128)(2,1)}, bf16[384,256]{1,0:T(8,128)(2,1)S(1)}, u32[]{:S(2)}, u32[]{:S(2)}) collective-permute-start(bf16[384,256]{1,0:T(8,128)(2,1)} %ratings_ref.1), channel_id=1, source_target_pairs={{11,0},{8,1},{7,2},{10,3},{9,4},{6,5},{5,6},{2,7},{1,8},{4,9},{3,1... | collective-permute-start | bytes 589832 | tf_op jit(solution)/shard_map/ppermute | solution.py:210
  18.2 32.3 %collective-permute-start.3 = (bf16[384,256]{1,0:T(8,128)(2,1)}, bf16[384,256]{1,0:T(8,128)(2,1)S(1)}, u32[]{:S(2)}, u32[]{:S(2)}) collective-permute-start(bf16[384,256]{1,0:T(8,128)(2,1)} %ratings_ref.1), channel_id=1, source_target_pairs={{9,0},{6,1},{3,2},{2,3},{11,4},{8,5},{4,6},{0,7},{10,8},{7,9},{5,1... | collective-permute-start | bytes 589832 | tf_op jit(solution)/shard_map/ppermute | solution.py:210
  26.7 0.9 copy-start
  28.4 22.1 %collective-permute-start.1 = (bf16[384,256]{1,0:T(8,128)(2,1)S(1)}, bf16[384,256]{1,0:T(8,128)(2,1)S(1)}, u32[]{:S(2)}, u32[]{:S(2)}) collective-permute-start(bf16[384,256]{1,0:T(8,128)(2,1)S(1)} %get-tuple-element.10.refs_0_), channel_id=1, source_target_pairs={{1,0},{2,1},{0,2},{4,3},{5,4},{3,5},{7,6},{8,7},{6,8},{10,9},{11,1... | collective-permute-start | bytes 589832 | tf_op jit(solution)/shard_map/ppermute | solution.py:210
  30.4 20.2 %collective-permute-start = (bf16[384,256]{1,0:T(8,128)(2,1)S(1)}, bf16[384,256]{1,0:T(8,128)(2,1)S(1)}, u32[]{:S(2)}, u32[]{:S(2)}) collective-permute-start(bf16[384,256]{1,0:T(8,128)(2,1)S(1)} %get-tuple-element.10.refs_0_), channel_id=1, source_target_pairs={{2,0},{0,1},{1,2},{5,3},{3,4},{4,5},{8,6},{6,7},{7,8},{11,9},{9,10... | collective-permute-start | bytes 589832 | tf_op jit(solution)/shard_map/ppermute | solution.py:210
  34.3 16.2 %all-to-all-start = ((f32[12,8,128]{2,1,0:T(8,128)}), f32[12,8,128]{2,1,0:T(8,128)S(1)}, u32[]{:S(2)}, u32[]{:S(2)}) async-start(f32[12,8,128]{2,1,0:T(8,128)} %get-tuple-element.9), calls=%async_computation | async-start | bytes 98304 | tf_op jit(solution)/shard_map/all_to_all | solution.py:224
  52.8 4.3 %collective-permute-start.5 = (bf16[32,104,128]{2,1,0:T(8,128)(2,1)S(1)}, bf16[32,104,128]{2,1,0:T(8,128)(2,1)S(1)}, u32[]{:S(2)}, u32[]{:S(2)}) collective-permute-start(bf16[32,104,128]{2,1,0:T(8,128)(2,1)S(1)} %get-tuple-element.12), channel_id=1, source_target_pairs={{0,12},{12,0},{1,13},{13,1},{2,14},{14,2},{3,15},{15,3},{4,16},{16... | collective-permute-start | bytes 2555912 | tf_op jit(solution)/shard_map/ppermute | solution.py:244
  91.2 13.6 %collective-permute-start.6 = (bf16[48,256]{1,0:T(8,128)(2,1)S(1)}, bf16[48,256]{1,0:T(8,128)(2,1)S(1)}, u32[]{:S(2)}, u32[]{:S(2)}) collective-permute-start(bf16[48,256]{1,0:T(8,128)(2,1)S(1)} %finish.1), channel_id=1, source_target_pairs={{0,10},{1,5},{2,4},{3,207},{4,208},{5,209},{6,390},{7,391},{8,392}... | collective-permute-start | bytes 73736 | tf_op jit(solution)/shard_map/ppermute | solution.py:262

commit v10 on v6

--- a/solution.py
+++ b/solution.py
@@ -1,3 +1,5 @@
+import itertools
+
 import jax
 import jax.numpy as jnp
 from jax import lax
@@ -59,10 +61,52 @@
     sums_ref[...] = jnp.concatenate(lying, axis=0)
 
 
-def partial_kernel(place_ref, near_ref, far_ref, *refs):
-    panels, (keep_ref, send_ref, gram_ref, row_ref, column_ref) = refs[:8], refs[8:]
-    core = place_ref[2]
-    member, triple = held(place_ref)
+def weigh(scale, ref):
+    values = ref[...].astype(jnp.float32)
+    return values, (scale * values).astype(jnp.bfloat16)
+
+
+def half_products(place_ref, scale, panels, gram_ref, partner):
+    core, (member, _) = place_ref[2], held(place_ref)
+    width = panels[0].shape[1]
+    for its_core, its_member in itertools.product(range(CORES), range(MEMBERS)):
+        first, columns = UNITS[its_member]
+        at = 2 * (1 - its_core if partner else its_core)
+
+        @pl.when((core == its_core) & (member == its_member))
+        def _(first=first, columns=columns[at : at + 2]):
+            for unit, offset in enumerate(columns):
+                weighted = weigh(scale, panels[REACH + offset])[1]
+                for i in range(MEMBERS):
+                    gram_ref[pl.ds((3 * unit + i) * width, width), :] = lax.dot_general(
+                        panels[REACH + first + i][...],
+                        weighted,
+                        (((0,), (0,)), ((), ())),
+                        preferred_element_type=jnp.float32,
+                    )
+
+
+def write_slots(place_ref, gram_ref, row_ref, column_ref, out_ref, partner):
+    core, (_, triple) = place_ref[2], held(place_ref)
+    width = gram_ref.shape[1]
+    base = 2 * (1 - core if partner else core)
+    for x in range(X):
+        slot = lax.rem(triple + x, X) * Y
+        for y in range(Y):
+            start = (2 * y + x % 2) * SHARE
+            low, high = start // LANES, (start + SHARE - 1) // LANES
+            unit = x // 2
+            four = [column_ref[pl.ds(2 * (base + unit) + half, 1), :] for half in range(2)]
+            four += [row_ref[pl.ds(i, 1), :] for i in (low, high)]
+            extra = split_rows(jnp.concatenate(four + four, axis=0))
+            block = gram_ref[pl.ds(unit * 3 * width + start, SHARE), :]
+            whole = jnp.concatenate([block[:, :LANES], block[:, LANES:], extra], axis=0)
+            out_ref[slot + y] = whole.astype(out_ref.dtype)
+
+
+def send_kernel(place_ref, near_ref, far_ref, *refs):
+    panels, (send_ref, scale_ref, row_ref, column_ref, gram_ref) = refs[:8], refs[8:]
+    member = held(place_ref)[0]
     rows, width = panels[0].shape
     squares = jnp.zeros((rows, width), jnp.float32)
     for ref in (panels[0], panels[2 * REACH]):
@@ -87,13 +131,11 @@
     )
     scale = live / jnp.sqrt(square_sum / ITEMS + 1e-05)
 
-    def degree(ref):
-        values = ref[...].astype(jnp.float32)
-        weighted = (scale * values).astype(jnp.bfloat16)
-        total = values * weighted.astype(jnp.float32)
-        return weighted, jnp.sum(total, axis=0, keepdims=True)
-
-    def keep_degree(target, at, total):
+    scale_ref[...] = scale
+
+    def keep_degree(target, at, ref):
+        values, weighted = weigh(scale, ref)
+        total = jnp.sum(values * weighted.astype(jnp.float32), axis=0, keepdims=True)
         for half in range(2):
             lanes = total[:, half * LANES : (half + 1) * LANES]
             target[pl.ds(2 * at + half, 1), :] = lanes
@@ -101,36 +143,20 @@
     for its_member, (first, columns) in enumerate(UNITS):
 
         @pl.when(member == its_member)
-        def _():
-            row_panels = [panels[REACH + first + i] for i in range(MEMBERS)]
-            for i, ref in enumerate(row_panels):
-                keep_degree(row_ref, i, degree(ref)[1])
+        def _(first=first, columns=columns):
+            for i in range(MEMBERS):
+                keep_degree(row_ref, i, panels[REACH + first + i])
             for unit, offset in enumerate(columns):
-                weighted, total = degree(panels[REACH + offset])
-                keep_degree(column_ref, unit, total)
-                for i, ref in enumerate(row_panels):
-                    gram_ref[pl.ds((3 * unit + i) * width, width), :] = lax.dot_general(
-                        ref[...],
-                        weighted,
-                        (((0,), (0,)), ((), ())),
-                        preferred_element_type=jnp.float32,
-                    )
-
-    for x in range(X):
-        slot = lax.rem(triple + x, X) * Y
-        for y in range(Y):
-            start = (2 * y + x % 2) * SHARE
-            low, high = start // LANES, (start + SHARE - 1) // LANES
-            for mine in (True, False):
-                unit = 2 * (core if mine else 1 - core) + x // 2
-                four = [column_ref[pl.ds(2 * unit + half, 1), :] for half in range(2)]
-                four += [row_ref[pl.ds(i, 1), :] for i in (low, high)]
-                extra = split_rows(jnp.concatenate(four + four, axis=0))
-                at = pl.multiple_of(unit * 3 * width + start, 16)
-                block = gram_ref[pl.ds(at, SHARE), :]
-                whole = jnp.concatenate([block[:, :LANES], block[:, LANES:], extra], axis=0)
-                ref = keep_ref if mine else send_ref
-                ref[slot + y] = whole.astype(ref.dtype)
+                keep_degree(column_ref, unit, panels[REACH + offset])
+
+    half_products(place_ref, scale, panels, gram_ref, True)
+    write_slots(place_ref, gram_ref, row_ref, column_ref, send_ref, True)
+
+
+def keep_kernel(place_ref, scale_ref, row_ref, column_ref, *refs):
+    panels, (keep_ref, gram_ref) = refs[:8], refs[8:]
+    half_products(place_ref, scale_ref[...], panels, gram_ref, False)
+    write_slots(place_ref, gram_ref, row_ref, column_ref, keep_ref, False)
 
 
 def add_kernel(keep_ref, got_ref, out_ref):
@@ -214,23 +240,37 @@
     panels = below[:0:-1] + [own] + above[1:] + [last]
 
     slots = (SLOTS, SLOT_ROWS, LANES)
-    keep, send = pl.pallas_call(
-        partial_kernel,
+    lanes = jax.ShapeDtypeStruct((8, LANES), jnp.float32)
+    gram = [pltpu.VMEM((6 * width, width), jnp.float32)]
+    cost = pl.CostEstimate(
+        flops=12 * rows * width * width, bytes_accessed=12 * rows * width, transcendentals=0
+    )
+    send, *known = pl.pallas_call(
+        send_kernel,
         out_shape=(
-            jax.ShapeDtypeStruct(slots, jnp.float32),
             jax.ShapeDtypeStruct(slots, jnp.bfloat16),
+            jax.ShapeDtypeStruct((rows, 1), jnp.float32),
+            lanes,
+            lanes,
         ),
         in_specs=[SMEM] + [VMEM] * 10,
-        out_specs=(VMEM, VMEM),
-        scratch_shapes=[
-            pltpu.VMEM((12 * width, width), jnp.float32),
-            pltpu.VMEM((8, LANES), jnp.float32),
-            pltpu.VMEM((8, LANES), jnp.float32),
-        ],
-        compiler_params=PARAMS,
-        name="partial",
+        out_specs=(VMEM,) * 4,
+        scratch_shapes=gram,
+        compiler_params=PARAMS,
+        cost_estimate=cost,
+        name="send",
     )(place, near, far, *panels)
     got = lax.ppermute(send, "core", [(0, 1), (1, 0)])
+    keep = pl.pallas_call(
+        keep_kernel,
+        out_shape=jax.ShapeDtypeStruct(slots, jnp.float32),
+        in_specs=[SMEM] + [VMEM] * 11,
+        out_specs=VMEM,
+        scratch_shapes=gram,
+        compiler_params=PARAMS,
+        cost_estimate=cost,
+        name="keep",
+    )(place, *known, *panels)
     total = pl.pallas_call(
         add_kernel,
         out_shape=jax.ShapeDtypeStruct(slots, jnp.bfloat16),

time: 104 us -> 104 us (level)
  waiting for transfers between devices: 22 us -> 20.7 us
  Pallas kernels: 3.58 us -> 4.88 us
    ppermute x1, waiting for transfers between devices: 2.34 us -> 0.89 us  [per_device(): got = lax.ppermute(send, 'core', [(0, 1), (1, 0)])]
    pallas_call x1 -> x2, Pallas kernels: 2.42 us -> 3.75 us  [the longest x1 2.3 us: per_device(): pl.pallas_call(send_kernel, out_shape=(jax.ShapeDtypeStruct(slots, jnp.bf...]
  transfers between devices with their start and end apart: 10 -> 10, of which waited for: 6 -> 6; matrix products, arithmetic and copies ran while one was open for 1% -> 1% of each run, Pallas kernels for 0% -> 2%
where the time goes in v10:
time: 104 us; the launch traced here: 103 us
  starting transfers between devices  40.4 us (39%)
  blocking collectives  34.7 us (33%)
  waiting for transfers between devices  20.7 us (20%)
  Pallas kernels  4.88 us (5%)
  local copies, waits for them, and re-layouts  2.26 us (2%)
    ppermute x8, starting transfers between devices, fetch(): return lax.ppermute(array, 'z', [((z + by) % PANELS, z) for z in at])  36.6 us
    all_to_all x1, blocking collectives, per_device(): parts = lax.all_to_all(total, ('x', 'y'), 0, 0, tiled=True)  34.7 us
    ppermute x8, waiting for transfers between devices, fetch(): return lax.ppermute(array, 'z', [((z + by) % PANELS, z) for z in at])  14.2 us
    ppermute x1, waiting for transfers between devices, per_device(): return lax.ppermute(block, AXES, homes())  5.62 us
    pallas_call x1, Pallas kernels, per_device(): pl.pallas_call(send_kernel, out_shape=(jax.ShapeDtypeStruct(slots, jnp.bf...  2.3 us
  transfers between devices with their start and end apart: 10, of which 6 were waited for; matrix products, arithmetic and copies ran while one was open for 1% of the time, Pallas kernels for 2%

profile of v10, /device:TPU:8, one launch (start us, length us, event | category | flops | bytes accessed | tf_op | source)
XLA Modules:
  0.0 103.1 jit_solution(18141920028651639926)
XLA Ops:
  0.0 4.3 %collective-permute-start.2 = (bf16[384,256]{1,0:T(8,128)(2,1)}, bf16[384,256]{1,0:T(8,128)(2,1)S(1)}, u32[]{:S(2)}, u32[]{:S(2)}) collective-permute-start(bf16[384,256]{1,0:T(8,128)(2,1)} %refs_0_.1), channel_id=1, source_target_pairs={{11,0},{0,1},{1,2},{2,3},{3,4},{4,5},{5,6},{6,7},{7,8},{8,9},{9,10... | collective-permute-start | bytes 589832 | tf_op jit(solution)/shard_map/ppermute | solution.py:221
  4.3 12.2 %collective-permute-start = (bf16[384,256]{1,0:T(8,128)(2,1)}, bf16[384,256]{1,0:T(8,128)(2,1)S(1)}, u32[]{:S(2)}, u32[]{:S(2)}) collective-permute-start(bf16[384,256]{1,0:T(8,128)(2,1)} %refs_0_.1), channel_id=1, source_target_pairs={{1,0},{2,1},{3,2},{4,3},{5,4},{6,5},{7,6},{8,7},{9,8},{10,9},{11,1... | collective-permute-start | bytes 589832 | tf_op jit(solution)/shard_map/ppermute | solution.py:221
  16.5 3.2 %collective-permute-done.2.refs_3_.refs_2_ = bf16[384,256]{1,0:T(8,128)(2,1)S(1)} collective-permute-done((bf16[384,256]{1,0:T(8,128)(2,1)}, bf16[384,256]{1,0:T(8,128)(2,1)S(1)}, u32[]{:S(2)}, u32[]{:S(2)}) %collective-permute-start.2) | collective-permute-done | bytes 196640 | tf_op jit(solution)/shard_map/ppermute | solution.py:221
  19.7 1.9 %collective-permute-start.3 = (bf16[384,256]{1,0:T(8,128)(2,1)S(1)}, bf16[384,256]{1,0:T(8,128)(2,1)S(1)}, u32[]{:S(2)}, u32[]{:S(2)}) collective-permute-start(bf16[384,256]{1,0:T(8,128)(2,1)S(1)} %collective-permute-done.2.refs_3_.refs_2_), channel_id=1, source_target_pairs={{11,0},{0,1},{1,2},{2,3},{3,4},{4,5},{5,6},{6,7},{7,8},{8,9},{9,10... | collective-permute-start | bytes 589832 | tf_op jit(solution)/shard_map/ppermute | solution.py:221
  21.6 0.0 collective-permute-done.refs_1_.refs_4_
  21.6 5.1 %collective-permute-start.1 = (bf16[384,256]{1,0:T(8,128)(2,1)S(1)}, bf16[384,256]{1,0:T(8,128)(2,1)S(1)}, u32[]{:S(2)}, u32[]{:S(2)}) collective-permute-start(bf16[384,256]{1,0:T(8,128)(2,1)S(1)} %collective-permute-done.refs_1_.refs_4_), channel_id=1, source_target_pairs={{1,0},{2,1},{3,2},{4,3},{5,4},{6,5},{7,6},{8,7},{9,8},{10,9},{11,1... | collective-permute-start | bytes 589832 | tf_op jit(solution)/shard_map/ppermute | solution.py:221
  26.7 1.3 %collective-permute-start.7 = (bf16[384,256]{1,0:T(8,128)(2,1)}, bf16[384,256]{1,0:T(8,128)(2,1)S(1)}, u32[]{:S(2)}, u32[]{:S(2)}) collective-permute-start(bf16[384,256]{1,0:T(8,128)(2,1)} %refs_0_.1), channel_id=1, source_target_pairs={{4,0},{7,3},{10,6},{1,9},{16,12},{19,15},{22,18},{13,21},{28,24},{... | collective-permute-start | bytes 589832 | tf_op jit(solution)/shard_map/ppermute | solution.py:221
  28.0 0.8 collective-permute-done.3.refs_4_.refs_1_
  28.9 3.7 %collective-permute-start.5 = (bf16[384,256]{1,0:T(8,128)(2,1)S(1)}, bf16[384,256]{1,0:T(8,128)(2,1)S(1)}, u32[]{:S(2)}, u32[]{:S(2)}) collective-permute-start(bf16[384,256]{1,0:T(8,128)(2,1)S(1)} %collective-permute-done.3.refs_4_.refs_1_), channel_id=1, source_target_pairs={{11,0},{0,1},{1,2},{2,3},{3,4},{4,5},{5,6},{6,7},{7,8},{8,9},{9,10... | collective-permute-start | bytes 589832 | tf_op jit(solution)/shard_map/ppermute | solution.py:221
  32.6 1.6 %collective-permute-done.1.refs_2_.refs_5_ = bf16[384,256]{1,0:T(8,128)(2,1)S(1)} collective-permute-done((bf16[384,256]{1,0:T(8,128)(2,1)S(1)}, bf16[384,256]{1,0:T(8,128)(2,1)S(1)}, u32[]{:S(2)}, u32[]{:S(2)}) %collective-permute-start.1) | collective-permute-done | bytes 196640 | tf_op jit(solution)/shard_map/ppermute | solution.py:221
  34.2 5.6 %collective-permute-start.6 = (bf16[384,256]{1,0:T(8,128)(2,1)S(1)}, bf16[384,256]{1,0:T(8,128)(2,1)S(1)}, u32[]{:S(2)}, u32[]{:S(2)}) collective-permute-start(bf16[384,256]{1,0:T(8,128)(2,1)S(1)} %collective-permute-done.1.refs_2_.refs_5_), channel_id=1, source_target_pairs={{1,0},{2,1},{3,2},{4,3},{5,4},{6,5},{7,6},{8,7},{9,8},{10,9},{11,1... | collective-permute-start | bytes 589832 | tf_op jit(solution)/shard_map/ppermute | solution.py:221
  39.8 0.0 copy-start
  39.8 0.9 copy-done
  40.7 0.3 sums.1
  40.9 2.5 %collective-permute-start.4 = (f32[8,128]{1,0:T(8,128)S(1)}, f32[8,128]{1,0:T(8,128)S(1)}, u32[]{:S(2)}, u32[]{:S(2)}) collective-permute-start(f32[8,128]{1,0:T(8,128)S(1)} %get-tuple-element.11.near_ref), channel_id=1, source_target_pairs={{6,0},{7,1},{8,2},{9,3},{10,4},{11,5},{0,6},{1,7},{2,8},{3,9},{4,1... | collective-permute-start | bytes 12296 | tf_op jit(solution)/shard_map/ppermute | solution.py:221
  43.4 0.7 concatenate.3.place_ref
  44.2 0.0 collective-permute-done.7.refs_7_
  44.2 8.6 %collective-permute-done.4.far_ref = f32[8,128]{1,0:T(8,128)S(1)} collective-permute-done((f32[8,128]{1,0:T(8,128)S(1)}, f32[8,128]{1,0:T(8,128)S(1)}, u32[]{:S(2)}, u32[]{:S(2)}) %collective-permute-start.4) | collective-permute-done | bytes 4128 | tf_op jit(solution)/shard_map/ppermute | solution.py:221
  52.8 0.0 collective-permute-done.5.refs_0_
  52.8 0.0 collective-permute-done.6.refs_6_
  52.8 2.3 %send.1 = (bf16[32,104,128]{2,1,0:T(8,128)(2,1)S(1)}, f32[384,1]{1,0:T(8,128)S(1)}, f32[8,128]{1,0:T(8,128)S(1)}, f32[8,128]{1,0:T(8,128)S(1)}) custom-call(s32[10]{0:T(128)S(1)} %concatenate.3.place_ref, f32[8,128]{1,0:T(8,128)S(1)} %get-tuple-element.11.near_ref, f32[8,128]{1,0:T(8,128)S(1)} %collective-permute-done.4.far_ref, ...), custom_call_target="tpu_custom_call" | custom-call | flops 301989888 | bytes 1179648 | tf_op jit(solution)/shard_map/send/pallas_call | solution.py:248
  55.1 1.9 %collective-permute-start.8 = (bf16[32,104,128]{2,1,0:T(8,128)(2,1)S(1)}, bf16[32,104,128]{2,1,0:T(8,128)(2,1)S(1)}, u32[]{:S(2)}, u32[]{:S(2)}) collective-permute-start(bf16[32,104,128]{2,1,0:T(8,128)(2,1)S(1)} %get-tuple-element.16), channel_id=1, source_target_pairs={{0,12},{12,0},{1,13},{13,1},{2,14},{14,2},{3,15},{15,3},{4,16},{16... | collective-permute-start | bytes 2555912 | tf_op jit(solution)/shard_map/ppermute | solution.py:263
  57.0 1.4 %keep.1.keep_ref = f32[32,104,128]{2,1,0:T(8,128)S(1)} custom-call(s32[10]{0:T(128)S(1)} %concatenate.3.place_ref, f32[384,1]{1,0:T(8,128)S(1)} %get-tuple-element.13.scale_ref, f32[8,128]{1,0:T(8,128)S(1)} %get-tuple-element.14.row_ref, f32[8,128]{1,0:T(8,128)S(1)} %get-tuple-element.15.column_ref, bf16[384,256]{1,0:T(8,128)(2,1)S(1)} %collective-permute-done.5.refs_0_, ...), custom_call_target="tpu_custom_call" | custom-call | flops 301989888 | bytes 1179648 | tf_op jit(solution)/shard_map/keep/pallas_call | solution.py:264
  58.4 0.9 collective-permute-done.8.got_ref
  59.3 0.2 add.1
  59.5 34.7 %all_to_all.5.got_ref = bf16[32,104,128]{2,1,0:T(8,128)(2,1)S(1)} all-to-all(bf16[32,104,128]{2,1,0:T(8,128)(2,1)S(1)} %add.1), channel_id=1, replica_groups=mesh['x'=4,'y'=8,'core'=2,'z'=12] {'x','y'}, dimensions={0} | all-to-all | bytes 1703936 | tf_op jit(solution)/shard_map/all_to_all | solution.py:282
  94.2 0.7 finish.1
  94.9 1.9 %collective-permute-start.9 = (bf16[48,256]{1,0:T(8,128)(2,1)S(1)}, bf16[48,256]{1,0:T(8,128)(2,1)S(1)}, u32[]{:S(2)}, u32[]{:S(2)}) collective-permute-start(bf16[48,256]{1,0:T(8,128)(2,1)S(1)} %finish.1), channel_id=1, source_target_pairs={{0,592},{1,3},{2,206},{3,7},{4,208},{5,389},{6,211},{7,391},{8,593... | collective-permute-start | bytes 73736 | tf_op jit(solution)/shard_map/ppermute | solution.py:291
  96.9 5.6 %collective-permute-done.9 = bf16[48,256]{1,0:T(8,128)(2,1)S(1)} collective-permute-done((bf16[48,256]{1,0:T(8,128)(2,1)S(1)}, bf16[48,256]{1,0:T(8,128)(2,1)S(1)}, u32[]{:S(2)}, u32[]{:S(2)}) %collective-permute-start.9) | collective-permute-done | bytes 24608 | tf_op jit(solution)/shard_map/ppermute | solution.py:291
  102.5 0.6 copy.4
Async XLA Ops:
  0.0 19.7 %collective-permute-start.2 = (bf16[384,256]{1,0:T(8,128)(2,1)}, bf16[384,256]{1,0:T(8,128)(2,1)S(1)}, u32[]{:S(2)}, u32[]{:S(2)}) collective-permute-start(bf16[384,256]{1,0:T(8,128)(2,1)} %refs_0_.1), channel_id=1, source_target_pairs={{11,0},{0,1},{1,2},{2,3},{3,4},{4,5},{5,6},{6,7},{7,8},{8,9},{9,10... | collective-permute-start | bytes 589832 | tf_op jit(solution)/shard_map/ppermute | solution.py:221
  4.3 17.3 %collective-permute-start = (bf16[384,256]{1,0:T(8,128)(2,1)}, bf16[384,256]{1,0:T(8,128)(2,1)S(1)}, u32[]{:S(2)}, u32[]{:S(2)}) collective-permute-start(bf16[384,256]{1,0:T(8,128)(2,1)} %refs_0_.1), channel_id=1, source_target_pairs={{1,0},{2,1},{3,2},{4,3},{5,4},{6,5},{7,6},{8,7},{9,8},{10,9},{11,1... | collective-permute-start | bytes 589832 | tf_op jit(solution)/shard_map/ppermute | solution.py:221
  19.7 9.2 %collective-permute-start.3 = (bf16[384,256]{1,0:T(8,128)(2,1)S(1)}, bf16[384,256]{1,0:T(8,128)(2,1)S(1)}, u32[]{:S(2)}, u32[]{:S(2)}) collective-permute-start(bf16[384,256]{1,0:T(8,128)(2,1)S(1)} %collective-permute-done.2.refs_3_.refs_2_), channel_id=1, source_target_pairs={{11,0},{0,1},{1,2},{2,3},{3,4},{4,5},{5,6},{6,7},{7,8},{8,9},{9,10... | collective-permute-start | bytes 589832 | tf_op jit(solution)/shard_map/ppermute | solution.py:221
  21.6 12.6 %collective-permute-start.1 = (bf16[384,256]{1,0:T(8,128)(2,1)S(1)}, bf16[384,256]{1,0:T(8,128)(2,1)S(1)}, u32[]{:S(2)}, u32[]{:S(2)}) collective-permute-start(bf16[384,256]{1,0:T(8,128)(2,1)S(1)} %collective-permute-done.refs_1_.refs_4_), channel_id=1, source_target_pairs={{1,0},{2,1},{3,2},{4,3},{5,4},{6,5},{7,6},{8,7},{9,8},{10,9},{11,1... | collective-permute-start | bytes 589832 | tf_op jit(solution)/shard_map/ppermute | solution.py:221
  26.7 17.4 %collective-permute-start.7 = (bf16[384,256]{1,0:T(8,128)(2,1)}, bf16[384,256]{1,0:T(8,128)(2,1)S(1)}, u32[]{:S(2)}, u32[]{:S(2)}) collective-permute-start(bf16[384,256]{1,0:T(8,128)(2,1)} %refs_0_.1), channel_id=1, source_target_pairs={{4,0},{7,3},{10,6},{1,9},{16,12},{19,15},{22,18},{13,21},{28,24},{... | collective-permute-start | bytes 589832 | tf_op jit(solution)/shard_map/ppermute | solution.py:221
  28.9 23.9 %collective-permute-start.5 = (bf16[384,256]{1,0:T(8,128)(2,1)S(1)}, bf16[384,256]{1,0:T(8,128)(2,1)S(1)}, u32[]{:S(2)}, u32[]{:S(2)}) collective-permute-start(bf16[384,256]{1,0:T(8,128)(2,1)S(1)} %collective-permute-done.3.refs_4_.refs_1_), channel_id=1, source_target_pairs={{11,0},{0,1},{1,2},{2,3},{3,4},{4,5},{5,6},{6,7},{7,8},{8,9},{9,10... | collective-permute-start | bytes 589832 | tf_op jit(solution)/shard_map/ppermute | solution.py:221
  34.2 18.6 %collective-permute-start.6 = (bf16[384,256]{1,0:T(8,128)(2,1)S(1)}, bf16[384,256]{1,0:T(8,128)(2,1)S(1)}, u32[]{:S(2)}, u32[]{:S(2)}) collective-permute-start(bf16[384,256]{1,0:T(8,128)(2,1)S(1)} %collective-permute-done.1.refs_2_.refs_5_), channel_id=1, source_target_pairs={{1,0},{2,1},{3,2},{4,3},{5,4},{6,5},{7,6},{8,7},{9,8},{10,9},{11,1... | collective-permute-start | bytes 589832 | tf_op jit(solution)/shard_map/ppermute | solution.py:221
  39.8 0.9 copy-start
  40.9 11.8 %collective-permute-start.4 = (f32[8,128]{1,0:T(8,128)S(1)}, f32[8,128]{1,0:T(8,128)S(1)}, u32[]{:S(2)}, u32[]{:S(2)}) collective-permute-start(f32[8,128]{1,0:T(8,128)S(1)} %get-tuple-element.11.near_ref), channel_id=1, source_target_pairs={{6,0},{7,1},{8,2},{9,3},{10,4},{11,5},{0,6},{1,7},{2,8},{3,9},{4,1... | collective-permute-start | bytes 12296 | tf_op jit(solution)/shard_map/ppermute | solution.py:221
  55.1 4.3 %collective-permute-start.8 = (bf16[32,104,128]{2,1,0:T(8,128)(2,1)S(1)}, bf16[32,104,128]{2,1,0:T(8,128)(2,1)S(1)}, u32[]{:S(2)}, u32[]{:S(2)}) collective-permute-start(bf16[32,104,128]{2,1,0:T(8,128)(2,1)S(1)} %get-tuple-element.16), channel_id=1, source_target_pairs={{0,12},{12,0},{1,13},{13,1},{2,14},{14,2},{3,15},{15,3},{4,16},{16... | collective-permute-start | bytes 2555912 | tf_op jit(solution)/shard_map/ppermute | solution.py:263
  94.9 7.5 %collective-permute-start.9 = (bf16[48,256]{1,0:T(8,128)(2,1)S(1)}, bf16[48,256]{1,0:T(8,128)(2,1)S(1)}, u32[]{:S(2)}, u32[]{:S(2)}) collective-permute-start(bf16[48,256]{1,0:T(8,128)(2,1)S(1)} %finish.1), channel_id=1, source_target_pairs={{0,592},{1,3},{2,206},{3,7},{4,208},{5,389},{6,211},{7,391},{8,593... | collective-permute-start | bytes 73736 | tf_op jit(solution)/shard_map/ppermute | solution.py:291

commit v11 on v10

--- a/solution.py
+++ b/solution.py
@@ -168,11 +168,22 @@
         )
 
 
+def fold_kernel(got_ref, out_ref):
+    for slot in range(Y):
+        total = got_ref[slot].astype(jnp.float32)
+        for x in range(1, X):
+            total = total + got_ref[x * Y + slot].astype(jnp.float32)
+        extra = split_rows(join_rows(total[2 * SHARE :]))
+        out_ref[slot] = jnp.concatenate([total[: 2 * SHARE], extra], axis=0).astype(
+            jnp.bfloat16
+        )
+
+
 def finish_kernel(place_ref, got_ref, out_ref):
     by = lax.rem(place_ref[0] - held(place_ref)[1] + X, X)
     offset = lax.rem((2 * place_ref[1] + lax.rem(by, 2)) * SHARE, LANES)
     total = got_ref[0].astype(jnp.float32)
-    for slot in range(1, SLOTS):
+    for slot in range(1, Y):
         total = total + got_ref[slot].astype(jnp.float32)
     extra = join_rows(total[2 * SHARE :])
     lane = lax.broadcasted_iota(jnp.int32, (SHARE, LANES), 1)
@@ -279,7 +290,16 @@
         compiler_params=PARAMS,
         name="add",
     )(keep, got)
-    parts = lax.all_to_all(total, ("x", "y"), 0, 0, tiled=True)
+    parts = lax.all_to_all(total, "x", 0, 0, tiled=True)
+    total = pl.pallas_call(
+        fold_kernel,
+        out_shape=jax.ShapeDtypeStruct((Y, SLOT_ROWS, LANES), jnp.bfloat16),
+        in_specs=[VMEM],
+        out_specs=VMEM,
+        compiler_params=PARAMS,
+        name="fold",
+    )(parts)
+    parts = lax.all_to_all(total, "y", 0, 0, tiled=True)
     block = pl.pallas_call(
         finish_kernel,
         out_shape=jax.ShapeDtypeStruct((SHARE, width), jnp.bfloat16),

time: 104 us -> 102 us (0.981)
  blocking collectives: 34.7 us -> 33.2 us
    all_to_all x1 -> x2, blocking collectives: 34.7 us -> 33.2 us  [the longest x1 17.4 us: per_device(): parts = lax.all_to_all(total, 'x', 0, 0, tiled=True)]
where the time goes in v11:
time: 102 us
  starting transfers between devices  40.4 us (40%)
  blocking collectives  33.2 us (33%)
  waiting for transfers between devices  20.7 us (20%)
  Pallas kernels  4.98 us (5%)
  local copies, waits for them, and re-layouts  2.26 us (2%)
    ppermute x8, starting transfers between devices, fetch(): return lax.ppermute(array, 'z', [((z + by) % PANELS, z) for z in at])  36.6 us
    all_to_all x1, blocking collectives, per_device(): parts = lax.all_to_all(total, 'x', 0, 0, tiled=True)  17.4 us
    all_to_all x1, blocking collectives, per_device(): parts = lax.all_to_all(total, 'y', 0, 0, tiled=True)  15.9 us
    ppermute x8, waiting for transfers between devices, fetch(): return lax.ppermute(array, 'z', [((z + by) % PANELS, z) for z in at])  14.2 us
    ppermute x1, waiting for transfers between devices, per_device(): return lax.ppermute(block, AXES, homes())  5.62 us
    pallas_call x1, Pallas kernels, per_device(): pl.pallas_call(send_kernel, out_shape=(jax.ShapeDtypeStruct(slots, jnp.bf...  2.3 us
  transfers between devices with their start and end apart: 10, of which 6 were waited for; matrix products, arithmetic and copies ran while one was open for 1% of the time, Pallas kernels for 2%

profile of v11, /device:TPU:8, one launch (start us, length us, event | category | flops | bytes accessed | tf_op | source)
XLA Modules:
  0.0 101.7 jit_solution(15866088573368361676)
XLA Ops:
  0.0 4.3 %collective-permute-start.2 = (bf16[384,256]{1,0:T(8,128)(2,1)}, bf16[384,256]{1,0:T(8,128)(2,1)S(1)}, u32[]{:S(2)}, u32[]{:S(2)}) collective-permute-start(bf16[384,256]{1,0:T(8,128)(2,1)} %refs_0_.1), channel_id=1, source_target_pairs={{11,0},{0,1},{1,2},{2,3},{3,4},{4,5},{5,6},{6,7},{7,8},{8,9},{9,10... | collective-permute-start | bytes 589832 | tf_op jit(solution)/shard_map/ppermute | solution.py:232
  4.3 12.2 %collective-permute-start = (bf16[384,256]{1,0:T(8,128)(2,1)}, bf16[384,256]{1,0:T(8,128)(2,1)S(1)}, u32[]{:S(2)}, u32[]{:S(2)}) collective-permute-start(bf16[384,256]{1,0:T(8,128)(2,1)} %refs_0_.1), channel_id=1, source_target_pairs={{1,0},{2,1},{3,2},{4,3},{5,4},{6,5},{7,6},{8,7},{9,8},{10,9},{11,1... | collective-permute-start | bytes 589832 | tf_op jit(solution)/shard_map/ppermute | solution.py:232
  16.5 3.2 %collective-permute-done.2.refs_3_.refs_2_ = bf16[384,256]{1,0:T(8,128)(2,1)S(1)} collective-permute-done((bf16[384,256]{1,0:T(8,128)(2,1)}, bf16[384,256]{1,0:T(8,128)(2,1)S(1)}, u32[]{:S(2)}, u32[]{:S(2)}) %collective-permute-start.2) | collective-permute-done | bytes 196640 | tf_op jit(solution)/shard_map/ppermute | solution.py:232
  19.7 1.9 %collective-permute-start.3 = (bf16[384,256]{1,0:T(8,128)(2,1)S(1)}, bf16[384,256]{1,0:T(8,128)(2,1)S(1)}, u32[]{:S(2)}, u32[]{:S(2)}) collective-permute-start(bf16[384,256]{1,0:T(8,128)(2,1)S(1)} %collective-permute-done.2.refs_3_.refs_2_), channel_id=1, source_target_pairs={{11,0},{0,1},{1,2},{2,3},{3,4},{4,5},{5,6},{6,7},{7,8},{8,9},{9,10... | collective-permute-start | bytes 589832 | tf_op jit(solution)/shard_map/ppermute | solution.py:232
  21.6 0.0 collective-permute-done.refs_1_.refs_4_
  21.6 5.1 %collective-permute-start.1 = (bf16[384,256]{1,0:T(8,128)(2,1)S(1)}, bf16[384,256]{1,0:T(8,128)(2,1)S(1)}, u32[]{:S(2)}, u32[]{:S(2)}) collective-permute-start(bf16[384,256]{1,0:T(8,128)(2,1)S(1)} %collective-permute-done.refs_1_.refs_4_), channel_id=1, source_target_pairs={{1,0},{2,1},{3,2},{4,3},{5,4},{6,5},{7,6},{8,7},{9,8},{10,9},{11,1... | collective-permute-start | bytes 589832 | tf_op jit(solution)/shard_map/ppermute | solution.py:232
  26.7 1.3 %collective-permute-start.7 = (bf16[384,256]{1,0:T(8,128)(2,1)}, bf16[384,256]{1,0:T(8,128)(2,1)S(1)}, u32[]{:S(2)}, u32[]{:S(2)}) collective-permute-start(bf16[384,256]{1,0:T(8,128)(2,1)} %refs_0_.1), channel_id=1, source_target_pairs={{4,0},{7,3},{10,6},{1,9},{16,12},{19,15},{22,18},{13,21},{28,24},{... | collective-permute-start | bytes 589832 | tf_op jit(solution)/shard_map/ppermute | solution.py:232
  28.0 0.8 collective-permute-done.3.refs_4_.refs_1_
  28.9 3.7 %collective-permute-start.5 = (bf16[384,256]{1,0:T(8,128)(2,1)S(1)}, bf16[384,256]{1,0:T(8,128)(2,1)S(1)}, u32[]{:S(2)}, u32[]{:S(2)}) collective-permute-start(bf16[384,256]{1,0:T(8,128)(2,1)S(1)} %collective-permute-done.3.refs_4_.refs_1_), channel_id=1, source_target_pairs={{11,0},{0,1},{1,2},{2,3},{3,4},{4,5},{5,6},{6,7},{7,8},{8,9},{9,10... | collective-permute-start | bytes 589832 | tf_op jit(solution)/shard_map/ppermute | solution.py:232
  32.6 1.6 %collective-permute-done.1.refs_2_.refs_5_ = bf16[384,256]{1,0:T(8,128)(2,1)S(1)} collective-permute-done((bf16[384,256]{1,0:T(8,128)(2,1)S(1)}, bf16[384,256]{1,0:T(8,128)(2,1)S(1)}, u32[]{:S(2)}, u32[]{:S(2)}) %collective-permute-start.1) | collective-permute-done | bytes 196640 | tf_op jit(solution)/shard_map/ppermute | solution.py:232
  34.2 5.6 %collective-permute-start.6 = (bf16[384,256]{1,0:T(8,128)(2,1)S(1)}, bf16[384,256]{1,0:T(8,128)(2,1)S(1)}, u32[]{:S(2)}, u32[]{:S(2)}) collective-permute-start(bf16[384,256]{1,0:T(8,128)(2,1)S(1)} %collective-permute-done.1.refs_2_.refs_5_), channel_id=1, source_target_pairs={{1,0},{2,1},{3,2},{4,3},{5,4},{6,5},{7,6},{8,7},{9,8},{10,9},{11,1... | collective-permute-start | bytes 589832 | tf_op jit(solution)/shard_map/ppermute | solution.py:232
  39.8 0.0 copy-start
  39.8 0.9 copy-done
  40.7 0.3 sums.1
  40.9 2.5 %collective-permute-start.4 = (f32[8,128]{1,0:T(8,128)S(1)}, f32[8,128]{1,0:T(8,128)S(1)}, u32[]{:S(2)}, u32[]{:S(2)}) collective-permute-start(f32[8,128]{1,0:T(8,128)S(1)} %get-tuple-element.11.near_ref), channel_id=1, source_target_pairs={{6,0},{7,1},{8,2},{9,3},{10,4},{11,5},{0,6},{1,7},{2,8},{3,9},{4,1... | collective-permute-start | bytes 12296 | tf_op jit(solution)/shard_map/ppermute | solution.py:232
  43.4 0.7 concatenate.3.place_ref
  44.2 0.0 collective-permute-done.7.refs_7_
  44.2 8.6 %collective-permute-done.4.far_ref = f32[8,128]{1,0:T(8,128)S(1)} collective-permute-done((f32[8,128]{1,0:T(8,128)S(1)}, f32[8,128]{1,0:T(8,128)S(1)}, u32[]{:S(2)}, u32[]{:S(2)}) %collective-permute-start.4) | collective-permute-done | bytes 4128 | tf_op jit(solution)/shard_map/ppermute | solution.py:232
  52.8 0.0 collective-permute-done.5.refs_0_
  52.8 0.0 collective-permute-done.6.refs_6_
  52.8 2.3 %send.1 = (bf16[32,104,128]{2,1,0:T(8,128)(2,1)S(1)}, f32[384,1]{1,0:T(8,128)S(1)}, f32[8,128]{1,0:T(8,128)S(1)}, f32[8,128]{1,0:T(8,128)S(1)}) custom-call(s32[10]{0:T(128)S(1)} %concatenate.3.place_ref, f32[8,128]{1,0:T(8,128)S(1)} %get-tuple-element.11.near_ref, f32[8,128]{1,0:T(8,128)S(1)} %collective-permute-done.4.far_ref, ...), custom_call_target="tpu_custom_call" | custom-call | flops 301989888 | bytes 1179648 | tf_op jit(solution)/shard_map/send/pallas_call | solution.py:259
  55.1 1.9 %collective-permute-start.8 = (bf16[32,104,128]{2,1,0:T(8,128)(2,1)S(1)}, bf16[32,104,128]{2,1,0:T(8,128)(2,1)S(1)}, u32[]{:S(2)}, u32[]{:S(2)}) collective-permute-start(bf16[32,104,128]{2,1,0:T(8,128)(2,1)S(1)} %get-tuple-element.16), channel_id=1, source_target_pairs={{0,12},{12,0},{1,13},{13,1},{2,14},{14,2},{3,15},{15,3},{4,16},{16... | collective-permute-start | bytes 2555912 | tf_op jit(solution)/shard_map/ppermute | solution.py:274
  57.0 1.4 %keep.1.keep_ref = f32[32,104,128]{2,1,0:T(8,128)S(1)} custom-call(s32[10]{0:T(128)S(1)} %concatenate.3.place_ref, f32[384,1]{1,0:T(8,128)S(1)} %get-tuple-element.13.scale_ref, f32[8,128]{1,0:T(8,128)S(1)} %get-tuple-element.14.row_ref, f32[8,128]{1,0:T(8,128)S(1)} %get-tuple-element.15.column_ref, bf16[384,256]{1,0:T(8,128)(2,1)S(1)} %collective-permute-done.5.refs_0_, ...), custom_call_target="tpu_custom_call" | custom-call | flops 301989888 | bytes 1179648 | tf_op jit(solution)/shard_map/keep/pallas_call | solution.py:275
  58.4 0.9 collective-permute-done.8.got_ref
  59.3 0.2 add.1
  59.5 17.4 %all_to_all.10.got_ref = bf16[32,104,128]{2,1,0:T(8,128)(2,1)S(1)} all-to-all(bf16[32,104,128]{2,1,0:T(8,128)(2,1)S(1)} %add.1), channel_id=1, replica_groups=mesh['x'=4,'y'=8,'core'=2,'z'=12] {'x'}, dimensions={0} | all-to-all | bytes 1703936 | tf_op jit(solution)/shard_map/all_to_all | solution.py:293
  76.9 0.1 fold.1
  77.0 15.9 %all_to_all.11.got_ref = bf16[8,104,128]{2,1,0:T(8,128)(2,1)S(1)} all-to-all(bf16[8,104,128]{2,1,0:T(8,128)(2,1)S(1)} %fold.1), channel_id=1, replica_groups=mesh['x'=4,'y'=8,'core'=2,'z'=12] {'y'}, dimensions={0} | all-to-all | bytes 425984 | tf_op jit(solution)/shard_map/all_to_all | solution.py:302
  92.9 0.7 finish.1
  93.6 1.9 %collective-permute-start.9 = (bf16[48,256]{1,0:T(8,128)(2,1)S(1)}, bf16[48,256]{1,0:T(8,128)(2,1)S(1)}, u32[]{:S(2)}, u32[]{:S(2)}) collective-permute-start(bf16[48,256]{1,0:T(8,128)(2,1)S(1)} %finish.1), channel_id=1, source_target_pairs={{0,592},{1,3},{2,206},{3,7},{4,208},{5,389},{6,211},{7,391},{8,593... | collective-permute-start | bytes 73736 | tf_op jit(solution)/shard_map/ppermute | solution.py:311
  95.5 5.6 %collective-permute-done.9 = bf16[48,256]{1,0:T(8,128)(2,1)S(1)} collective-permute-done((bf16[48,256]{1,0:T(8,128)(2,1)S(1)}, bf16[48,256]{1,0:T(8,128)(2,1)S(1)}, u32[]{:S(2)}, u32[]{:S(2)}) %collective-permute-start.9) | collective-permute-done | bytes 24608 | tf_op jit(solution)/shard_map/ppermute | solution.py:311
  101.1 0.6 copy.4
Async XLA Ops:
  0.0 19.7 %collective-permute-start.2 = (bf16[384,256]{1,0:T(8,128)(2,1)}, bf16[384,256]{1,0:T(8,128)(2,1)S(1)}, u32[]{:S(2)}, u32[]{:S(2)}) collective-permute-start(bf16[384,256]{1,0:T(8,128)(2,1)} %refs_0_.1), channel_id=1, source_target_pairs={{11,0},{0,1},{1,2},{2,3},{3,4},{4,5},{5,6},{6,7},{7,8},{8,9},{9,10... | collective-permute-start | bytes 589832 | tf_op jit(solution)/shard_map/ppermute | solution.py:232
  4.3 17.3 %collective-permute-start = (bf16[384,256]{1,0:T(8,128)(2,1)}, bf16[384,256]{1,0:T(8,128)(2,1)S(1)}, u32[]{:S(2)}, u32[]{:S(2)}) collective-permute-start(bf16[384,256]{1,0:T(8,128)(2,1)} %refs_0_.1), channel_id=1, source_target_pairs={{1,0},{2,1},{3,2},{4,3},{5,4},{6,5},{7,6},{8,7},{9,8},{10,9},{11,1... | collective-permute-start | bytes 589832 | tf_op jit(solution)/shard_map/ppermute | solution.py:232
  19.7 9.2 %collective-permute-start.3 = (bf16[384,256]{1,0:T(8,128)(2,1)S(1)}, bf16[384,256]{1,0:T(8,128)(2,1)S(1)}, u32[]{:S(2)}, u32[]{:S(2)}) collective-permute-start(bf16[384,256]{1,0:T(8,128)(2,1)S(1)} %collective-permute-done.2.refs_3_.refs_2_), channel_id=1, source_target_pairs={{11,0},{0,1},{1,2},{2,3},{3,4},{4,5},{5,6},{6,7},{7,8},{8,9},{9,10... | collective-permute-start | bytes 589832 | tf_op jit(solution)/shard_map/ppermute | solution.py:232
  21.6 12.6 %collective-permute-start.1 = (bf16[384,256]{1,0:T(8,128)(2,1)S(1)}, bf16[384,256]{1,0:T(8,128)(2,1)S(1)}, u32[]{:S(2)}, u32[]{:S(2)}) collective-permute-start(bf16[384,256]{1,0:T(8,128)(2,1)S(1)} %collective-permute-done.refs_1_.refs_4_), channel_id=1, source_target_pairs={{1,0},{2,1},{3,2},{4,3},{5,4},{6,5},{7,6},{8,7},{9,8},{10,9},{11,1... | collective-permute-start | bytes 589832 | tf_op jit(solution)/shard_map/ppermute | solution.py:232
  26.7 17.4 %collective-permute-start.7 = (bf16[384,256]{1,0:T(8,128)(2,1)}, bf16[384,256]{1,0:T(8,128)(2,1)S(1)}, u32[]{:S(2)}, u32[]{:S(2)}) collective-permute-start(bf16[384,256]{1,0:T(8,128)(2,1)} %refs_0_.1), channel_id=1, source_target_pairs={{4,0},{7,3},{10,6},{1,9},{16,12},{19,15},{22,18},{13,21},{28,24},{... | collective-permute-start | bytes 589832 | tf_op jit(solution)/shard_map/ppermute | solution.py:232
  28.9 23.9 %collective-permute-start.5 = (bf16[384,256]{1,0:T(8,128)(2,1)S(1)}, bf16[384,256]{1,0:T(8,128)(2,1)S(1)}, u32[]{:S(2)}, u32[]{:S(2)}) collective-permute-start(bf16[384,256]{1,0:T(8,128)(2,1)S(1)} %collective-permute-done.3.refs_4_.refs_1_), channel_id=1, source_target_pairs={{11,0},{0,1},{1,2},{2,3},{3,4},{4,5},{5,6},{6,7},{7,8},{8,9},{9,10... | collective-permute-start | bytes 589832 | tf_op jit(solution)/shard_map/ppermute | solution.py:232
  34.2 18.6 %collective-permute-start.6 = (bf16[384,256]{1,0:T(8,128)(2,1)S(1)}, bf16[384,256]{1,0:T(8,128)(2,1)S(1)}, u32[]{:S(2)}, u32[]{:S(2)}) collective-permute-start(bf16[384,256]{1,0:T(8,128)(2,1)S(1)} %collective-permute-done.1.refs_2_.refs_5_), channel_id=1, source_target_pairs={{1,0},{2,1},{3,2},{4,3},{5,4},{6,5},{7,6},{8,7},{9,8},{10,9},{11,1... | collective-permute-start | bytes 589832 | tf_op jit(solution)/shard_map/ppermute | solution.py:232
  39.8 0.9 copy-start
  40.9 11.8 %collective-permute-start.4 = (f32[8,128]{1,0:T(8,128)S(1)}, f32[8,128]{1,0:T(8,128)S(1)}, u32[]{:S(2)}, u32[]{:S(2)}) collective-permute-start(f32[8,128]{1,0:T(8,128)S(1)} %get-tuple-element.11.near_ref), channel_id=1, source_target_pairs={{6,0},{7,1},{8,2},{9,3},{10,4},{11,5},{0,6},{1,7},{2,8},{3,9},{4,1... | collective-permute-start | bytes 12296 | tf_op jit(solution)/shard_map/ppermute | solution.py:232
  55.1 4.3 %collective-permute-start.8 = (bf16[32,104,128]{2,1,0:T(8,128)(2,1)S(1)}, bf16[32,104,128]{2,1,0:T(8,128)(2,1)S(1)}, u32[]{:S(2)}, u32[]{:S(2)}) collective-permute-start(bf16[32,104,128]{2,1,0:T(8,128)(2,1)S(1)} %get-tuple-element.16), channel_id=1, source_target_pairs={{0,12},{12,0},{1,13},{13,1},{2,14},{14,2},{3,15},{15,3},{4,16},{16... | collective-permute-start | bytes 2555912 | tf_op jit(solution)/shard_map/ppermute | solution.py:274
  93.6 7.5 %collective-permute-start.9 = (bf16[48,256]{1,0:T(8,128)(2,1)S(1)}, bf16[48,256]{1,0:T(8,128)(2,1)S(1)}, u32[]{:S(2)}, u32[]{:S(2)}) collective-permute-start(bf16[48,256]{1,0:T(8,128)(2,1)S(1)} %finish.1), channel_id=1, source_target_pairs={{0,592},{1,3},{2,206},{3,7},{4,208},{5,389},{6,211},{7,391},{8,593... | collective-permute-start | bytes 73736 | tf_op jit(solution)/shard_map/ppermute | solution.py:311

commit v12 on v11

--- a/solution.py
+++ b/solution.py
@@ -66,6 +66,12 @@
     return values, (scale * values).astype(jnp.bfloat16)
 
 
+def panel_at(panels, core, offset):
+    if offset > REACH:
+        return panels[-1]
+    return panels[REACH - offset if core else REACH + offset]
+
+
 def half_products(place_ref, scale, panels, gram_ref, partner):
     core, (member, _) = place_ref[2], held(place_ref)
     width = panels[0].shape[1]
@@ -74,12 +80,12 @@
         at = 2 * (1 - its_core if partner else its_core)
 
         @pl.when((core == its_core) & (member == its_member))
-        def _(first=first, columns=columns[at : at + 2]):
+        def _(its_core=its_core, first=first, columns=columns[at : at + 2]):
             for unit, offset in enumerate(columns):
-                weighted = weigh(scale, panels[REACH + offset])[1]
+                weighted = weigh(scale, panel_at(panels, its_core, offset))[1]
                 for i in range(MEMBERS):
                     gram_ref[pl.ds((3 * unit + i) * width, width), :] = lax.dot_general(
-                        panels[REACH + first + i][...],
+                        panel_at(panels, its_core, first + i)[...],
                         weighted,
                         (((0,), (0,)), ((), ())),
                         preferred_element_type=jnp.float32,
@@ -106,7 +112,7 @@
 
 def send_kernel(place_ref, near_ref, far_ref, *refs):
     panels, (send_ref, scale_ref, row_ref, column_ref, gram_ref) = refs[:8], refs[8:]
-    member = held(place_ref)[0]
+    core, (member, _) = place_ref[2], held(place_ref)
     rows, width = panels[0].shape
     squares = jnp.zeros((rows, width), jnp.float32)
     for ref in (panels[0], panels[2 * REACH]):
@@ -140,14 +146,15 @@
             lanes = total[:, half * LANES : (half + 1) * LANES]
             target[pl.ds(2 * at + half, 1), :] = lanes
 
-    for its_member, (first, columns) in enumerate(UNITS):
-
-        @pl.when(member == its_member)
-        def _(first=first, columns=columns):
+    for its_core, its_member in itertools.product(range(CORES), range(MEMBERS)):
+        first, columns = UNITS[its_member]
+
+        @pl.when((core == its_core) & (member == its_member))
+        def _(its_core=its_core, first=first, columns=columns):
             for i in range(MEMBERS):
-                keep_degree(row_ref, i, panels[REACH + first + i])
+                keep_degree(row_ref, i, panel_at(panels, its_core, first + i))
             for unit, offset in enumerate(columns):
-                keep_degree(column_ref, unit, panels[REACH + offset])
+                keep_degree(column_ref, unit, panel_at(panels, its_core, offset))
 
     half_products(place_ref, scale, panels, gram_ref, True)
     write_slots(place_ref, gram_ref, row_ref, column_ref, send_ref, True)
@@ -231,10 +238,17 @@
     def fetch(array, by, at=range(PANELS)):
         return lax.ppermute(array, "z", [((z + by) % PANELS, z) for z in at])
 
+    def relay(array, by):
+        pairs = []
+        for c in range(CORES):
+            shift = -by if c else by
+            pairs += [(c * PANELS + (z + shift) % PANELS, c * PANELS + z) for z in range(PANELS)]
+        return lax.ppermute(array, ("core", "z"), pairs)
+
     above, below = [ratings], [ratings]
     for _ in range(REACH):
-        above.append(fetch(above[-1], 1))
-        below.append(fetch(below[-1], -1))
+        above.append(relay(above[-1], 1))
+        below.append(relay(below[-1], -1))
     last = fetch(ratings, REACH + 1, range(0, PANELS, MEMBERS))
     near, own = pl.pallas_call(
         sums_kernel,

time: 102 us -> 97.9 us (0.960)
  the two profiles are of different devices: /device:TPU:8 before, /device:TPU:6 now
where the time goes in v12:
time: 97.9 us; the launch traced here: 97.4 us
  starting transfers between devices  47.5 us (49%)
  blocking collectives  32.7 us (33%)
  waiting for transfers between devices  9.87 us (10%)
  Pallas kernels  5 us (5%)
  local copies, waits for them, and re-layouts  2.26 us (2%)
    ppermute x6, starting transfers between devices, relay(): return lax.ppermute(array, ('core', 'z'), pairs)  31.1 us
    all_to_all x1, blocking collectives, per_device(): parts = lax.all_to_all(total, 'y', 0, 0, tiled=True)  16.9 us
    all_to_all x1, blocking collectives, per_device(): parts = lax.all_to_all(total, 'x', 0, 0, tiled=True)  15.8 us
    ppermute x1, starting transfers between devices, per_device(): return lax.ppermute(block, AXES, homes())  7.28 us
    ppermute x2, starting transfers between devices, fetch(): return lax.ppermute(array, 'z', [((z + by) % PANELS, z) for z in at])  7.18 us
    ppermute x2, waiting for transfers between devices, fetch(): return lax.ppermute(array, 'z', [((z + by) % PANELS, z) for z in at])  5.16 us
    ppermute x6, waiting for transfers between devices, relay(): return lax.ppermute(array, ('core', 'z'), pairs)  2.32 us
    pallas_call x1, Pallas kernels, per_device(): pl.pallas_call(send_kernel, out_shape=(jax.ShapeDtypeStruct(slots, jnp.bf...  2.32 us
  transfers between devices with their start and end apart: 10, of which 5 were waited for; matrix products, arithmetic and copies ran while one was open for 1% of the time, Pallas kernels for 2%

profile of v12, /device:TPU:6, one launch (start us, length us, event | category | flops | bytes accessed | tf_op | source)
XLA Modules:
  0.0 97.4 jit_solution(2806962016666667337)
XLA Ops:
  0.0 4.3 %collective-permute-start.2 = (bf16[384,256]{1,0:T(8,128)(2,1)}, bf16[384,256]{1,0:T(8,128)(2,1)S(1)}, u32[]{:S(2)}, u32[]{:S(2)}) collective-permute-start(bf16[384,256]{1,0:T(8,128)(2,1)} %refs_0_.1), channel_id=1, source_target_pairs={{11,0},{0,1},{1,2},{2,3},{3,4},{4,5},{5,6},{6,7},{7,8},{8,9},{9,10... | collective-permute-start | bytes 589832 | tf_op jit(solution)/shard_map/ppermute | solution.py:246
  4.3 12.2 %collective-permute-start = (bf16[384,256]{1,0:T(8,128)(2,1)}, bf16[384,256]{1,0:T(8,128)(2,1)S(1)}, u32[]{:S(2)}, u32[]{:S(2)}) collective-permute-start(bf16[384,256]{1,0:T(8,128)(2,1)} %refs_0_.1), channel_id=1, source_target_pairs={{1,0},{2,1},{3,2},{4,3},{5,4},{6,5},{7,6},{8,7},{9,8},{10,9},{11,1... | collective-permute-start | bytes 589832 | tf_op jit(solution)/shard_map/ppermute | solution.py:246
  16.5 1.9 %collective-permute-done.2.refs_3_.refs_2_ = bf16[384,256]{1,0:T(8,128)(2,1)S(1)} collective-permute-done((bf16[384,256]{1,0:T(8,128)(2,1)}, bf16[384,256]{1,0:T(8,128)(2,1)S(1)}, u32[]{:S(2)}, u32[]{:S(2)}) %collective-permute-start.2) | collective-permute-done | bytes 196640 | tf_op jit(solution)/shard_map/ppermute | solution.py:246
  18.4 1.9 %collective-permute-start.3 = (bf16[384,256]{1,0:T(8,128)(2,1)S(1)}, bf16[384,256]{1,0:T(8,128)(2,1)S(1)}, u32[]{:S(2)}, u32[]{:S(2)}) collective-permute-start(bf16[384,256]{1,0:T(8,128)(2,1)S(1)} %collective-permute-done.2.refs_3_.refs_2_), channel_id=1, source_target_pairs={{11,0},{0,1},{1,2},{2,3},{3,4},{4,5},{5,6},{6,7},{7,8},{8,9},{9,10... | collective-permute-start | bytes 589832 | tf_op jit(solution)/shard_map/ppermute | solution.py:246
  20.3 0.0 collective-permute-done.refs_1_.refs_4_
  20.4 5.1 %collective-permute-start.1 = (bf16[384,256]{1,0:T(8,128)(2,1)S(1)}, bf16[384,256]{1,0:T(8,128)(2,1)S(1)}, u32[]{:S(2)}, u32[]{:S(2)}) collective-permute-start(bf16[384,256]{1,0:T(8,128)(2,1)S(1)} %collective-permute-done.refs_1_.refs_4_), channel_id=1, source_target_pairs={{1,0},{2,1},{3,2},{4,3},{5,4},{6,5},{7,6},{8,7},{9,8},{10,9},{11,1... | collective-permute-start | bytes 589832 | tf_op jit(solution)/shard_map/ppermute | solution.py:246
  25.5 1.3 %collective-permute-start.7 = (bf16[384,256]{1,0:T(8,128)(2,1)}, bf16[384,256]{1,0:T(8,128)(2,1)S(1)}, u32[]{:S(2)}, u32[]{:S(2)}) collective-permute-start(bf16[384,256]{1,0:T(8,128)(2,1)} %refs_0_.1), channel_id=1, source_target_pairs={{4,0},{7,3},{10,6},{1,9},{16,12},{19,15},{22,18},{13,21},{28,24},{... | collective-permute-start | bytes 589832 | tf_op jit(solution)/shard_map/ppermute | solution.py:239
  26.8 0.4 collective-permute-done.3.refs_4_.refs_1_
  27.2 5.4 %collective-permute-start.5 = (bf16[384,256]{1,0:T(8,128)(2,1)S(1)}, bf16[384,256]{1,0:T(8,128)(2,1)S(1)}, u32[]{:S(2)}, u32[]{:S(2)}) collective-permute-start(bf16[384,256]{1,0:T(8,128)(2,1)S(1)} %collective-permute-done.3.refs_4_.refs_1_), channel_id=1, source_target_pairs={{11,0},{0,1},{1,2},{2,3},{3,4},{4,5},{5,6},{6,7},{7,8},{8,9},{9,10... | collective-permute-start | bytes 589832 | tf_op jit(solution)/shard_map/ppermute | solution.py:246
  32.6 0.0 collective-permute-done.1.refs_2_.refs_5_
  32.6 2.2 %collective-permute-start.6 = (bf16[384,256]{1,0:T(8,128)(2,1)S(1)}, bf16[384,256]{1,0:T(8,128)(2,1)S(1)}, u32[]{:S(2)}, u32[]{:S(2)}) collective-permute-start(bf16[384,256]{1,0:T(8,128)(2,1)S(1)} %collective-permute-done.1.refs_2_.refs_5_), channel_id=1, source_target_pairs={{1,0},{2,1},{3,2},{4,3},{5,4},{6,5},{7,6},{8,7},{9,8},{10,9},{11,1... | collective-permute-start | bytes 589832 | tf_op jit(solution)/shard_map/ppermute | solution.py:246
  34.8 0.0 copy-start
  34.8 0.9 copy-done
  35.7 0.3 sums.1
  36.0 5.9 %collective-permute-start.4 = (f32[8,128]{1,0:T(8,128)S(1)}, f32[8,128]{1,0:T(8,128)S(1)}, u32[]{:S(2)}, u32[]{:S(2)}) collective-permute-start(f32[8,128]{1,0:T(8,128)S(1)} %get-tuple-element.11.near_ref), channel_id=1, source_target_pairs={{6,0},{7,1},{8,2},{9,3},{10,4},{11,5},{0,6},{1,7},{2,8},{3,9},{4,1... | collective-permute-start | bytes 12296 | tf_op jit(solution)/shard_map/ppermute | solution.py:239
  41.9 0.7 concatenate.3.place_ref
  42.6 0.0 collective-permute-done.7.refs_7_
  42.6 5.2 %collective-permute-done.4.far_ref = f32[8,128]{1,0:T(8,128)S(1)} collective-permute-done((f32[8,128]{1,0:T(8,128)S(1)}, f32[8,128]{1,0:T(8,128)S(1)}, u32[]{:S(2)}, u32[]{:S(2)}) %collective-permute-start.4) | collective-permute-done | bytes 4128 | tf_op jit(solution)/shard_map/ppermute | solution.py:239
  47.8 0.0 collective-permute-done.5.refs_0_
  47.8 0.0 collective-permute-done.6.refs_6_
  47.8 2.3 %send.1 = (bf16[32,104,128]{2,1,0:T(8,128)(2,1)S(1)}, f32[384,1]{1,0:T(8,128)S(1)}, f32[8,128]{1,0:T(8,128)S(1)}, f32[8,128]{1,0:T(8,128)S(1)}) custom-call(s32[10]{0:T(128)S(1)} %concatenate.3.place_ref, f32[8,128]{1,0:T(8,128)S(1)} %get-tuple-element.11.near_ref, f32[8,128]{1,0:T(8,128)S(1)} %collective-permute-done.4.far_ref, ...), custom_call_target="tpu_custom_call" | custom-call | flops 301989888 | bytes 1179648 | tf_op jit(solution)/shard_map/send/pallas_call | solution.py:273
  50.1 1.9 %collective-permute-start.8 = (bf16[32,104,128]{2,1,0:T(8,128)(2,1)S(1)}, bf16[32,104,128]{2,1,0:T(8,128)(2,1)S(1)}, u32[]{:S(2)}, u32[]{:S(2)}) collective-permute-start(bf16[32,104,128]{2,1,0:T(8,128)(2,1)S(1)} %get-tuple-element.16), channel_id=1, source_target_pairs={{0,12},{12,0},{1,13},{13,1},{2,14},{14,2},{3,15},{15,3},{4,16},{16... | collective-permute-start | bytes 2555912 | tf_op jit(solution)/shard_map/ppermute | solution.py:288
  52.0 1.4 %keep.1.keep_ref = f32[32,104,128]{2,1,0:T(8,128)S(1)} custom-call(s32[10]{0:T(128)S(1)} %concatenate.3.place_ref, f32[384,1]{1,0:T(8,128)S(1)} %get-tuple-element.13.scale_ref, f32[8,128]{1,0:T(8,128)S(1)} %get-tuple-element.14.row_ref, f32[8,128]{1,0:T(8,128)S(1)} %get-tuple-element.15.column_ref, bf16[384,256]{1,0:T(8,128)(2,1)S(1)} %collective-permute-done.5.refs_0_, ...), custom_call_target="tpu_custom_call" | custom-call | flops 301989888 | bytes 1179648 | tf_op jit(solution)/shard_map/keep/pallas_call | solution.py:289
  53.5 0.9 collective-permute-done.8.got_ref
  54.4 0.2 add.1
  54.6 15.8 %all_to_all.10.got_ref = bf16[32,104,128]{2,1,0:T(8,128)(2,1)S(1)} all-to-all(bf16[32,104,128]{2,1,0:T(8,128)(2,1)S(1)} %add.1), channel_id=1, replica_groups=mesh['x'=4,'y'=8,'core'=2,'z'=12] {'x'}, dimensions={0} | all-to-all | bytes 1703936 | tf_op jit(solution)/shard_map/all_to_all | solution.py:307
  70.4 0.1 fold.1
  70.5 16.9 %all_to_all.11.got_ref = bf16[8,104,128]{2,1,0:T(8,128)(2,1)S(1)} all-to-all(bf16[8,104,128]{2,1,0:T(8,128)(2,1)S(1)} %fold.1), channel_id=1, replica_groups=mesh['x'=4,'y'=8,'core'=2,'z'=12] {'y'}, dimensions={0} | all-to-all | bytes 425984 | tf_op jit(solution)/shard_map/all_to_all | solution.py:316
  87.4 0.7 finish.1
  88.0 7.3 %collective-permute-start.9 = (bf16[48,256]{1,0:T(8,128)(2,1)S(1)}, bf16[48,256]{1,0:T(8,128)(2,1)S(1)}, u32[]{:S(2)}, u32[]{:S(2)}) collective-permute-start(bf16[48,256]{1,0:T(8,128)(2,1)S(1)} %finish.1), channel_id=1, source_target_pairs={{0,592},{1,3},{2,206},{3,7},{4,208},{5,389},{6,211},{7,391},{8,593... | collective-permute-start | bytes 73736 | tf_op jit(solution)/shard_map/ppermute | solution.py:325
  95.3 1.5 %collective-permute-done.9 = bf16[48,256]{1,0:T(8,128)(2,1)S(1)} collective-permute-done((bf16[48,256]{1,0:T(8,128)(2,1)S(1)}, bf16[48,256]{1,0:T(8,128)(2,1)S(1)}, u32[]{:S(2)}, u32[]{:S(2)}) %collective-permute-start.9) | collective-permute-done | bytes 24608 | tf_op jit(solution)/shard_map/ppermute | solution.py:325
  96.8 0.6 copy.4
Async XLA Ops:
  0.0 18.4 %collective-permute-start.2 = (bf16[384,256]{1,0:T(8,128)(2,1)}, bf16[384,256]{1,0:T(8,128)(2,1)S(1)}, u32[]{:S(2)}, u32[]{:S(2)}) collective-permute-start(bf16[384,256]{1,0:T(8,128)(2,1)} %refs_0_.1), channel_id=1, source_target_pairs={{11,0},{0,1},{1,2},{2,3},{3,4},{4,5},{5,6},{6,7},{7,8},{8,9},{9,10... | collective-permute-start | bytes 589832 | tf_op jit(solution)/shard_map/ppermute | solution.py:246
  4.3 16.1 %collective-permute-start = (bf16[384,256]{1,0:T(8,128)(2,1)}, bf16[384,256]{1,0:T(8,128)(2,1)S(1)}, u32[]{:S(2)}, u32[]{:S(2)}) collective-permute-start(bf16[384,256]{1,0:T(8,128)(2,1)} %refs_0_.1), channel_id=1, source_target_pairs={{1,0},{2,1},{3,2},{4,3},{5,4},{6,5},{7,6},{8,7},{9,8},{10,9},{11,1... | collective-permute-start | bytes 589832 | tf_op jit(solution)/shard_map/ppermute | solution.py:246
  18.4 8.8 %collective-permute-start.3 = (bf16[384,256]{1,0:T(8,128)(2,1)S(1)}, bf16[384,256]{1,0:T(8,128)(2,1)S(1)}, u32[]{:S(2)}, u32[]{:S(2)}) collective-permute-start(bf16[384,256]{1,0:T(8,128)(2,1)S(1)} %collective-permute-done.2.refs_3_.refs_2_), channel_id=1, source_target_pairs={{11,0},{0,1},{1,2},{2,3},{3,4},{4,5},{5,6},{6,7},{7,8},{8,9},{9,10... | collective-permute-start | bytes 589832 | tf_op jit(solution)/shard_map/ppermute | solution.py:246
  20.4 12.2 %collective-permute-start.1 = (bf16[384,256]{1,0:T(8,128)(2,1)S(1)}, bf16[384,256]{1,0:T(8,128)(2,1)S(1)}, u32[]{:S(2)}, u32[]{:S(2)}) collective-permute-start(bf16[384,256]{1,0:T(8,128)(2,1)S(1)} %collective-permute-done.refs_1_.refs_4_), channel_id=1, source_target_pairs={{1,0},{2,1},{3,2},{4,3},{5,4},{6,5},{7,6},{8,7},{9,8},{10,9},{11,1... | collective-permute-start | bytes 589832 | tf_op jit(solution)/shard_map/ppermute | solution.py:246
  25.5 17.1 %collective-permute-start.7 = (bf16[384,256]{1,0:T(8,128)(2,1)}, bf16[384,256]{1,0:T(8,128)(2,1)S(1)}, u32[]{:S(2)}, u32[]{:S(2)}) collective-permute-start(bf16[384,256]{1,0:T(8,128)(2,1)} %refs_0_.1), channel_id=1, source_target_pairs={{4,0},{7,3},{10,6},{1,9},{16,12},{19,15},{22,18},{13,21},{28,24},{... | collective-permute-start | bytes 589832 | tf_op jit(solution)/shard_map/ppermute | solution.py:239
  27.2 20.6 %collective-permute-start.5 = (bf16[384,256]{1,0:T(8,128)(2,1)S(1)}, bf16[384,256]{1,0:T(8,128)(2,1)S(1)}, u32[]{:S(2)}, u32[]{:S(2)}) collective-permute-start(bf16[384,256]{1,0:T(8,128)(2,1)S(1)} %collective-permute-done.3.refs_4_.refs_1_), channel_id=1, source_target_pairs={{11,0},{0,1},{1,2},{2,3},{3,4},{4,5},{5,6},{6,7},{7,8},{8,9},{9,10... | collective-permute-start | bytes 589832 | tf_op jit(solution)/shard_map/ppermute | solution.py:246
  32.6 15.2 %collective-permute-start.6 = (bf16[384,256]{1,0:T(8,128)(2,1)S(1)}, bf16[384,256]{1,0:T(8,128)(2,1)S(1)}, u32[]{:S(2)}, u32[]{:S(2)}) collective-permute-start(bf16[384,256]{1,0:T(8,128)(2,1)S(1)} %collective-permute-done.1.refs_2_.refs_5_), channel_id=1, source_target_pairs={{1,0},{2,1},{3,2},{4,3},{5,4},{6,5},{7,6},{8,7},{9,8},{10,9},{11,1... | collective-permute-start | bytes 589832 | tf_op jit(solution)/shard_map/ppermute | solution.py:246
  34.8 0.9 copy-start
  36.0 11.8 %collective-permute-start.4 = (f32[8,128]{1,0:T(8,128)S(1)}, f32[8,128]{1,0:T(8,128)S(1)}, u32[]{:S(2)}, u32[]{:S(2)}) collective-permute-start(f32[8,128]{1,0:T(8,128)S(1)} %get-tuple-element.11.near_ref), channel_id=1, source_target_pairs={{6,0},{7,1},{8,2},{9,3},{10,4},{11,5},{0,6},{1,7},{2,8},{3,9},{4,1... | collective-permute-start | bytes 12296 | tf_op jit(solution)/shard_map/ppermute | solution.py:239
  50.1 4.3 %collective-permute-start.8 = (bf16[32,104,128]{2,1,0:T(8,128)(2,1)S(1)}, bf16[32,104,128]{2,1,0:T(8,128)(2,1)S(1)}, u32[]{:S(2)}, u32[]{:S(2)}) collective-permute-start(bf16[32,104,128]{2,1,0:T(8,128)(2,1)S(1)} %get-tuple-element.16), channel_id=1, source_target_pairs={{0,12},{12,0},{1,13},{13,1},{2,14},{14,2},{3,15},{15,3},{4,16},{16... | collective-permute-start | bytes 2555912 | tf_op jit(solution)/shard_map/ppermute | solution.py:288
  88.0 8.8 %collective-permute-start.9 = (bf16[48,256]{1,0:T(8,128)(2,1)S(1)}, bf16[48,256]{1,0:T(8,128)(2,1)S(1)}, u32[]{:S(2)}, u32[]{:S(2)}) collective-permute-start(bf16[48,256]{1,0:T(8,128)(2,1)S(1)} %finish.1), channel_id=1, source_target_pairs={{0,592},{1,3},{2,206},{3,7},{4,208},{5,389},{6,211},{7,391},{8,593... | collective-permute-start | bytes 73736 | tf_op jit(solution)/shard_map/ppermute | solution.py:325

commit v13 on v12

--- a/solution.py
+++ b/solution.py
@@ -44,10 +44,18 @@
     return rows == lax.broadcasted_iota(jnp.int32, shape, 1)
 
 
+def own_kernel(ratings_ref, own_ref):
+    own_ref[...] = ratings_ref[...]
+
+
+def outer_kernel(low_ref, high_ref, out_ref):
+    low, high = low_ref[...].astype(jnp.float32), high_ref[...].astype(jnp.float32)
+    out_ref[...] = jnp.sum(low * low + high * high, axis=1, keepdims=True)
+
+
 def sums_kernel(*refs):
-    panels, (sums_ref, own_ref) = refs[:-2], refs[-2:]
-    own_ref[...] = panels[0][...]
-    squares = jnp.zeros(own_ref.shape, jnp.float32)
+    panels, sums_ref = refs[:-1], refs[-1]
+    squares = jnp.zeros(panels[0].shape, jnp.float32)
     for ref in panels:
         values = ref[...].astype(jnp.float32)
         squares = squares + values * values
@@ -110,17 +118,13 @@
             out_ref[slot + y] = whole.astype(out_ref.dtype)
 
 
-def send_kernel(place_ref, near_ref, far_ref, *refs):
+def send_kernel(place_ref, near_ref, far_ref, outer_ref, *refs):
     panels, (send_ref, scale_ref, row_ref, column_ref, gram_ref) = refs[:8], refs[8:]
     core, (member, _) = place_ref[2], held(place_ref)
     rows, width = panels[0].shape
-    squares = jnp.zeros((rows, width), jnp.float32)
-    for ref in (panels[0], panels[2 * REACH]):
-        values = ref[...].astype(jnp.float32)
-        squares = squares + values * values
     sums = near_ref[...] + far_ref[...]
     corner = diagonal()
-    square_sum = jnp.sum(squares, axis=1, keepdims=True) + jnp.concatenate(
+    square_sum = outer_ref[...] + jnp.concatenate(
         [
             jnp.sum(jnp.where(corner, sums[i : i + 1], 0.0), axis=1, keepdims=True)
             for i in range(rows // LANES)
@@ -245,23 +249,38 @@
             pairs += [(c * PANELS + (z + shift) % PANELS, c * PANELS + z) for z in range(PANELS)]
         return lax.ppermute(array, ("core", "z"), pairs)
 
+    own = pl.pallas_call(
+        own_kernel,
+        out_shape=jax.ShapeDtypeStruct((rows, width), ratings.dtype),
+        in_specs=[VMEM],
+        out_specs=VMEM,
+        compiler_params=PARAMS,
+        name="own",
+    )(ratings)
     above, below = [ratings], [ratings]
-    for _ in range(REACH):
+    for i in range(REACH):
         above.append(relay(above[-1], 1))
         below.append(relay(below[-1], -1))
+        if i == 0:
+            below[1], own = lax.optimization_barrier((below[1], own))
     last = fetch(ratings, REACH + 1, range(0, PANELS, MEMBERS))
-    near, own = pl.pallas_call(
+    near = pl.pallas_call(
         sums_kernel,
-        out_shape=(
-            jax.ShapeDtypeStruct((8, LANES), jnp.float32),
-            jax.ShapeDtypeStruct((rows, width), ratings.dtype),
-        ),
+        out_shape=jax.ShapeDtypeStruct((8, LANES), jnp.float32),
         in_specs=[VMEM] * 5,
-        out_specs=(VMEM, VMEM),
+        out_specs=VMEM,
         compiler_params=PARAMS,
         name="sums",
-    )(*above[:3], *below[1:3])
+    )(own, *above[1:3], *below[1:3])
     far = fetch(near, PANELS // 2)
+    outer = pl.pallas_call(
+        outer_kernel,
+        out_shape=jax.ShapeDtypeStruct((rows, 1), jnp.float32),
+        in_specs=[VMEM] * 2,
+        out_specs=VMEM,
+        compiler_params=PARAMS,
+        name="outer",
+    )(below[REACH], above[REACH])
     panels = below[:0:-1] + [own] + above[1:] + [last]
 
     slots = (SLOTS, SLOT_ROWS, LANES)
@@ -278,13 +297,13 @@
             lanes,
             lanes,
         ),
-        in_specs=[SMEM] + [VMEM] * 10,
+        in_specs=[SMEM] + [VMEM] * 11,
         out_specs=(VMEM,) * 4,
         scratch_shapes=gram,
         compiler_params=PARAMS,
         cost_estimate=cost,
         name="send",
-    )(place, near, far, *panels)
+    )(place, near, far, outer, *panels)
     got = lax.ppermute(send, "core", [(0, 1), (1, 0)])
     keep = pl.pallas_call(
         keep_kernel,

time: 97.9 us -> 100 us (1.021)
  the two profiles are of different devices: /device:TPU:6 before, /device:TPU:68 now
where the time goes in v13:
time: 100 us; the launch traced here: 99.6 us
  starting transfers between devices  43.3 us (43%)
  blocking collectives  32.2 us (32%)
  waiting for transfers between devices  16.8 us (17%)
  Pallas kernels  4.81 us (5%)
  local copies, waits for them, and re-layouts  2.27 us (2%)
    ppermute x6, starting transfers between devices, relay(): return lax.ppermute(array, ('core', 'z'), pairs)  26 us
    all_to_all x1, blocking collectives, per_device(): parts = lax.all_to_all(total, 'y', 0, 0, tiled=True)  16.9 us
    all_to_all x1, blocking collectives, per_device(): parts = lax.all_to_all(total, 'x', 0, 0, tiled=True)  15.4 us
    ppermute x2, starting transfers between devices, fetch(): return lax.ppermute(array, 'z', [((z + by) % PANELS, z) for z in at])  10.9 us
    ppermute x2, waiting for transfers between devices, fetch(): return lax.ppermute(array, 'z', [((z + by) % PANELS, z) for z in at])  7.13 us
    ppermute x1, waiting for transfers between devices, per_device(): return lax.ppermute(block, AXES, homes())  5.15 us
    ppermute x1, starting transfers between devices, per_device(): return lax.ppermute(block, AXES, homes())  4.47 us
    ppermute x6, waiting for transfers between devices, relay(): return lax.ppermute(array, ('core', 'z'), pairs)  3.65 us
  transfers between devices with their start and end apart: 10, of which 6 were waited for; matrix products, arithmetic and copies ran while one was open for 1% of the time, Pallas kernels for 2%

profile of v13, /device:TPU:68, one launch (start us, length us, event | category | flops | bytes accessed | tf_op | source)
XLA Modules:
  0.0 99.6 jit_solution(17978553783387959940)
XLA Ops:
  0.0 4.3 %collective-permute-start = (bf16[384,256]{1,0:T(8,128)(2,1)}, bf16[384,256]{1,0:T(8,128)(2,1)S(1)}, u32[]{:S(2)}, u32[]{:S(2)}) collective-permute-start(bf16[384,256]{1,0:T(8,128)(2,1)} %ratings_ref.1), channel_id=1, source_target_pairs={{11,0},{0,1},{1,2},{2,3},{3,4},{4,5},{5,6},{6,7},{7,8},{8,9},{9,10... | collective-permute-start | bytes 589832 | tf_op jit(solution)/shard_map/ppermute | solution.py:250
  4.3 1.9 %collective-permute-start.1 = (bf16[384,256]{1,0:T(8,128)(2,1)}, bf16[384,256]{1,0:T(8,128)(2,1)S(1)}, u32[]{:S(2)}, u32[]{:S(2)}) collective-permute-start(bf16[384,256]{1,0:T(8,128)(2,1)} %ratings_ref.1), channel_id=1, source_target_pairs={{1,0},{2,1},{3,2},{4,3},{5,4},{6,5},{7,6},{8,7},{9,8},{10,9},{11,1... | collective-permute-start | bytes 589832 | tf_op jit(solution)/shard_map/ppermute | solution.py:250
  6.2 0.0 copy-start
  6.2 0.9 copy-done
  7.2 1.9 %collective-permute-done.refs_3_.refs_2_ = bf16[384,256]{1,0:T(8,128)(2,1)S(1)} collective-permute-done((bf16[384,256]{1,0:T(8,128)(2,1)}, bf16[384,256]{1,0:T(8,128)(2,1)S(1)}, u32[]{:S(2)}, u32[]{:S(2)}) %collective-permute-start) | collective-permute-done | bytes 196640 | tf_op jit(solution)/shard_map/ppermute | solution.py:250
  9.1 4.3 %collective-permute-start.3 = (bf16[384,256]{1,0:T(8,128)(2,1)S(1)}, bf16[384,256]{1,0:T(8,128)(2,1)S(1)}, u32[]{:S(2)}, u32[]{:S(2)}) collective-permute-start(bf16[384,256]{1,0:T(8,128)(2,1)S(1)} %collective-permute-done.refs_3_.refs_2_), channel_id=1, source_target_pairs={{11,0},{0,1},{1,2},{2,3},{3,4},{4,5},{5,6},{6,7},{7,8},{8,9},{9,10... | collective-permute-start | bytes 589832 | tf_op jit(solution)/shard_map/ppermute | solution.py:250
  13.4 0.0 collective-permute-done.1.refs_1_.refs_4_
  13.4 8.5 %collective-permute-start.2 = (bf16[384,256]{1,0:T(8,128)(2,1)S(1)}, bf16[384,256]{1,0:T(8,128)(2,1)S(1)}, u32[]{:S(2)}, u32[]{:S(2)}) collective-permute-start(bf16[384,256]{1,0:T(8,128)(2,1)S(1)} %collective-permute-done.1.refs_1_.refs_4_), channel_id=1, source_target_pairs={{1,0},{2,1},{3,2},{4,3},{5,4},{6,5},{7,6},{8,7},{9,8},{10,9},{11,1... | collective-permute-start | bytes 589832 | tf_op jit(solution)/shard_map/ppermute | solution.py:250
  21.9 1.7 %collective-permute-done.3.refs_4_.refs_1_ = bf16[384,256]{1,0:T(8,128)(2,1)S(1)} collective-permute-done((bf16[384,256]{1,0:T(8,128)(2,1)S(1)}, bf16[384,256]{1,0:T(8,128)(2,1)S(1)}, u32[]{:S(2)}, u32[]{:S(2)}) %collective-permute-start.3) | collective-permute-done | bytes 196640 | tf_op jit(solution)/shard_map/ppermute | solution.py:250
  23.6 1.9 %collective-permute-start.5 = (bf16[384,256]{1,0:T(8,128)(2,1)S(1)}, bf16[384,256]{1,0:T(8,128)(2,1)S(1)}, u32[]{:S(2)}, u32[]{:S(2)}) collective-permute-start(bf16[384,256]{1,0:T(8,128)(2,1)S(1)} %collective-permute-done.3.refs_4_.refs_1_), channel_id=1, source_target_pairs={{11,0},{0,1},{1,2},{2,3},{3,4},{4,5},{5,6},{6,7},{7,8},{8,9},{9,10... | collective-permute-start | bytes 589832 | tf_op jit(solution)/shard_map/ppermute | solution.py:250
  25.5 0.0 collective-permute-done.2.refs_2_.refs_5_
  25.5 5.1 %collective-permute-start.6 = (bf16[384,256]{1,0:T(8,128)(2,1)S(1)}, bf16[384,256]{1,0:T(8,128)(2,1)S(1)}, u32[]{:S(2)}, u32[]{:S(2)}) collective-permute-start(bf16[384,256]{1,0:T(8,128)(2,1)S(1)} %collective-permute-done.2.refs_2_.refs_5_), channel_id=1, source_target_pairs={{1,0},{2,1},{3,2},{4,3},{5,4},{6,5},{7,6},{8,7},{9,8},{10,9},{11,1... | collective-permute-start | bytes 589832 | tf_op jit(solution)/shard_map/ppermute | solution.py:250
  30.7 7.0 %collective-permute-start.7 = (bf16[384,256]{1,0:T(8,128)(2,1)}, bf16[384,256]{1,0:T(8,128)(2,1)S(1)}, u32[]{:S(2)}, u32[]{:S(2)}) collective-permute-start(bf16[384,256]{1,0:T(8,128)(2,1)} %ratings_ref.1), channel_id=1, source_target_pairs={{4,0},{7,3},{10,6},{1,9},{16,12},{19,15},{22,18},{13,21},{28,24},{... | collective-permute-start | bytes 589832 | tf_op jit(solution)/shard_map/ppermute | solution.py:243
  37.7 0.3 sums.1.near_ref
  38.0 3.9 %collective-permute-start.4 = (f32[8,128]{1,0:T(8,128)S(1)}, f32[8,128]{1,0:T(8,128)S(1)}, u32[]{:S(2)}, u32[]{:S(2)}) collective-permute-start(f32[8,128]{1,0:T(8,128)S(1)} %sums.1.near_ref), channel_id=1, source_target_pairs={{6,0},{7,1},{8,2},{9,3},{10,4},{11,5},{0,6},{1,7},{2,8},{3,9},{4,1... | collective-permute-start | bytes 12296 | tf_op jit(solution)/shard_map/ppermute | solution.py:243
  41.9 0.7 concatenate.3.place_ref
  42.6 0.0 collective-permute-done.5.low_ref.refs_0_
  42.6 0.0 collective-permute-done.6.high_ref.refs_6_
  42.6 0.1 outer.1.outer_ref
  42.8 1.2 %collective-permute-done.7.refs_7_ = bf16[384,256]{1,0:T(8,128)(2,1)S(1)} collective-permute-done((bf16[384,256]{1,0:T(8,128)(2,1)}, bf16[384,256]{1,0:T(8,128)(2,1)S(1)}, u32[]{:S(2)}, u32[]{:S(2)}) %collective-permute-start.7) | collective-permute-done | bytes 196640 | tf_op jit(solution)/shard_map/ppermute | solution.py:243
  44.0 5.9 %collective-permute-done.4.far_ref = f32[8,128]{1,0:T(8,128)S(1)} collective-permute-done((f32[8,128]{1,0:T(8,128)S(1)}, f32[8,128]{1,0:T(8,128)S(1)}, u32[]{:S(2)}, u32[]{:S(2)}) %collective-permute-start.4) | collective-permute-done | bytes 4128 | tf_op jit(solution)/shard_map/ppermute | solution.py:243
  49.9 2.0 %send.1 = (bf16[32,104,128]{2,1,0:T(8,128)(2,1)S(1)}, f32[384,1]{1,0:T(8,128)S(1)}, f32[8,128]{1,0:T(8,128)S(1)}, f32[8,128]{1,0:T(8,128)S(1)}) custom-call(s32[10]{0:T(128)S(1)} %concatenate.3.place_ref, f32[8,128]{1,0:T(8,128)S(1)} %sums.1.near_ref, f32[8,128]{1,0:T(8,128)S(1)} %collective-permute-done.4.far_ref, f32[384,1]{1,0:T(8,128)S(1)} %outer.1.outer_ref, ...), custom_call_target="tpu_custom_call" | custom-call | flops 301989888 | bytes 1179648 | tf_op jit(solution)/shard_map/send/pallas_call | solution.py:292
  51.9 1.9 %collective-permute-start.8 = (bf16[32,104,128]{2,1,0:T(8,128)(2,1)S(1)}, bf16[32,104,128]{2,1,0:T(8,128)(2,1)S(1)}, u32[]{:S(2)}, u32[]{:S(2)}) collective-permute-start(bf16[32,104,128]{2,1,0:T(8,128)(2,1)S(1)} %get-tuple-element.16), channel_id=1, source_target_pairs={{0,12},{12,0},{1,13},{13,1},{2,14},{14,2},{3,15},{15,3},{4,16},{16... | collective-permute-start | bytes 2555912 | tf_op jit(solution)/shard_map/ppermute | solution.py:307
  53.8 1.5 %keep.1.keep_ref = f32[32,104,128]{2,1,0:T(8,128)S(1)} custom-call(s32[10]{0:T(128)S(1)} %concatenate.3.place_ref, f32[384,1]{1,0:T(8,128)S(1)} %get-tuple-element.13.scale_ref, f32[8,128]{1,0:T(8,128)S(1)} %get-tuple-element.14.row_ref, f32[8,128]{1,0:T(8,128)S(1)} %get-tuple-element.15.column_ref, ...), custom_call_target="tpu_custom_call" | custom-call | flops 301989888 | bytes 1179648 | tf_op jit(solution)/shard_map/keep/pallas_call | solution.py:308
  55.3 0.9 collective-permute-done.8.got_ref
  56.2 0.2 add.1
  56.3 15.4 %all_to_all.10.got_ref = bf16[32,104,128]{2,1,0:T(8,128)(2,1)S(1)} all-to-all(bf16[32,104,128]{2,1,0:T(8,128)(2,1)S(1)} %add.1), channel_id=1, replica_groups=mesh['x'=4,'y'=8,'core'=2,'z'=12] {'x'}, dimensions={0} | all-to-all | bytes 1703936 | tf_op jit(solution)/shard_map/all_to_all | solution.py:326
  71.7 0.1 fold.1
  71.8 16.9 %all_to_all.11.got_ref = bf16[8,104,128]{2,1,0:T(8,128)(2,1)S(1)} all-to-all(bf16[8,104,128]{2,1,0:T(8,128)(2,1)S(1)} %fold.1), channel_id=1, replica_groups=mesh['x'=4,'y'=8,'core'=2,'z'=12] {'y'}, dimensions={0} | all-to-all | bytes 425984 | tf_op jit(solution)/shard_map/all_to_all | solution.py:335
  88.7 0.7 finish.1
  89.3 4.5 %collective-permute-start.9 = (bf16[48,256]{1,0:T(8,128)(2,1)S(1)}, bf16[48,256]{1,0:T(8,128)(2,1)S(1)}, u32[]{:S(2)}, u32[]{:S(2)}) collective-permute-start(bf16[48,256]{1,0:T(8,128)(2,1)S(1)} %finish.1), channel_id=1, source_target_pairs={{0,592},{1,3},{2,206},{3,7},{4,208},{5,389},{6,211},{7,391},{8,593... | collective-permute-start | bytes 73736 | tf_op jit(solution)/shard_map/ppermute | solution.py:344
  93.8 5.2 %collective-permute-done.9 = bf16[48,256]{1,0:T(8,128)(2,1)S(1)} collective-permute-done((bf16[48,256]{1,0:T(8,128)(2,1)S(1)}, bf16[48,256]{1,0:T(8,128)(2,1)S(1)}, u32[]{:S(2)}, u32[]{:S(2)}) %collective-permute-start.9) | collective-permute-done | bytes 24608 | tf_op jit(solution)/shard_map/ppermute | solution.py:344
  99.0 0.6 copy.4
  (1 shorter events, 0.0 us)
Async XLA Ops:
  0.0 9.1 %collective-permute-start = (bf16[384,256]{1,0:T(8,128)(2,1)}, bf16[384,256]{1,0:T(8,128)(2,1)S(1)}, u32[]{:S(2)}, u32[]{:S(2)}) collective-permute-start(bf16[384,256]{1,0:T(8,128)(2,1)} %ratings_ref.1), channel_id=1, source_target_pairs={{11,0},{0,1},{1,2},{2,3},{3,4},{4,5},{5,6},{6,7},{7,8},{8,9},{9,10... | collective-permute-start | bytes 589832 | tf_op jit(solution)/shard_map/ppermute | solution.py:250
  4.3 9.1 %collective-permute-start.1 = (bf16[384,256]{1,0:T(8,128)(2,1)}, bf16[384,256]{1,0:T(8,128)(2,1)S(1)}, u32[]{:S(2)}, u32[]{:S(2)}) collective-permute-start(bf16[384,256]{1,0:T(8,128)(2,1)} %ratings_ref.1), channel_id=1, source_target_pairs={{1,0},{2,1},{3,2},{4,3},{5,4},{6,5},{7,6},{8,7},{9,8},{10,9},{11,1... | collective-permute-start | bytes 589832 | tf_op jit(solution)/shard_map/ppermute | solution.py:250
  6.2 0.9 copy-start
  9.1 14.5 %collective-permute-start.3 = (bf16[384,256]{1,0:T(8,128)(2,1)S(1)}, bf16[384,256]{1,0:T(8,128)(2,1)S(1)}, u32[]{:S(2)}, u32[]{:S(2)}) collective-permute-start(bf16[384,256]{1,0:T(8,128)(2,1)S(1)} %collective-permute-done.refs_3_.refs_2_), channel_id=1, source_target_pairs={{11,0},{0,1},{1,2},{2,3},{3,4},{4,5},{5,6},{6,7},{7,8},{8,9},{9,10... | collective-permute-start | bytes 589832 | tf_op jit(solution)/shard_map/ppermute | solution.py:250
  13.4 12.1 %collective-permute-start.2 = (bf16[384,256]{1,0:T(8,128)(2,1)S(1)}, bf16[384,256]{1,0:T(8,128)(2,1)S(1)}, u32[]{:S(2)}, u32[]{:S(2)}) collective-permute-start(bf16[384,256]{1,0:T(8,128)(2,1)S(1)} %collective-permute-done.1.refs_1_.refs_4_), channel_id=1, source_target_pairs={{1,0},{2,1},{3,2},{4,3},{5,4},{6,5},{7,6},{8,7},{9,8},{10,9},{11,1... | collective-permute-start | bytes 589832 | tf_op jit(solution)/shard_map/ppermute | solution.py:250
  23.6 19.0 %collective-permute-start.5 = (bf16[384,256]{1,0:T(8,128)(2,1)S(1)}, bf16[384,256]{1,0:T(8,128)(2,1)S(1)}, u32[]{:S(2)}, u32[]{:S(2)}) collective-permute-start(bf16[384,256]{1,0:T(8,128)(2,1)S(1)} %collective-permute-done.3.refs_4_.refs_1_), channel_id=1, source_target_pairs={{11,0},{0,1},{1,2},{2,3},{3,4},{4,5},{5,6},{6,7},{7,8},{8,9},{9,10... | collective-permute-start | bytes 589832 | tf_op jit(solution)/shard_map/ppermute | solution.py:250
  25.5 17.1 %collective-permute-start.6 = (bf16[384,256]{1,0:T(8,128)(2,1)S(1)}, bf16[384,256]{1,0:T(8,128)(2,1)S(1)}, u32[]{:S(2)}, u32[]{:S(2)}) collective-permute-start(bf16[384,256]{1,0:T(8,128)(2,1)S(1)} %collective-permute-done.2.refs_2_.refs_5_), channel_id=1, source_target_pairs={{1,0},{2,1},{3,2},{4,3},{5,4},{6,5},{7,6},{8,7},{9,8},{10,9},{11,1... | collective-permute-start | bytes 589832 | tf_op jit(solution)/shard_map/ppermute | solution.py:250
  30.7 13.4 %collective-permute-start.7 = (bf16[384,256]{1,0:T(8,128)(2,1)}, bf16[384,256]{1,0:T(8,128)(2,1)S(1)}, u32[]{:S(2)}, u32[]{:S(2)}) collective-permute-start(bf16[384,256]{1,0:T(8,128)(2,1)} %ratings_ref.1), channel_id=1, source_target_pairs={{4,0},{7,3},{10,6},{1,9},{16,12},{19,15},{22,18},{13,21},{28,24},{... | collective-permute-start | bytes 589832 | tf_op jit(solution)/shard_map/ppermute | solution.py:243
  38.0 11.9 %collective-permute-start.4 = (f32[8,128]{1,0:T(8,128)S(1)}, f32[8,128]{1,0:T(8,128)S(1)}, u32[]{:S(2)}, u32[]{:S(2)}) collective-permute-start(f32[8,128]{1,0:T(8,128)S(1)} %sums.1.near_ref), channel_id=1, source_target_pairs={{6,0},{7,1},{8,2},{9,3},{10,4},{11,5},{0,6},{1,7},{2,8},{3,9},{4,1... | collective-permute-start | bytes 12296 | tf_op jit(solution)/shard_map/ppermute | solution.py:243
  51.9 4.3 %collective-permute-start.8 = (bf16[32,104,128]{2,1,0:T(8,128)(2,1)S(1)}, bf16[32,104,128]{2,1,0:T(8,128)(2,1)S(1)}, u32[]{:S(2)}, u32[]{:S(2)}) collective-permute-start(bf16[32,104,128]{2,1,0:T(8,128)(2,1)S(1)} %get-tuple-element.16), channel_id=1, source_target_pairs={{0,12},{12,0},{1,13},{13,1},{2,14},{14,2},{3,15},{15,3},{4,16},{16... | collective-permute-start | bytes 2555912 | tf_op jit(solution)/shard_map/ppermute | solution.py:307
  89.3 9.6 %collective-permute-start.9 = (bf16[48,256]{1,0:T(8,128)(2,1)S(1)}, bf16[48,256]{1,0:T(8,128)(2,1)S(1)}, u32[]{:S(2)}, u32[]{:S(2)}) collective-permute-start(bf16[48,256]{1,0:T(8,128)(2,1)S(1)} %finish.1), channel_id=1, source_target_pairs={{0,592},{1,3},{2,206},{3,7},{4,208},{5,389},{6,211},{7,391},{8,593... | collective-permute-start | bytes 73736 | tf_op jit(solution)/shard_map/ppermute | solution.py:344

commit v14 on v13

--- a/solution.py
+++ b/solution.py
@@ -46,11 +46,6 @@
 
 def own_kernel(ratings_ref, own_ref):
     own_ref[...] = ratings_ref[...]
-
-
-def outer_kernel(low_ref, high_ref, out_ref):
-    low, high = low_ref[...].astype(jnp.float32), high_ref[...].astype(jnp.float32)
-    out_ref[...] = jnp.sum(low * low + high * high, axis=1, keepdims=True)
 
 
 def sums_kernel(*refs):
@@ -118,13 +113,17 @@
             out_ref[slot + y] = whole.astype(out_ref.dtype)
 
 
-def send_kernel(place_ref, near_ref, far_ref, outer_ref, *refs):
+def send_kernel(place_ref, near_ref, far_ref, *refs):
     panels, (send_ref, scale_ref, row_ref, column_ref, gram_ref) = refs[:8], refs[8:]
     core, (member, _) = place_ref[2], held(place_ref)
     rows, width = panels[0].shape
+    squares = jnp.zeros((rows, width), jnp.float32)
+    for ref in (panels[0], panels[2 * REACH]):
+        values = ref[...].astype(jnp.float32)
+        squares = squares + values * values
     sums = near_ref[...] + far_ref[...]
     corner = diagonal()
-    square_sum = outer_ref[...] + jnp.concatenate(
+    square_sum = jnp.sum(squares, axis=1, keepdims=True) + jnp.concatenate(
         [
             jnp.sum(jnp.where(corner, sums[i : i + 1], 0.0), axis=1, keepdims=True)
             for i in range(rows // LANES)
@@ -273,14 +272,6 @@
         name="sums",
     )(own, *above[1:3], *below[1:3])
     far = fetch(near, PANELS // 2)
-    outer = pl.pallas_call(
-        outer_kernel,
-        out_shape=jax.ShapeDtypeStruct((rows, 1), jnp.float32),
-        in_specs=[VMEM] * 2,
-        out_specs=VMEM,
-        compiler_params=PARAMS,
-        name="outer",
-    )(below[REACH], above[REACH])
     panels = below[:0:-1] + [own] + above[1:] + [last]
 
     slots = (SLOTS, SLOT_ROWS, LANES)
@@ -297,13 +288,13 @@
             lanes,
             lanes,
         ),
-        in_specs=[SMEM] + [VMEM] * 11,
+        in_specs=[SMEM] + [VMEM] * 10,
         out_specs=(VMEM,) * 4,
         scratch_shapes=gram,
         compiler_params=PARAMS,
         cost_estimate=cost,
         name="send",
-    )(place, near, far, outer, *panels)
+    )(place, near, far, *panels)
     got = lax.ppermute(send, "core", [(0, 1), (1, 0)])
     keep = pl.pallas_call(
         keep_kernel,

time: 100 us -> 97 us (0.970)
  the two profiles are of different devices: /device:TPU:68 before, /device:TPU:6 now
where the time goes in v14:
time: 97 us; the launch traced here: 96.5 us
  starting transfers between devices  47.5 us (49%)
  blocking collectives  32.7 us (34%)
  waiting for transfers between devices  8.89 us (9%)
  Pallas kernels  5.95 us (6%)
  local copies, waits for them, and re-layouts  1.34 us (1%)
    ppermute x6, starting transfers between devices, relay(): return lax.ppermute(array, ('core', 'z'), pairs)  31.1 us
    all_to_all x1, blocking collectives, per_device(): parts = lax.all_to_all(total, 'y', 0, 0, tiled=True)  16.9 us
    all_to_all x1, blocking collectives, per_device(): parts = lax.all_to_all(total, 'x', 0, 0, tiled=True)  15.8 us
    ppermute x1, starting transfers between devices, per_device(): return lax.ppermute(block, AXES, homes())  7.3 us
    ppermute x2, starting transfers between devices, fetch(): return lax.ppermute(array, 'z', [((z + by) % PANELS, z) for z in at])  7.2 us
    ppermute x2, waiting for transfers between devices, fetch(): return lax.ppermute(array, 'z', [((z + by) % PANELS, z) for z in at])  5.14 us
    pallas_call x1, Pallas kernels, per_device(): pl.pallas_call(send_kernel, out_shape=(jax.ShapeDtypeStruct(slots, jnp.bf...  2.31 us
  transfers between devices with their start and end apart: 10, of which 5 were waited for; matrix products, arithmetic and copies ran while one was open for 1% of the time, Pallas kernels for 3%

profile of v14, /device:TPU:6, one launch (start us, length us, event | category | flops | bytes accessed | tf_op | source)
XLA Modules:
  0.0 96.5 jit_solution(16540152600941751397)
XLA Ops:
  0.0 4.3 %collective-permute-start = (bf16[384,256]{1,0:T(8,128)(2,1)}, bf16[384,256]{1,0:T(8,128)(2,1)S(1)}, u32[]{:S(2)}, u32[]{:S(2)}) collective-permute-start(bf16[384,256]{1,0:T(8,128)(2,1)} %ratings_ref.1), channel_id=1, source_target_pairs={{11,0},{0,1},{1,2},{2,3},{3,4},{4,5},{5,6},{6,7},{7,8},{8,9},{9,10... | collective-permute-start | bytes 589832 | tf_op jit(solution)/shard_map/ppermute | solution.py:249
  4.3 12.2 %collective-permute-start.1 = (bf16[384,256]{1,0:T(8,128)(2,1)}, bf16[384,256]{1,0:T(8,128)(2,1)S(1)}, u32[]{:S(2)}, u32[]{:S(2)}) collective-permute-start(bf16[384,256]{1,0:T(8,128)(2,1)} %ratings_ref.1), channel_id=1, source_target_pairs={{1,0},{2,1},{3,2},{4,3},{5,4},{6,5},{7,6},{8,7},{9,8},{10,9},{11,1... | collective-permute-start | bytes 589832 | tf_op jit(solution)/shard_map/ppermute | solution.py:249
  16.5 1.0 own.1.refs_0_.refs_3_
  17.5 1.0 collective-permute-done.refs_3_.refs_2_
  18.4 1.9 %collective-permute-start.3 = (bf16[384,256]{1,0:T(8,128)(2,1)S(1)}, bf16[384,256]{1,0:T(8,128)(2,1)S(1)}, u32[]{:S(2)}, u32[]{:S(2)}) collective-permute-start(bf16[384,256]{1,0:T(8,128)(2,1)S(1)} %collective-permute-done.refs_3_.refs_2_), channel_id=1, source_target_pairs={{11,0},{0,1},{1,2},{2,3},{3,4},{4,5},{5,6},{6,7},{7,8},{8,9},{9,10... | collective-permute-start | bytes 589832 | tf_op jit(solution)/shard_map/ppermute | solution.py:249
  20.3 0.0 collective-permute-done.1.refs_1_.refs_4_
  20.4 5.1 %collective-permute-start.2 = (bf16[384,256]{1,0:T(8,128)(2,1)S(1)}, bf16[384,256]{1,0:T(8,128)(2,1)S(1)}, u32[]{:S(2)}, u32[]{:S(2)}) collective-permute-start(bf16[384,256]{1,0:T(8,128)(2,1)S(1)} %collective-permute-done.1.refs_1_.refs_4_), channel_id=1, source_target_pairs={{1,0},{2,1},{3,2},{4,3},{5,4},{6,5},{7,6},{8,7},{9,8},{10,9},{11,1... | collective-permute-start | bytes 589832 | tf_op jit(solution)/shard_map/ppermute | solution.py:249
  25.5 1.3 %collective-permute-start.7 = (bf16[384,256]{1,0:T(8,128)(2,1)}, bf16[384,256]{1,0:T(8,128)(2,1)S(1)}, u32[]{:S(2)}, u32[]{:S(2)}) collective-permute-start(bf16[384,256]{1,0:T(8,128)(2,1)} %ratings_ref.1), channel_id=1, source_target_pairs={{4,0},{7,3},{10,6},{1,9},{16,12},{19,15},{22,18},{13,21},{28,24},{... | collective-permute-start | bytes 589832 | tf_op jit(solution)/shard_map/ppermute | solution.py:242
  26.8 0.4 collective-permute-done.3.refs_4_.refs_1_
  27.2 5.4 %collective-permute-start.5 = (bf16[384,256]{1,0:T(8,128)(2,1)S(1)}, bf16[384,256]{1,0:T(8,128)(2,1)S(1)}, u32[]{:S(2)}, u32[]{:S(2)}) collective-permute-start(bf16[384,256]{1,0:T(8,128)(2,1)S(1)} %collective-permute-done.3.refs_4_.refs_1_), channel_id=1, source_target_pairs={{11,0},{0,1},{1,2},{2,3},{3,4},{4,5},{5,6},{6,7},{7,8},{8,9},{9,10... | collective-permute-start | bytes 589832 | tf_op jit(solution)/shard_map/ppermute | solution.py:249
  32.6 0.0 collective-permute-done.2.refs_2_.refs_5_
  32.6 2.2 %collective-permute-start.6 = (bf16[384,256]{1,0:T(8,128)(2,1)S(1)}, bf16[384,256]{1,0:T(8,128)(2,1)S(1)}, u32[]{:S(2)}, u32[]{:S(2)}) collective-permute-start(bf16[384,256]{1,0:T(8,128)(2,1)S(1)} %collective-permute-done.2.refs_2_.refs_5_), channel_id=1, source_target_pairs={{1,0},{2,1},{3,2},{4,3},{5,4},{6,5},{7,6},{8,7},{9,8},{10,9},{11,1... | collective-permute-start | bytes 589832 | tf_op jit(solution)/shard_map/ppermute | solution.py:249
  34.8 0.3 sums.1.near_ref
  35.0 5.9 %collective-permute-start.4 = (f32[8,128]{1,0:T(8,128)S(1)}, f32[8,128]{1,0:T(8,128)S(1)}, u32[]{:S(2)}, u32[]{:S(2)}) collective-permute-start(f32[8,128]{1,0:T(8,128)S(1)} %sums.1.near_ref), channel_id=1, source_target_pairs={{6,0},{7,1},{8,2},{9,3},{10,4},{11,5},{0,6},{1,7},{2,8},{3,9},{4,1... | collective-permute-start | bytes 12296 | tf_op jit(solution)/shard_map/ppermute | solution.py:242
  41.0 0.7 concatenate.3.place_ref
  41.7 0.0 collective-permute-done.7.refs_7_
  41.7 5.1 %collective-permute-done.4.far_ref = f32[8,128]{1,0:T(8,128)S(1)} collective-permute-done((f32[8,128]{1,0:T(8,128)S(1)}, f32[8,128]{1,0:T(8,128)S(1)}, u32[]{:S(2)}, u32[]{:S(2)}) %collective-permute-start.4) | collective-permute-done | bytes 4128 | tf_op jit(solution)/shard_map/ppermute | solution.py:242
  46.9 0.0 collective-permute-done.5.refs_0_
  46.9 0.0 collective-permute-done.6.refs_6_
  46.9 2.3 %send.1 = (bf16[32,104,128]{2,1,0:T(8,128)(2,1)S(1)}, f32[384,1]{1,0:T(8,128)S(1)}, f32[8,128]{1,0:T(8,128)S(1)}, f32[8,128]{1,0:T(8,128)S(1)}) custom-call(s32[10]{0:T(128)S(1)} %concatenate.3.place_ref, f32[8,128]{1,0:T(8,128)S(1)} %sums.1.near_ref, f32[8,128]{1,0:T(8,128)S(1)} %collective-permute-done.4.far_ref, ...), custom_call_target="tpu_custom_call" | custom-call | flops 301989888 | bytes 1179648 | tf_op jit(solution)/shard_map/send/pallas_call | solution.py:283
  49.2 1.9 %collective-permute-start.8 = (bf16[32,104,128]{2,1,0:T(8,128)(2,1)S(1)}, bf16[32,104,128]{2,1,0:T(8,128)(2,1)S(1)}, u32[]{:S(2)}, u32[]{:S(2)}) collective-permute-start(bf16[32,104,128]{2,1,0:T(8,128)(2,1)S(1)} %get-tuple-element.16), channel_id=1, source_target_pairs={{0,12},{12,0},{1,13},{13,1},{2,14},{14,2},{3,15},{15,3},{4,16},{16... | collective-permute-start | bytes 2555912 | tf_op jit(solution)/shard_map/ppermute | solution.py:298
  51.1 1.4 %keep.1.keep_ref = f32[32,104,128]{2,1,0:T(8,128)S(1)} custom-call(s32[10]{0:T(128)S(1)} %concatenate.3.place_ref, f32[384,1]{1,0:T(8,128)S(1)} %get-tuple-element.13.scale_ref, f32[8,128]{1,0:T(8,128)S(1)} %get-tuple-element.14.row_ref, f32[8,128]{1,0:T(8,128)S(1)} %get-tuple-element.15.column_ref, bf16[384,256]{1,0:T(8,128)(2,1)S(1)} %collective-permute-done.5.refs_0_, ...), custom_call_target="tpu_custom_call" | custom-call | flops 301989888 | bytes 1179648 | tf_op jit(solution)/shard_map/keep/pallas_call | solution.py:299
  52.6 0.9 collective-permute-done.8.got_ref
  53.4 0.2 add.1
  53.6 15.8 %all_to_all.10.got_ref = bf16[32,104,128]{2,1,0:T(8,128)(2,1)S(1)} all-to-all(bf16[32,104,128]{2,1,0:T(8,128)(2,1)S(1)} %add.1), channel_id=1, replica_groups=mesh['x'=4,'y'=8,'core'=2,'z'=12] {'x'}, dimensions={0} | all-to-all | bytes 1703936 | tf_op jit(solution)/shard_map/all_to_all | solution.py:317
  69.4 0.1 fold.1
  69.5 16.9 %all_to_all.11.got_ref = bf16[8,104,128]{2,1,0:T(8,128)(2,1)S(1)} all-to-all(bf16[8,104,128]{2,1,0:T(8,128)(2,1)S(1)} %fold.1), channel_id=1, replica_groups=mesh['x'=4,'y'=8,'core'=2,'z'=12] {'y'}, dimensions={0} | all-to-all | bytes 425984 | tf_op jit(solution)/shard_map/all_to_all | solution.py:326
  86.4 0.7 finish.1
  87.1 7.3 %collective-permute-start.9 = (bf16[48,256]{1,0:T(8,128)(2,1)S(1)}, bf16[48,256]{1,0:T(8,128)(2,1)S(1)}, u32[]{:S(2)}, u32[]{:S(2)}) collective-permute-start(bf16[48,256]{1,0:T(8,128)(2,1)S(1)} %finish.1), channel_id=1, source_target_pairs={{0,592},{1,3},{2,206},{3,7},{4,208},{5,389},{6,211},{7,391},{8,593... | collective-permute-start | bytes 73736 | tf_op jit(solution)/shard_map/ppermute | solution.py:335
  94.4 1.5 %collective-permute-done.9 = bf16[48,256]{1,0:T(8,128)(2,1)S(1)} collective-permute-done((bf16[48,256]{1,0:T(8,128)(2,1)S(1)}, bf16[48,256]{1,0:T(8,128)(2,1)S(1)}, u32[]{:S(2)}, u32[]{:S(2)}) %collective-permute-start.9) | collective-permute-done | bytes 24608 | tf_op jit(solution)/shard_map/ppermute | solution.py:335
  95.9 0.6 copy.4
Async XLA Ops:
  0.0 18.4 %collective-permute-start = (bf16[384,256]{1,0:T(8,128)(2,1)}, bf16[384,256]{1,0:T(8,128)(2,1)S(1)}, u32[]{:S(2)}, u32[]{:S(2)}) collective-permute-start(bf16[384,256]{1,0:T(8,128)(2,1)} %ratings_ref.1), channel_id=1, source_target_pairs={{11,0},{0,1},{1,2},{2,3},{3,4},{4,5},{5,6},{6,7},{7,8},{8,9},{9,10... | collective-permute-start | bytes 589832 | tf_op jit(solution)/shard_map/ppermute | solution.py:249
  4.3 16.1 %collective-permute-start.1 = (bf16[384,256]{1,0:T(8,128)(2,1)}, bf16[384,256]{1,0:T(8,128)(2,1)S(1)}, u32[]{:S(2)}, u32[]{:S(2)}) collective-permute-start(bf16[384,256]{1,0:T(8,128)(2,1)} %ratings_ref.1), channel_id=1, source_target_pairs={{1,0},{2,1},{3,2},{4,3},{5,4},{6,5},{7,6},{8,7},{9,8},{10,9},{11,1... | collective-permute-start | bytes 589832 | tf_op jit(solution)/shard_map/ppermute | solution.py:249
  18.4 8.8 %collective-permute-start.3 = (bf16[384,256]{1,0:T(8,128)(2,1)S(1)}, bf16[384,256]{1,0:T(8,128)(2,1)S(1)}, u32[]{:S(2)}, u32[]{:S(2)}) collective-permute-start(bf16[384,256]{1,0:T(8,128)(2,1)S(1)} %collective-permute-done.refs_3_.refs_2_), channel_id=1, source_target_pairs={{11,0},{0,1},{1,2},{2,3},{3,4},{4,5},{5,6},{6,7},{7,8},{8,9},{9,10... | collective-permute-start | bytes 589832 | tf_op jit(solution)/shard_map/ppermute | solution.py:249
  20.4 12.2 %collective-permute-start.2 = (bf16[384,256]{1,0:T(8,128)(2,1)S(1)}, bf16[384,256]{1,0:T(8,128)(2,1)S(1)}, u32[]{:S(2)}, u32[]{:S(2)}) collective-permute-start(bf16[384,256]{1,0:T(8,128)(2,1)S(1)} %collective-permute-done.1.refs_1_.refs_4_), channel_id=1, source_target_pairs={{1,0},{2,1},{3,2},{4,3},{5,4},{6,5},{7,6},{8,7},{9,8},{10,9},{11,1... | collective-permute-start | bytes 589832 | tf_op jit(solution)/shard_map/ppermute | solution.py:249
  25.5 16.2 %collective-permute-start.7 = (bf16[384,256]{1,0:T(8,128)(2,1)}, bf16[384,256]{1,0:T(8,128)(2,1)S(1)}, u32[]{:S(2)}, u32[]{:S(2)}) collective-permute-start(bf16[384,256]{1,0:T(8,128)(2,1)} %ratings_ref.1), channel_id=1, source_target_pairs={{4,0},{7,3},{10,6},{1,9},{16,12},{19,15},{22,18},{13,21},{28,24},{... | collective-permute-start | bytes 589832 | tf_op jit(solution)/shard_map/ppermute | solution.py:242
  27.2 19.7 %collective-permute-start.5 = (bf16[384,256]{1,0:T(8,128)(2,1)S(1)}, bf16[384,256]{1,0:T(8,128)(2,1)S(1)}, u32[]{:S(2)}, u32[]{:S(2)}) collective-permute-start(bf16[384,256]{1,0:T(8,128)(2,1)S(1)} %collective-permute-done.3.refs_4_.refs_1_), channel_id=1, source_target_pairs={{11,0},{0,1},{1,2},{2,3},{3,4},{4,5},{5,6},{6,7},{7,8},{8,9},{9,10... | collective-permute-start | bytes 589832 | tf_op jit(solution)/shard_map/ppermute | solution.py:249
  32.6 14.2 %collective-permute-start.6 = (bf16[384,256]{1,0:T(8,128)(2,1)S(1)}, bf16[384,256]{1,0:T(8,128)(2,1)S(1)}, u32[]{:S(2)}, u32[]{:S(2)}) collective-permute-start(bf16[384,256]{1,0:T(8,128)(2,1)S(1)} %collective-permute-done.2.refs_2_.refs_5_), channel_id=1, source_target_pairs={{1,0},{2,1},{3,2},{4,3},{5,4},{6,5},{7,6},{8,7},{9,8},{10,9},{11,1... | collective-permute-start | bytes 589832 | tf_op jit(solution)/shard_map/ppermute | solution.py:249
  35.0 11.8 %collective-permute-start.4 = (f32[8,128]{1,0:T(8,128)S(1)}, f32[8,128]{1,0:T(8,128)S(1)}, u32[]{:S(2)}, u32[]{:S(2)}) collective-permute-start(f32[8,128]{1,0:T(8,128)S(1)} %sums.1.near_ref), channel_id=1, source_target_pairs={{6,0},{7,1},{8,2},{9,3},{10,4},{11,5},{0,6},{1,7},{2,8},{3,9},{4,1... | collective-permute-start | bytes 12296 | tf_op jit(solution)/shard_map/ppermute | solution.py:242
  49.2 4.3 %collective-permute-start.8 = (bf16[32,104,128]{2,1,0:T(8,128)(2,1)S(1)}, bf16[32,104,128]{2,1,0:T(8,128)(2,1)S(1)}, u32[]{:S(2)}, u32[]{:S(2)}) collective-permute-start(bf16[32,104,128]{2,1,0:T(8,128)(2,1)S(1)} %get-tuple-element.16), channel_id=1, source_target_pairs={{0,12},{12,0},{1,13},{13,1},{2,14},{14,2},{3,15},{15,3},{4,16},{16... | collective-permute-start | bytes 2555912 | tf_op jit(solution)/shard_map/ppermute | solution.py:298
  87.1 8.8 %collective-permute-start.9 = (bf16[48,256]{1,0:T(8,128)(2,1)S(1)}, bf16[48,256]{1,0:T(8,128)(2,1)S(1)}, u32[]{:S(2)}, u32[]{:S(2)}) collective-permute-start(bf16[48,256]{1,0:T(8,128)(2,1)S(1)} %finish.1), channel_id=1, source_target_pairs={{0,592},{1,3},{2,206},{3,7},{4,208},{5,389},{6,211},{7,391},{8,593... | collective-permute-start | bytes 73736 | tf_op jit(solution)/shard_map/ppermute | solution.py:335

commit v15 on v14

--- a/solution.py
+++ b/solution.py
@@ -72,7 +72,7 @@
 def panel_at(panels, core, offset):
     if offset > REACH:
         return panels[-1]
-    return panels[REACH - offset if core else REACH + offset]
+    return panels[REACH + offset if core else REACH - offset]
 
 
 def half_products(place_ref, scale, panels, gram_ref, partner):
@@ -244,7 +244,7 @@
     def relay(array, by):
         pairs = []
         for c in range(CORES):
-            shift = -by if c else by
+            shift = by if c else -by
             pairs += [(c * PANELS + (z + shift) % PANELS, c * PANELS + z) for z in range(PANELS)]
         return lax.ppermute(array, ("core", "z"), pairs)
 

time: 97 us -> 103 us (1.062)
  the two profiles are of different devices: /device:TPU:6 before, /device:TPU:8 now
where the time goes in v15:
time: 103 us
  starting transfers between devices  38.5 us (37%)
  blocking collectives  33.2 us (32%)
  waiting for transfers between devices  23.5 us (23%)
  Pallas kernels  5.95 us (6%)
  local copies, waits for them, and re-layouts  1.34 us (1%)
    ppermute x6, starting transfers between devices, relay(): return lax.ppermute(array, ('core', 'z'), pairs)  31.4 us
    all_to_all x1, blocking collectives, per_device(): parts = lax.all_to_all(total, 'x', 0, 0, tiled=True)  17.4 us
    all_to_all x1, blocking collectives, per_device(): parts = lax.all_to_all(total, 'y', 0, 0, tiled=True)  15.9 us
    ppermute x2, waiting for transfers between devices, fetch(): return lax.ppermute(array, 'z', [((z + by) % PANELS, z) for z in at])  9.13 us
    ppermute x6, waiting for transfers between devices, relay(): return lax.ppermute(array, ('core', 'z'), pairs)  7.81 us
    ppermute x1, waiting for transfers between devices, per_device(): return lax.ppermute(block, AXES, homes())  5.63 us
    ppermute x2, starting transfers between devices, fetch(): return lax.ppermute(array, 'z', [((z + by) % PANELS, z) for z in at])  3.21 us
    pallas_call x1, Pallas kernels, per_device(): pl.pallas_call(send_kernel, out_shape=(jax.ShapeDtypeStruct(slots, jnp.bf...  2.32 us
  transfers between devices with their start and end apart: 10, of which 5 were waited for; matrix products, arithmetic and copies ran while one was open for 1% of the time, Pallas kernels for 3%

profile of v15, /device:TPU:8, one launch (start us, length us, event | category | flops | bytes accessed | tf_op | source)
XLA Modules:
  0.0 102.6 jit_solution(1592015550252797834)
XLA Ops:
  0.0 14.6 %collective-permute-start = (bf16[384,256]{1,0:T(8,128)(2,1)}, bf16[384,256]{1,0:T(8,128)(2,1)S(1)}, u32[]{:S(2)}, u32[]{:S(2)}) collective-permute-start(bf16[384,256]{1,0:T(8,128)(2,1)} %ratings_ref.1), channel_id=1, source_target_pairs={{1,0},{2,1},{3,2},{4,3},{5,4},{6,5},{7,6},{8,7},{9,8},{10,9},{11,1... | collective-permute-start | bytes 589832 | tf_op jit(solution)/shard_map/ppermute | solution.py:249
  14.6 1.9 %collective-permute-start.1 = (bf16[384,256]{1,0:T(8,128)(2,1)}, bf16[384,256]{1,0:T(8,128)(2,1)S(1)}, u32[]{:S(2)}, u32[]{:S(2)}) collective-permute-start(bf16[384,256]{1,0:T(8,128)(2,1)} %ratings_ref.1), channel_id=1, source_target_pairs={{11,0},{0,1},{1,2},{2,3},{3,4},{4,5},{5,6},{6,7},{7,8},{8,9},{9,10... | collective-permute-start | bytes 589832 | tf_op jit(solution)/shard_map/ppermute | solution.py:249
  16.5 1.0 own.1.refs_0_.refs_3_
  17.5 1.9 %collective-permute-done.refs_3_.refs_2_ = bf16[384,256]{1,0:T(8,128)(2,1)S(1)} collective-permute-done((bf16[384,256]{1,0:T(8,128)(2,1)}, bf16[384,256]{1,0:T(8,128)(2,1)S(1)}, u32[]{:S(2)}, u32[]{:S(2)}) %collective-permute-start) | collective-permute-done | bytes 196640 | tf_op jit(solution)/shard_map/ppermute | solution.py:249
  19.4 5.5 %collective-permute-start.3 = (bf16[384,256]{1,0:T(8,128)(2,1)S(1)}, bf16[384,256]{1,0:T(8,128)(2,1)S(1)}, u32[]{:S(2)}, u32[]{:S(2)}) collective-permute-start(bf16[384,256]{1,0:T(8,128)(2,1)S(1)} %collective-permute-done.refs_3_.refs_2_), channel_id=1, source_target_pairs={{1,0},{2,1},{3,2},{4,3},{5,4},{6,5},{7,6},{8,7},{9,8},{10,9},{11,1... | collective-permute-start | bytes 589832 | tf_op jit(solution)/shard_map/ppermute | solution.py:249
  24.9 0.0 collective-permute-done.1.refs_1_.refs_4_
  24.9 1.9 %collective-permute-start.2 = (bf16[384,256]{1,0:T(8,128)(2,1)S(1)}, bf16[384,256]{1,0:T(8,128)(2,1)S(1)}, u32[]{:S(2)}, u32[]{:S(2)}) collective-permute-start(bf16[384,256]{1,0:T(8,128)(2,1)S(1)} %collective-permute-done.1.refs_1_.refs_4_), channel_id=1, source_target_pairs={{11,0},{0,1},{1,2},{2,3},{3,4},{4,5},{5,6},{6,7},{7,8},{8,9},{9,10... | collective-permute-start | bytes 589832 | tf_op jit(solution)/shard_map/ppermute | solution.py:249
  26.8 1.3 %collective-permute-start.7 = (bf16[384,256]{1,0:T(8,128)(2,1)}, bf16[384,256]{1,0:T(8,128)(2,1)S(1)}, u32[]{:S(2)}, u32[]{:S(2)}) collective-permute-start(bf16[384,256]{1,0:T(8,128)(2,1)} %ratings_ref.1), channel_id=1, source_target_pairs={{4,0},{7,3},{10,6},{1,9},{16,12},{19,15},{22,18},{13,21},{28,24},{... | collective-permute-start | bytes 589832 | tf_op jit(solution)/shard_map/ppermute | solution.py:242
  28.1 5.9 %collective-permute-done.3.refs_4_.refs_1_ = bf16[384,256]{1,0:T(8,128)(2,1)S(1)} collective-permute-done((bf16[384,256]{1,0:T(8,128)(2,1)S(1)}, bf16[384,256]{1,0:T(8,128)(2,1)S(1)}, u32[]{:S(2)}, u32[]{:S(2)}) %collective-permute-start.3) | collective-permute-done | bytes 196640 | tf_op jit(solution)/shard_map/ppermute | solution.py:249
  34.0 5.6 %collective-permute-start.5 = (bf16[384,256]{1,0:T(8,128)(2,1)S(1)}, bf16[384,256]{1,0:T(8,128)(2,1)S(1)}, u32[]{:S(2)}, u32[]{:S(2)}) collective-permute-start(bf16[384,256]{1,0:T(8,128)(2,1)S(1)} %collective-permute-done.3.refs_4_.refs_1_), channel_id=1, source_target_pairs={{1,0},{2,1},{3,2},{4,3},{5,4},{6,5},{7,6},{8,7},{9,8},{10,9},{11,1... | collective-permute-start | bytes 589832 | tf_op jit(solution)/shard_map/ppermute | solution.py:249
  39.6 0.0 collective-permute-done.2.refs_2_.refs_5_
  39.6 1.9 %collective-permute-start.6 = (bf16[384,256]{1,0:T(8,128)(2,1)S(1)}, bf16[384,256]{1,0:T(8,128)(2,1)S(1)}, u32[]{:S(2)}, u32[]{:S(2)}) collective-permute-start(bf16[384,256]{1,0:T(8,128)(2,1)S(1)} %collective-permute-done.2.refs_2_.refs_5_), channel_id=1, source_target_pairs={{11,0},{0,1},{1,2},{2,3},{3,4},{4,5},{5,6},{6,7},{7,8},{8,9},{9,10... | collective-permute-start | bytes 589832 | tf_op jit(solution)/shard_map/ppermute | solution.py:249
  41.5 0.3 sums.1.near_ref
  41.8 1.9 %collective-permute-start.4 = (f32[8,128]{1,0:T(8,128)S(1)}, f32[8,128]{1,0:T(8,128)S(1)}, u32[]{:S(2)}, u32[]{:S(2)}) collective-permute-start(f32[8,128]{1,0:T(8,128)S(1)} %sums.1.near_ref), channel_id=1, source_target_pairs={{6,0},{7,1},{8,2},{9,3},{10,4},{11,5},{0,6},{1,7},{2,8},{3,9},{4,1... | collective-permute-start | bytes 12296 | tf_op jit(solution)/shard_map/ppermute | solution.py:242
  43.7 0.7 concatenate.3.place_ref
  44.5 0.0 collective-permute-done.7.refs_7_
  44.5 9.1 %collective-permute-done.4.far_ref = f32[8,128]{1,0:T(8,128)S(1)} collective-permute-done((f32[8,128]{1,0:T(8,128)S(1)}, f32[8,128]{1,0:T(8,128)S(1)}, u32[]{:S(2)}, u32[]{:S(2)}) %collective-permute-start.4) | collective-permute-done | bytes 4128 | tf_op jit(solution)/shard_map/ppermute | solution.py:242
  53.6 0.0 collective-permute-done.5.refs_0_
  53.6 0.0 collective-permute-done.6.refs_6_
  53.6 2.3 %send.1 = (bf16[32,104,128]{2,1,0:T(8,128)(2,1)S(1)}, f32[384,1]{1,0:T(8,128)S(1)}, f32[8,128]{1,0:T(8,128)S(1)}, f32[8,128]{1,0:T(8,128)S(1)}) custom-call(s32[10]{0:T(128)S(1)} %concatenate.3.place_ref, f32[8,128]{1,0:T(8,128)S(1)} %sums.1.near_ref, f32[8,128]{1,0:T(8,128)S(1)} %collective-permute-done.4.far_ref, ...), custom_call_target="tpu_custom_call" | custom-call | flops 301989888 | bytes 1179648 | tf_op jit(solution)/shard_map/send/pallas_call | solution.py:283
  55.9 1.9 %collective-permute-start.8 = (bf16[32,104,128]{2,1,0:T(8,128)(2,1)S(1)}, bf16[32,104,128]{2,1,0:T(8,128)(2,1)S(1)}, u32[]{:S(2)}, u32[]{:S(2)}) collective-permute-start(bf16[32,104,128]{2,1,0:T(8,128)(2,1)S(1)} %get-tuple-element.16), channel_id=1, source_target_pairs={{0,12},{12,0},{1,13},{13,1},{2,14},{14,2},{3,15},{15,3},{4,16},{16... | collective-permute-start | bytes 2555912 | tf_op jit(solution)/shard_map/ppermute | solution.py:298
  57.9 1.5 %keep.1.keep_ref = f32[32,104,128]{2,1,0:T(8,128)S(1)} custom-call(s32[10]{0:T(128)S(1)} %concatenate.3.place_ref, f32[384,1]{1,0:T(8,128)S(1)} %get-tuple-element.13.scale_ref, f32[8,128]{1,0:T(8,128)S(1)} %get-tuple-element.14.row_ref, f32[8,128]{1,0:T(8,128)S(1)} %get-tuple-element.15.column_ref, bf16[384,256]{1,0:T(8,128)(2,1)S(1)} %collective-permute-done.5.refs_0_, ...), custom_call_target="tpu_custom_call" | custom-call | flops 301989888 | bytes 1179648 | tf_op jit(solution)/shard_map/keep/pallas_call | solution.py:299
  59.3 0.9 collective-permute-done.8.got_ref
  60.2 0.2 add.1
  60.4 17.4 %all_to_all.10.got_ref = bf16[32,104,128]{2,1,0:T(8,128)(2,1)S(1)} all-to-all(bf16[32,104,128]{2,1,0:T(8,128)(2,1)S(1)} %add.1), channel_id=1, replica_groups=mesh['x'=4,'y'=8,'core'=2,'z'=12] {'x'}, dimensions={0} | all-to-all | bytes 1703936 | tf_op jit(solution)/shard_map/all_to_all | solution.py:317
  77.8 0.1 fold.1
  77.9 15.9 %all_to_all.11.got_ref = bf16[8,104,128]{2,1,0:T(8,128)(2,1)S(1)} all-to-all(bf16[8,104,128]{2,1,0:T(8,128)(2,1)S(1)} %fold.1), channel_id=1, replica_groups=mesh['x'=4,'y'=8,'core'=2,'z'=12] {'y'}, dimensions={0} | all-to-all | bytes 425984 | tf_op jit(solution)/shard_map/all_to_all | solution.py:326
  93.8 0.7 finish.1
  94.4 1.9 %collective-permute-start.9 = (bf16[48,256]{1,0:T(8,128)(2,1)S(1)}, bf16[48,256]{1,0:T(8,128)(2,1)S(1)}, u32[]{:S(2)}, u32[]{:S(2)}) collective-permute-start(bf16[48,256]{1,0:T(8,128)(2,1)S(1)} %finish.1), channel_id=1, source_target_pairs={{0,592},{1,3},{2,206},{3,7},{4,208},{5,389},{6,211},{7,391},{8,593... | collective-permute-start | bytes 73736 | tf_op jit(solution)/shard_map/ppermute | solution.py:335
  96.4 5.6 %collective-permute-done.9 = bf16[48,256]{1,0:T(8,128)(2,1)S(1)} collective-permute-done((bf16[48,256]{1,0:T(8,128)(2,1)S(1)}, bf16[48,256]{1,0:T(8,128)(2,1)S(1)}, u32[]{:S(2)}, u32[]{:S(2)}) %collective-permute-start.9) | collective-permute-done | bytes 24608 | tf_op jit(solution)/shard_map/ppermute | solution.py:335
  102.0 0.6 copy.4
Async XLA Ops:
  0.0 19.4 %collective-permute-start = (bf16[384,256]{1,0:T(8,128)(2,1)}, bf16[384,256]{1,0:T(8,128)(2,1)S(1)}, u32[]{:S(2)}, u32[]{:S(2)}) collective-permute-start(bf16[384,256]{1,0:T(8,128)(2,1)} %ratings_ref.1), channel_id=1, source_target_pairs={{1,0},{2,1},{3,2},{4,3},{5,4},{6,5},{7,6},{8,7},{9,8},{10,9},{11,1... | collective-permute-start | bytes 589832 | tf_op jit(solution)/shard_map/ppermute | solution.py:249
  14.6 10.3 %collective-permute-start.1 = (bf16[384,256]{1,0:T(8,128)(2,1)}, bf16[384,256]{1,0:T(8,128)(2,1)S(1)}, u32[]{:S(2)}, u32[]{:S(2)}) collective-permute-start(bf16[384,256]{1,0:T(8,128)(2,1)} %ratings_ref.1), channel_id=1, source_target_pairs={{11,0},{0,1},{1,2},{2,3},{3,4},{4,5},{5,6},{6,7},{7,8},{8,9},{9,10... | collective-permute-start | bytes 589832 | tf_op jit(solution)/shard_map/ppermute | solution.py:249
  19.4 14.6 %collective-permute-start.3 = (bf16[384,256]{1,0:T(8,128)(2,1)S(1)}, bf16[384,256]{1,0:T(8,128)(2,1)S(1)}, u32[]{:S(2)}, u32[]{:S(2)}) collective-permute-start(bf16[384,256]{1,0:T(8,128)(2,1)S(1)} %collective-permute-done.refs_3_.refs_2_), channel_id=1, source_target_pairs={{1,0},{2,1},{3,2},{4,3},{5,4},{6,5},{7,6},{8,7},{9,8},{10,9},{11,1... | collective-permute-start | bytes 589832 | tf_op jit(solution)/shard_map/ppermute | solution.py:249
  24.9 14.7 %collective-permute-start.2 = (bf16[384,256]{1,0:T(8,128)(2,1)S(1)}, bf16[384,256]{1,0:T(8,128)(2,1)S(1)}, u32[]{:S(2)}, u32[]{:S(2)}) collective-permute-start(bf16[384,256]{1,0:T(8,128)(2,1)S(1)} %collective-permute-done.1.refs_1_.refs_4_), channel_id=1, source_target_pairs={{11,0},{0,1},{1,2},{2,3},{3,4},{4,5},{5,6},{6,7},{7,8},{8,9},{9,10... | collective-permute-start | bytes 589832 | tf_op jit(solution)/shard_map/ppermute | solution.py:249
  26.8 17.6 %collective-permute-start.7 = (bf16[384,256]{1,0:T(8,128)(2,1)}, bf16[384,256]{1,0:T(8,128)(2,1)S(1)}, u32[]{:S(2)}, u32[]{:S(2)}) collective-permute-start(bf16[384,256]{1,0:T(8,128)(2,1)} %ratings_ref.1), channel_id=1, source_target_pairs={{4,0},{7,3},{10,6},{1,9},{16,12},{19,15},{22,18},{13,21},{28,24},{... | collective-permute-start | bytes 589832 | tf_op jit(solution)/shard_map/ppermute | solution.py:242
  34.0 19.6 %collective-permute-start.5 = (bf16[384,256]{1,0:T(8,128)(2,1)S(1)}, bf16[384,256]{1,0:T(8,128)(2,1)S(1)}, u32[]{:S(2)}, u32[]{:S(2)}) collective-permute-start(bf16[384,256]{1,0:T(8,128)(2,1)S(1)} %collective-permute-done.3.refs_4_.refs_1_), channel_id=1, source_target_pairs={{1,0},{2,1},{3,2},{4,3},{5,4},{6,5},{7,6},{8,7},{9,8},{10,9},{11,1... | collective-permute-start | bytes 589832 | tf_op jit(solution)/shard_map/ppermute | solution.py:249
  39.6 14.0 %collective-permute-start.6 = (bf16[384,256]{1,0:T(8,128)(2,1)S(1)}, bf16[384,256]{1,0:T(8,128)(2,1)S(1)}, u32[]{:S(2)}, u32[]{:S(2)}) collective-permute-start(bf16[384,256]{1,0:T(8,128)(2,1)S(1)} %collective-permute-done.2.refs_2_.refs_5_), channel_id=1, source_target_pairs={{11,0},{0,1},{1,2},{2,3},{3,4},{4,5},{5,6},{6,7},{7,8},{8,9},{9,10... | collective-permute-start | bytes 589832 | tf_op jit(solution)/shard_map/ppermute | solution.py:249
  41.8 11.8 %collective-permute-start.4 = (f32[8,128]{1,0:T(8,128)S(1)}, f32[8,128]{1,0:T(8,128)S(1)}, u32[]{:S(2)}, u32[]{:S(2)}) collective-permute-start(f32[8,128]{1,0:T(8,128)S(1)} %sums.1.near_ref), channel_id=1, source_target_pairs={{6,0},{7,1},{8,2},{9,3},{10,4},{11,5},{0,6},{1,7},{2,8},{3,9},{4,1... | collective-permute-start | bytes 12296 | tf_op jit(solution)/shard_map/ppermute | solution.py:242
  55.9 4.3 %collective-permute-start.8 = (bf16[32,104,128]{2,1,0:T(8,128)(2,1)S(1)}, bf16[32,104,128]{2,1,0:T(8,128)(2,1)S(1)}, u32[]{:S(2)}, u32[]{:S(2)}) collective-permute-start(bf16[32,104,128]{2,1,0:T(8,128)(2,1)S(1)} %get-tuple-element.16), channel_id=1, source_target_pairs={{0,12},{12,0},{1,13},{13,1},{2,14},{14,2},{3,15},{15,3},{4,16},{16... | collective-permute-start | bytes 2555912 | tf_op jit(solution)/shard_map/ppermute | solution.py:298
  94.4 7.6 %collective-permute-start.9 = (bf16[48,256]{1,0:T(8,128)(2,1)S(1)}, bf16[48,256]{1,0:T(8,128)(2,1)S(1)}, u32[]{:S(2)}, u32[]{:S(2)}) collective-permute-start(bf16[48,256]{1,0:T(8,128)(2,1)S(1)} %finish.1), channel_id=1, source_target_pairs={{0,592},{1,3},{2,206},{3,7},{4,208},{5,389},{6,211},{7,391},{8,593... | collective-permute-start | bytes 73736 | tf_op jit(solution)/shard_map/ppermute | solution.py:335
